TPU v7x, 256 devices: a whole 4x4x8 slice. The times are simulated.
256 devices in a mesh: sign: 2 (over y_hi), context: 128 (over y_lo, x, z, core).
Axes of the slice: x: 4, y: 4 (y_hi: 2, y_lo: 2; y = y_hi * 2 + y_lo), z: 8, core: 2. Of those that a mesh axis runs over, the one named last changes fastest.
Arguments:
- inputs: bfloat16 [32768, 1024], P('context'), may hold values from -6 to 6
- cotangent: bfloat16 [32768, 1024], P('context'), may hold values from -24 to 24
- weights: bfloat16 [2, 1024, 1024], P('sign'), may hold values from -0.1875 to 0.1875
- filter_taps: float32 [32768], replicated, may hold values from -0.03125 to 0.03125
Outputs:
- input_grad: bfloat16 [32768, 1024], P('context', 'sign')
- weight_grad: float32 [2, 1024, 1024], P('sign', 'context')
All inputs are finite; a program needn't handle non-finite values.
Results may differ from a plain program's by a relative error of at most 0.0058.
Values may be sent and summed in bfloat16 or wider, within the bound.
No kernel may reach another device: no remote copies, remote signals or barrier semaphores. Data moves between devices by JAX's collectives and lax.ppermute only.
A program may use at most 64 MiB of HBM per device.

v0:
```python
import math

import jax
import jax.numpy as jnp
from jax import lax
from jax.sharding import PartitionSpec as P

HIGHEST = lax.Precision.HIGHEST


def product(pattern, left_re, left_im, right_re, right_im):
    real_part = jnp.einsum(pattern, left_re, right_re, precision=HIGHEST) - jnp.einsum(
        pattern, left_im, right_im, precision=HIGHEST
    )
    imag_part = jnp.einsum(pattern, left_re, right_im, precision=HIGHEST) + jnp.einsum(
        pattern, left_im, right_re, precision=HIGHEST
    )
    return (real_part, imag_part)


def elementwise(left_re, left_im, right_re, right_im):
    return (left_re * right_re - left_im * right_im, left_re * right_im + left_im * right_re)


def angles(row_count, col_count, period):
    row_index = lax.broadcasted_iota(jnp.int32, (row_count, col_count), 0)
    col_index = lax.broadcasted_iota(jnp.int32, (row_count, col_count), 1)
    phase = (row_index * col_index % period).astype(jnp.float32) * (2.0 * math.pi / period)
    return (jnp.cos(phase), -jnp.sin(phase))


def spectral_tables(outer_size, inner_size):
    return (
        angles(outer_size, outer_size, outer_size),
        angles(outer_size, inner_size, outer_size * inner_size),
        angles(inner_size, inner_size, inner_size),
    )


def forward(signal_re, signal_im, tables, half_rows):
    first, twist, second = tables
    step_re, step_im = product(
        "kn,pnm->pkm", first[0][:, :half_rows], first[1][:, :half_rows], signal_re, signal_im
    )
    step_re, step_im = elementwise(step_re, step_im, twist[0], twist[1])
    return product("pkn,nm->pkm", step_re, step_im, second[0], second[1])


def inverse(spec_re, spec_im, tables, half_rows):
    first, twist, second = tables
    step_re, step_im = product("pkm,mn->pkn", spec_re, spec_im, second[0], -second[1])
    step_re, step_im = elementwise(step_re, step_im, twist[0], -twist[1])
    out_re, out_im = product(
        "nk,pkm->pnm", first[0][:half_rows], -first[1][:half_rows], step_re, step_im
    )
    total_len = first[0].shape[0] * twist[0].shape[1]
    return (out_re / total_len, out_im / total_len)


def convolve(channels, kernel_re, kernel_im, tables, half_rows, inner_size):
    chan_count, seq_len = channels.shape
    signal = channels.astype(jnp.float32).reshape(chan_count // 2, 2, half_rows, inner_size)
    spec_re, spec_im = forward(signal[:, 0], signal[:, 1], tables, half_rows)
    spec_re, spec_im = elementwise(spec_re, spec_im, kernel_re, kernel_im)
    out_re, out_im = inverse(spec_re, spec_im, tables, half_rows)
    return jnp.stack([out_re, out_im], 1).reshape(chan_count, seq_len)


def send_features(features):
    return lax.all_to_all(features, "context", split_axis=1, concat_axis=0, tiled=True)


def body(inputs, cotangent, weights, filter_taps):
    tok_rows = inputs.shape[0]
    model_width = inputs.shape[1]
    groups = lax.axis_size("context")
    length = tok_rows * groups
    inner_size = 2 * groups
    half_rows = tok_rows // 2
    local_width = model_width // groups
    tables = spectral_tables(tok_rows, inner_size)
    lag_index = lax.broadcasted_iota(jnp.int32, (length,), 0)
    flipped = (lax.axis_index("sign") == 1) & (lag_index % 2 == 1)
    signed_taps = jnp.where(flipped, -filter_taps, filter_taps)
    blank_imag = jnp.zeros((1, half_rows, inner_size), jnp.float32)
    kernel_re, kernel_im = forward(
        signed_taps.reshape(1, half_rows, inner_size), blank_imag, tables, half_rows
    )
    grad_rows = lax.dot_general(
        weights[0], cotangent, (((0,), (1,)), ((), ())), preferred_element_type=jnp.float32
    ).astype(jnp.bfloat16)
    grad_rows = (
        grad_rows.reshape(2, groups, local_width // 2, tok_rows)
        .transpose(1, 0, 2, 3)
        .reshape(model_width, tok_rows)
    )
    spread = lax.all_to_all(inputs.T, "context", split_axis=0, concat_axis=1, tiled=True)
    grad_cols = lax.all_to_all(grad_rows, "context", split_axis=0, concat_axis=1, tiled=True)
    features = convolve(spread, kernel_re, kernel_im, tables, half_rows, inner_size).astype(
        jnp.bfloat16
    )
    backward = convolve(grad_cols, kernel_re, -kernel_im, tables, half_rows, inner_size).astype(
        jnp.bfloat16
    )
    grad_scale = 1.0 / math.sqrt(length)
    feature_rows = send_features(features)
    returned = lax.all_to_all(backward, "context", split_axis=1, concat_axis=0, tiled=True)
    paired = lax.psum_scatter(
        returned.reshape(groups, 2, local_width // 2, tok_rows)
        .astype(jnp.float32)
        .astype(jnp.bfloat16),
        "sign",
        scatter_dimension=1,
        tiled=True,
    ).astype(jnp.float32)
    summed = paired.reshape(model_width // 2, tok_rows)
    weight_grad = lax.psum_scatter(
        lax.dot_general(
            cotangent, feature_rows, (((0,), (1,)), ((), ())), preferred_element_type=jnp.float32
        )
        * grad_scale,
        "context",
        scatter_dimension=0,
        tiled=True,
    )
    input_grad = summed.T.astype(jnp.bfloat16)
    return (input_grad, weight_grad[None])


def solution(mesh):
    in_specs = (P("context", None), P("context", None), P("sign", None, None), P())
    out_specs = (P("context", "sign"), P("sign", "context", None))
    return jax.shard_map(body, mesh=mesh, in_specs=in_specs, out_specs=out_specs, check_vma=False)
```

profile of v0, /device:TPU:1, one launch (start us, length us, event | category | flops | bytes accessed | tf_op | source)
XLA Modules:
  0.0 771.4 jit_solution(11276738410285890811)
XLA Ops:
  7.2 1.6 copy-done
  8.8 1.8 fusion.4
  10.8 1.1 copy.51
  11.9 15.6 %all-to-all-start = ((bf16[128,8,256]{2,1,0:T(8,128)(2,1)}), bf16[128,8,256]{2,1,0:T(8,128)(2,1)}, u32[]{:S(2)}, u32[]{:S(2)}) async-start(bf16[128,8,256]{2,1,0:T(8,128)(2,1)} %copy.51), calls=%async_computation | async-start | bytes 1048576 | tf_op jit(solution)/shard_map/all_to_all | solution.py:98
  30.9 1.1 fusion.22
  32.0 1.1 fusion.20
  35.0 2.0 copy.70
  38.0 3.6 fusion.45
  41.6 3.5 fusion.47
  45.1 15.1 %convolution_subtract_fusion.8 = f32[256,256]{1,0:T(8,128)S(1)} fusion(f32[256,256]{1,0:T(8,128)S(1)} %fusion.47, f32[1,256,256]{1,2,0:T(8,128)S(1)} %copy-done.31, f32[1,256,256]{1,2,0:T(8,128)S(1)} %copy-done.32), kind=kOutput, calls=%fused_computation.31 | convolution fusion | flops 203554816 | bytes 1048576 | tf_op jit(solution)/shard_map/pkn,nm->pkm/dot_general | solution.py:12
  60.3 3.3 fusion.230
  63.6 12.9 %all-to-all-start.2 = ((bf16[128,8,256]{2,1,0:T(8,128)(2,1)}), bf16[128,8,256]{2,1,0:T(8,128)(2,1)}, u32[]{:S(2)}, u32[]{:S(2)}) async-start(bf16[128,8,256]{2,1,0:T(8,128)(2,1)} %bitcast.192), calls=%async_computation.3 | async-start | bytes 1048576 | tf_op jit(solution)/shard_map/all_to_all | solution.py:97
  76.5 1.1 copy.52
  80.2 2.8 fusion.51
  83.0 2.8 fusion.63
  85.7 2.8 convolution_add_fusion.4
  88.5 3.2 convolution_subtract_fusion.4
  91.7 2.2 fusion.40
  93.9 3.2 convolution_add_fusion.3
  97.1 2.2 fusion.60
  99.3 2.2 convolution_subtract_fusion.3
  101.5 2.0 fusion.132
  103.5 1.9 fusion.133
  105.4 1.2 copy.71
  106.6 1.5 fusion.78
  108.1 1.5 fusion.77
  109.6 1.5 convolution_add_fusion.2
  111.7 2.0 fusion.25
  113.7 2.0 fusion.27
  115.7 2.0 convolution_add_fusion.1
  117.8 2.0 convolution_subtract_fusion.1
  119.9 3.4 fusion.37
  123.2 3.1 fusion.55
  126.4 1.1 fusion.16
  129.4 2.0 copy.66
  131.4 2.1 copy.67
  133.6 13.3 %all-to-all-start.1 = ((bf16[8,128,256]{2,0,1:T(8,128)(2,1)}), bf16[8,128,256]{2,0,1:T(8,128)(2,1)}, u32[]{:S(2)}, u32[]{:S(2)}) async-start(bf16[8,128,256]{2,0,1:T(8,128)(2,1)} %copy.67), calls=%async_computation.1 | async-start | bytes 1048576 | tf_op jit(solution)/shard_map/all_to_all | solution.py:107
  147.0 4.1 convolution_add_fusion
  151.1 2.2 convolution_subtract_fusion
  157.7 1.1 copy.79
  158.8 6.0 all-to-all-done.1
  164.8 6.8 all-to-all-start.3
  171.7 2.0 copy.68
  173.8 16.4 %all-to-all-done.3 = bf16[8,128,256]{2,0,1:T(8,128)(2,1)S(1)} async-done(((bf16[8,128,256]{2,0,1:T(8,128)(2,1)}), bf16[8,128,256]{2,0,1:T(8,128)(2,1)S(1)}, u32[]{:S(2)}, u32[]{:S(2)}) %all-to-all-start.3) | async-done | bytes 524320 | tf_op jit(solution)/shard_map/all_to_all | solution.py:70
  190.1 3.8 multiply_bitcast_fusion
  193.9 5.4 copy.94
  199.4 1.2 copy.69
  201.4 560.9 %reduce-scatter.7.cloned.1.call-done = f32[8,1024]{1,0:T(8,128)} async-done(((f32[1024,1024]{1,0:T(8,128)}), f32[8,1024]{1,0:T(8,128)}) %reduce-scatter.7.cloned.1.call-update) | async-done | bytes 32784
  (104 shorter events, 18.6 us)
Async XLA Ops:
  7.2 1.6 copy-start
  7.2 23.4 %copy-start.33 = (f32[32768]{0:T(1024)S(1)}, f32[32768]{0:T(1024)}, u32[]{:S(2)}) copy-start(f32[32768]{0:T(1024)} %param.7) | copy-start | bytes 393220
  11.9 51.7 %all-to-all-start = ((bf16[128,8,256]{2,1,0:T(8,128)(2,1)}), bf16[128,8,256]{2,1,0:T(8,128)(2,1)}, u32[]{:S(2)}, u32[]{:S(2)}) async-start(bf16[128,8,256]{2,1,0:T(8,128)(2,1)} %copy.51), calls=%async_computation | async-start | bytes 1048576 | tf_op jit(solution)/shard_map/all_to_all | solution.py:98
  28.5 51.1 %copy-start.14 = (f32[256,256]{1,0:T(8,128)}, f32[256,256]{1,0:T(8,128)S(1)}, u32[]{:S(2)}) copy-start(f32[256,256]{1,0:T(8,128)S(1)} %fusion.110) | copy-start | bytes 786436
  29.5 48.8 %copy-start.21 = (f32[256,256]{1,0:T(8,128)}, f32[256,256]{1,0:T(8,128)S(1)}, u32[]{:S(2)}) copy-start(f32[256,256]{1,0:T(8,128)S(1)} %fusion.95) | copy-start | bytes 786436
  30.5 11.1 %copy-start.17 = (f32[256,256]{1,0:T(8,128)}, f32[256,256]{1,0:T(8,128)S(1)}, u32[]{:S(2)}) copy-start(f32[256,256]{1,0:T(8,128)S(1)} %get-tuple-element.10) | copy-start | bytes 786436
  30.5 14.6 %copy-start.19 = (f32[256,256]{1,0:T(8,128)}, f32[256,256]{1,0:T(8,128)S(1)}, u32[]{:S(2)}) copy-start(f32[256,256]{1,0:T(8,128)S(1)} %get-tuple-element.11) | copy-start | bytes 786436
  38.0 7.1 copy-start.31
  38.0 7.2 copy-start.32
  60.3 31.4 %copy-start.10 = (f32[256,256]{1,0:T(8,128)}, f32[256,256]{1,0:T(8,128)S(1)}, u32[]{:S(2)}) copy-start(f32[256,256]{1,0:T(8,128)S(1)} %convolution_subtract_fusion.8) | copy-start | bytes 786436
  63.6 41.8 %all-to-all-start.2 = ((bf16[128,8,256]{2,1,0:T(8,128)(2,1)}), bf16[128,8,256]{2,1,0:T(8,128)(2,1)}, u32[]{:S(2)}, u32[]{:S(2)}) async-start(bf16[128,8,256]{2,1,0:T(8,128)(2,1)} %bitcast.192), calls=%async_computation.3 | async-start | bytes 1048576 | tf_op jit(solution)/shard_map/all_to_all | solution.py:97
  77.6 2.5 copy-start.24
  85.7 6.0 copy-start.27
  93.9 3.2 copy-start.11
  97.1 4.4 copy-start.7
  97.1 4.4 copy-start.22
  101.5 2.0 copy-start.1
  105.4 5.7 copy-start.15
  106.6 5.1 copy-start.18
  106.6 5.1 copy-start.20
  115.7 4.1 copy-start.12
  115.7 4.1 copy-start.25
  117.8 5.5 copy-start.3
  119.8 7.6 copy-start.5
  119.8 6.5 copy-start.2
  119.8 6.5 copy-start.8
  119.8 6.5 copy-start.30
  123.2 4.2 copy-start.29
  128.5 18.4 %copy-start.4 = (f32[4,256,256]{2,1,0:T(8,128)S(1)}, f32[4,256,256]{2,1,0:T(8,128)}, u32[]{:S(2)}) copy-start(f32[4,256,256]{2,1,0:T(8,128)} %copy-done.3) | copy-start | bytes 3145732
  133.6 31.3 %all-to-all-start.1 = ((bf16[8,128,256]{2,0,1:T(8,128)(2,1)}), bf16[8,128,256]{2,0,1:T(8,128)(2,1)}, u32[]{:S(2)}, u32[]{:S(2)}) async-start(bf16[8,128,256]{2,0,1:T(8,128)(2,1)} %copy.67), calls=%async_computation.1 | async-start | bytes 1048576 | tf_op jit(solution)/shard_map/all_to_all | solution.py:107
  146.9 4.1 copy-start.6
  146.9 4.1 copy-start.13
  146.9 4.1 copy-start.26
  147.0 4.1 copy-start.28
  147.0 6.3 copy-start.9
  147.0 6.3 copy-start.23
  151.1 3.2 copy-start.16
  164.8 25.3 %all-to-all-start.3 = ((bf16[8,128,256]{2,0,1:T(8,128)(2,1)}), bf16[8,128,256]{2,0,1:T(8,128)(2,1)S(1)}, u32[]{:S(2)}, u32[]{:S(2)}) async-start(bf16[8,128,256]{2,0,1:T(8,128)(2,1)} %copy.79), calls=%async_computation.4 | async-start | bytes 1048576 | tf_op jit(solution)/shard_map/all_to_all | solution.py:70
  171.7 27.7 %reduce-scatter.5.cloned.1.call-start = ((), (), s32[]{:S(2)}) async-start(), calls=%async_computation.6 | async-start | bytes 786432 | tf_op jit(solution)/shard_map/reduce_scatter | solution.py:108
  173.7 588.6 %reduce-scatter.7.cloned.1.call-start = ((), (), s32[]{:S(2)}) async-start(), calls=%async_computation.7 | async-start | bytes 4227072
Sparse Core Ops, SparseCore 0:
  175.0 22.5 reduce-scatter.4
  200.2 562.0 reduce-scatter.6
where the time goes:
time: 781 us; the launch traced here: 771 us
  waiting for transfers between devices  583 us (75%)
  matrix products  92.9 us (12%)
  starting transfers between devices  48.8 us (6%)
  local copies, waits for them, and re-layouts  25.9 us (3%)
  between operations  15.3 us (2%)
    unnamed x3, waiting for transfers between devices  561 us
    dot_general x9, matrix products, product(): jnp.einsum(pattern, left_im, right_im, precision=HIGHEST)  27.9 us
    dot_general x10, matrix products, product(): jnp.einsum(pattern, left_im, right_re, precision=HIGHEST)  20.6 us
    dot_general x10, matrix products, product(): jnp.einsum(pattern, left_re, right_re, precision=HIGHEST)  19.7 us
    dot_general x9, matrix products, product(): jnp.einsum(pattern, left_re, right_im, precision=HIGHEST)  19.1 us
    all_to_all x1, waiting for transfers between devices, send_features(): lax.all_to_all(features, 'context', split_axis=1, concat_axis=0, tiled=True)  16.4 us
  transfers between devices with their start and end apart: 6, of which 3 were waited for; matrix products, arithmetic and copies ran while one was open for 12% of the time, Pallas kernels for 0%

commit v1 on v0

v1 whole, which is shorter than its diff:
```python
import math

import jax
import jax.numpy as jnp
from jax import lax
from jax.experimental import pallas as pl
from jax.experimental.pallas import tpu as pltpu
from jax.sharding import Mesh, PartitionSpec as P

BF16, F32 = jnp.bfloat16, jnp.float32
LANES = 128
AXES = ("s", "yl", "x", "z", "c")
SIZES = (2, 2, 4, 8, 2)
VMEM = pl.BlockSpec(memory_space=pltpu.VMEM)


def toeplitz_kernel(taps_ref, out_ref, rows):
    blocks = out_ref.shape[0] // LANES
    source = lax.broadcasted_iota(jnp.int32, (2 * LANES, 2 * LANES), 0)
    target = lax.broadcasted_iota(jnp.int32, (2 * LANES, 2 * LANES), 1)
    select = source == 2 * (LANES - 1 - target % LANES) + target // LANES

    @pl.when(pl.program_id(0) == 0)
    def _():
        chosen = jnp.dot(
            taps_ref[...],
            select.astype(F32),
            precision=lax.Precision.HIGHEST,
            preferred_element_type=F32,
        )
        for parity in range(2):
            rows[parity, 0:8, :] = jnp.zeros((8, LANES), F32)
            rows[parity, 8:, :] = chosen[:, parity * LANES : (parity + 1) * LANES]

    keep = lax.broadcasted_iota(jnp.int32, (LANES, LANES), 1) < LANES - 1 - lax.broadcasted_iota(
        jnp.int32, (LANES, LANES), 0
    )
    first = pl.program_id(0) * blocks

    def body(m, carry):
        row = pl.multiple_of(m * LANES, LANES)
        for parity in range(2):
            before = jnp.broadcast_to(rows[parity, pl.ds(first + m + 7, 1), :], (LANES, LANES))
            here = jnp.broadcast_to(rows[parity, pl.ds(first + m + 8, 1), :], (LANES, LANES))
            tile = pltpu.roll(jnp.where(keep, before, here), 1, 1, stride=1, stride_axis=0)
            high = tile.astype(BF16)
            out_ref[pl.ds(row, LANES), parity * LANES : (parity + 1) * LANES] = high
            out_ref[pl.ds(row, LANES), (2 + parity) * LANES : (3 + parity) * LANES] = (
                tile - high.astype(F32)
            ).astype(BF16)
        return carry

    lax.fori_loop(0, blocks, body, 0, unroll=4)


def toeplitz(filter_taps):
    count = filter_taps.shape[0] // 2
    parts = 8
    return pl.pallas_call(
        toeplitz_kernel,
        grid=(parts,),
        out_shape=pltpu.MemorySpace.HBM((count, 4 * LANES), BF16),
        in_specs=[pl.BlockSpec((count // LANES, 2 * LANES), lambda i: (0, 0))],
        out_specs=pl.BlockSpec((count // parts, 4 * LANES), lambda i: (i, 0)),
        scratch_shapes=[pltpu.VMEM((2, count // LANES + 8, LANES), F32)],
        compiler_params=pltpu.CompilerParams(vmem_limit_bytes=16 << 20),
        cost_estimate=pl.CostEstimate(
            flops=count * 2048, bytes_accessed=count * 1024, transcendentals=0
        ),
    )(filter_taps.reshape(count // LANES, 2 * LANES))


SHIFTS = 8
GROUPS = 8


def filter_kernel(signal_ref, taps_ref, out_ref, left, total):
    blocks = signal_ref.shape[0] - SHIFTS
    rows = blocks * 8
    steps = blocks // SHIFTS
    per = steps // GROUPS

    step = pl.program_id(0)

    def fill(i, carry):
        row = pl.multiple_of(i * LANES, LANES)
        for d in range(SHIFTS):
            left[pl.ds(row, LANES), d * LANES : (d + 1) * LANES] = (
                signal_ref[pl.ds(i * 16 + d, 16)].astype(F32).reshape(LANES, LANES).astype(BF16)
            )
        total[pl.ds(row, LANES), :] = jnp.zeros((LANES, 2 * LANES), F32)
        return carry

    @pl.when(step == 0)
    def _():
        lax.fori_loop(0, blocks // 16, fill, 0)
        left[rows:, :] = jnp.zeros_like(left[rows:, :])
        total[rows:, :] = jnp.zeros_like(total[rows:, :])

    for g in range(GROUPS):
        count = rows - g * per * SHIFTS * 8

        @pl.when(step // per == g)
        def _(count=count):
            a = left[pl.ds(pl.multiple_of(step * SHIFTS * 8, SHIFTS * 8), count), :]
            y = jnp.dot(a, taps_ref[...], preferred_element_type=F32)
            total[0:count, :] += y[:, : 2 * LANES] + y[:, 2 * LANES :]

    lane = lax.broadcasted_iota(jnp.int32, (8, LANES), 1)
    sublane = lax.broadcasted_iota(jnp.int32, (8, LANES), 0)
    _, y_count, z_count, c_count, x_count = out_ref.shape[:5]

    def finish(i, carry):
        yx, z = i // z_count, i % z_count
        y, x = yx // x_count, yx % x_count
        for c in range(c_count):
            row = pl.multiple_of((i * c_count + c) * 8, 8)
            same = total[pl.ds(row, 8), :LANES]
            cross = total[pl.ds(row, 8), LANES:]
            after = total[pl.ds(pl.multiple_of(row + 8, 8), 8), LANES:]
            moved = pltpu.roll(jnp.where(lane == 0, after, cross), LANES - 1, 1)
            other = pltpu.roll(jnp.where(sublane < 4, moved, cross), 4, 0)
            out_ref[0, y, z, c, x] = (same + other).astype(BF16)
            out_ref[1, y, z, c, x] = (same - other).astype(BF16)
        return carry

    @pl.when(step == steps - 1)
    def _():
        lax.fori_loop(0, blocks // c_count, finish, 0, unroll=4)


def filtered(signal, taps, sizes):
    s, yl, x, z, c = sizes
    blocks = signal.shape[0]
    padded = jnp.concatenate([signal, jnp.zeros((SHIFTS,) + signal.shape[1:], BF16)], 0)
    depth = SHIFTS * LANES
    return pl.pallas_call(
        filter_kernel,
        grid=(blocks // SHIFTS,),
        out_shape=jax.ShapeDtypeStruct((s, yl, z, c, x, 8, LANES), BF16),
        in_specs=[
            pl.BlockSpec(padded.shape, lambda i: (0, 0, 0)),
            pl.BlockSpec((depth, 4 * LANES), lambda i: (i, 0)),
        ],
        out_specs=pl.BlockSpec((s, yl, z, c, x, 8, LANES), lambda i: (0,) * 7),
        scratch_shapes=[
            pltpu.VMEM((blocks * 8 + LANES, depth), BF16),
            pltpu.VMEM((blocks * 8 + 8, 2 * LANES), F32),
        ],
        compiler_params=pltpu.CompilerParams(vmem_limit_bytes=24 << 20),
    )(padded, taps)


def along(array, axis, size, offset):
    return lax.ppermute(array, axis, [(i, (i + offset) % size) for i in range(size)])


def body(inputs, cotangent, weights, filter_taps):
    sizes = SIZES
    s, yl, x, z, c = sizes
    tokens, width = inputs.shape
    half = tokens // 2
    groups = yl * x * z * c
    sign, x_here, c_here = (lax.axis_index(name) for name in ("s", "x", "c"))
    row = lax.broadcasted_iota(jnp.int32, (tokens, tokens), 0)
    col = lax.broadcasted_iota(jnp.int32, (tokens, tokens), 1)
    order = (row == 2 * (col % half) + col // half).astype(BF16)
    taps = toeplitz(filter_taps)

    turned = lax.dot_general(
        cotangent, order, (((0,), (0,)), ((), ())), preferred_element_type=F32
    ).astype(BF16)
    chosen = lax.dynamic_index_in_dim(
        turned.reshape(groups, s, 4, 2, half), sign, 1, keepdims=False
    )
    send = chosen.transpose(0, 2, 1, 3).reshape(groups, 8, half)
    signal = lax.all_to_all(send, ("yl", "x", "z", "c"), split_axis=0, concat_axis=0, tiled=True)

    sorted_inputs = lax.dot_general(
        order, inputs, (((0,), (0,)), ((), ())), preferred_element_type=F32
    ).astype(BF16)
    gathered = [sorted_inputs] + [along(sorted_inputs, "x", x, k) for k in range(1, x)]
    split = weights[0].reshape(yl, x, z, c, s, 4, width)
    rows = jnp.stack(
        [lax.dynamic_index_in_dim(split, (x_here - k) % x, 1, keepdims=False) for k in range(x)]
    )
    rows = rows.transpose(0, 4, 1, 2, 3, 5, 6).reshape(width, width)

    signal, rows, gathered = lax.optimization_barrier((signal, rows, gathered))
    result = filtered(signal, taps, sizes).reshape(s * yl * z * c, x, 8, half)
    spread = lax.all_to_all(result, ("s", "yl", "z", "c"), split_axis=0, concat_axis=0, tiled=True)
    home = [
        along(
            lax.dynamic_index_in_dim(spread, (x_here + k) % x, 1, keepdims=False), "x", x, k
        )
        if k
        else lax.dynamic_index_in_dim(spread, x_here, 1, keepdims=False)
        for k in range(x)
    ]

    partial = 0
    for k in range(x):
        block = lax.dynamic_index_in_dim(spread, (x_here - k) % x, 1, keepdims=False)
        partial = partial + jnp.einsum(
            "qpka,pae->qke",
            block.reshape(s * yl * z * c, 2, 4, half),
            gathered[k].reshape(2, half, width),
            preferred_element_type=F32,
        )
    partial = partial.reshape(s, yl, z, c, 4, width).transpose(3, 1, 2, 0, 4, 5)
    partial = partial.reshape(c, yl * z, 8, width)
    other = lax.dynamic_index_in_dim(partial, 1 - c_here, 0, keepdims=False).astype(BF16)
    own = lax.dynamic_index_in_dim(partial, c_here, 0, keepdims=False)
    reduced = own + along(other, "c", c, 1).astype(F32)
    pieces = lax.all_to_all(
        reduced.astype(BF16), ("yl", "z"), split_axis=0, concat_axis=0, tiled=True
    )
    grad_scale = 1.0 / math.sqrt(tokens * groups)
    weight_grad = jnp.sum(pieces.astype(F32), 0) * grad_scale

    columns = jnp.stack(home).reshape(groups * s, 2, 4, half).transpose(1, 0, 2, 3)
    columns = columns.reshape(2, width, half)

    def project(side):
        matrix = lax.dynamic_slice_in_dim(rows, side * (width // 2), width // 2, 1)
        return jnp.einsum("pda,de->pae", columns, matrix, preferred_element_type=F32).astype(BF16)

    arrived = along(project(1 - sign), "s", s, 1)
    both = jnp.stack([project(sign), arrived]).reshape(2, tokens, width // 2)
    input_grad = jnp.einsum("tu,nue->te", order, both, preferred_element_type=F32).astype(BF16)
    return input_grad, weight_grad[None]


def solution(mesh):
    fine = Mesh(mesh.devices.reshape(SIZES), AXES)
    context = ("yl", "x", "z", "c")
    in_specs = (P(context, None), P(context, None), P("s", None, None), P())
    out_specs = (P(context, "s"), P("s", context, None))
    return jax.shard_map(body, mesh=fine, in_specs=in_specs, out_specs=out_specs, check_vma=False)
```

time: 781 us -> 131 us (0.17); the launches traced: 771 us -> 130 us
  waiting for transfers between devices: 583 us -> 24 us
  matrix products: 92.9 us -> 9.72 us
  Pallas kernels: 0 us -> 25.9 us
  between operations: 15.3 us -> 1.17 us
    unnamed x3 -> x0, waiting for transfers between devices: 561 us -> none
    dot_general x40 -> x9, matrix products: 92.9 us -> 9.72 us  [the longest x4 5.39 us: body(): jnp.einsum('qpka,pae->qke', block.reshape(s * yl * z * c, 2, 4, half), ga...]
    pallas_call x0 -> x2, Pallas kernels: none -> 25.9 us  [the longest x1 15.8 us: filtered(): pl.pallas_call(filter_kernel, grid=(blocks // SHIFTS,), out_shape=jax.Sha...]
    all_to_all x4 -> x3, starting transfers between devices: 48.7 us -> 26.4 us  [the longest x1 12.4 us: body(): lax.all_to_all(send, ('yl', 'x', 'z', 'c'), split_axis=0, concat_axis=0,...]
    ppermute x0 -> x8, starting transfers between devices: none -> 14.8 us  [along(): lax.ppermute(array, axis, [(i, (i + offset) % size) for i in range(size)])]
    all_to_all x4 -> x3, waiting for transfers between devices: 22.4 us -> 21.6 us  [the longest x1 17.3 us: body(): lax.all_to_all(result, ('s', 'yl', 'z', 'c'), split_axis=0, concat_axis=0...]
  transfers between devices with their start and end apart: 6 -> 11, of which waited for: 3 -> 3; matrix products, arithmetic and copies ran while one was open for 12% -> 23% of each run, Pallas kernels for 0% -> 8%
where the time goes in v1:
time: 131 us; the launch traced here: 130 us
  starting transfers between devices  41.2 us (31%)
  Pallas kernels  25.9 us (20%)
  waiting for transfers between devices  24 us (18%)
  local copies, waits for them, and re-layouts  22.9 us (17%)
  matrix products  9.72 us (7%)
  other arithmetic  4.76 us (4%)
    all_to_all x1, waiting for transfers between devices, body(): lax.all_to_all(result, ('s', 'yl', 'z', 'c'), split_axis=0, concat_axis=0...  17.3 us
    pallas_call x1, Pallas kernels, filtered(): pl.pallas_call(filter_kernel, grid=(blocks // SHIFTS,), out_shape=jax.Sha...  15.8 us
    ppermute x8, starting transfers between devices, along(): lax.ppermute(array, axis, [(i, (i + offset) % size) for i in range(size)])  14.8 us
    all_to_all x1, starting transfers between devices, body(): lax.all_to_all(send, ('yl', 'x', 'z', 'c'), split_axis=0, concat_axis=0,...  12.4 us
    all_to_all x1, starting transfers between devices, body(): lax.all_to_all(result, ('s', 'yl', 'z', 'c'), split_axis=0, concat_axis=0...  10.5 us
    pallas_call x1, Pallas kernels, toeplitz(): pl.pallas_call(toeplitz_kernel, grid=(parts,), out_shape=pltpu.MemorySpac...  10 us
    unnamed x20, local copies, waits for them, and re-layouts  6.86 us
    dot_general x4, matrix products, body(): jnp.einsum('qpka,pae->qke', block.reshape(s * yl * z * c, 2, 4, half), ga...  5.39 us
  transfers between devices with their start and end apart: 11, of which 3 were waited for; matrix products, arithmetic and copies ran while one was open for 23% of the time, Pallas kernels for 8%

profile of v1, /device:TPU:1, one launch (start us, length us, event | category | flops | bytes accessed | tf_op | source)
XLA Modules:
  0.0 129.6 jit_solution(3847092773620934543)
XLA Ops:
  0.6 0.0 copy-start
  0.7 1.0 copy-done
  1.7 0.3 convolution_convert_fusion
  2.0 2.1 %collective-permute-start = (bf16[256,1024]{1,0:T(8,128)(2,1)S(1)}, bf16[256,1024]{1,0:T(8,128)(2,1)}, u32[]{:S(2)}, u32[]{:S(2)}) collective-permute-start(bf16[256,1024]{1,0:T(8,128)(2,1)S(1)} %convolution_convert_fusion), channel_id=1, source_target_pairs={{0,16},{16,32},{32,48},{48,0},{1,17},{17,33},{33,49},{49,1},{2,18}... | collective-permute-start | bytes 1572872 | tf_op jit(solution)/shard_map/ppermute | solution.py:155
  4.2 2.4 %collective-permute-start.1 = (bf16[256,1024]{1,0:T(8,128)(2,1)S(1)}, bf16[256,1024]{1,0:T(8,128)(2,1)}, u32[]{:S(2)}, u32[]{:S(2)}) collective-permute-start(bf16[256,1024]{1,0:T(8,128)(2,1)S(1)} %convolution_convert_fusion), channel_id=1, source_target_pairs={{0,32},{16,48},{32,0},{48,16},{1,33},{17,49},{33,1},{49,17},{2,34}... | collective-permute-start | bytes 1572872 | tf_op jit(solution)/shard_map/ppermute | solution.py:155
  6.6 1.2 collective-permute-start.2
  7.8 1.4 %fusion.3 = bf16[1024,256]{0,1:T(8,128)(2,1)S(1)} fusion(bf16[256,1024]{1,0:T(8,128)(2,1)} %param.5, s32[256]{0:T(256)S(1)} %get-tuple-element.28, s32[256]{0:T(256)S(1)} %get-tuple-element.31, s32[256]{0:T(256)S(1)} %get-tuple-element.29, s32[256]{0:T(256)S(1)} %get-tuple-element.30, pred[256]{0:T(512)(128)(4,1)S(1)} %get-tuple-element.26, ...), kind=kOutput, calls=%fused_computation.10 | convolution fusion | flops 134807552 | bytes 1053184 | tf_op jit(solution)/shard_map/dot_general | solution.py:170
  9.2 0.2 copy.37
  9.4 0.1 reshape.79
  9.5 0.2 constant_dynamic-slice_fusion.12
  9.8 0.9 copy.39
  10.7 12.4 %all-to-all-start = ((bf16[128,8,128]{2,1,0:T(8,128)(2,1)}), bf16[128,8,128]{2,1,0:T(8,128)(2,1)S(1)}, u32[]{:S(2)}, u32[]{:S(2)}) async-start(bf16[128,8,128]{2,1,0:T(8,128)(2,1)} %bitcast.3), calls=%async_computation | async-start | bytes 524288 | tf_op jit(solution)/shard_map/all_to_all | solution.py:177
  23.1 2.7 %reshape_squeeze.3 = bf16[2,4,8,2,2,4,1024]{6,5,4,3,2,1,0:T(4,128)(2,1)S(1)} reshape(bf16[1,1024,1024]{2,1,0:T(8,128)(2,1)} %param.6) | data formatting | bytes 4194304 | tf_op jit(solution)/shard_map/reshape;squeeze | solution.py:183
  25.9 1.1 constant_dynamic-slice_fusion.11
  27.0 0.6 copy_bitcast_fusion.2
  27.6 0.6 copy_bitcast_fusion
  28.3 2.9 %maximum_bitcast_fusion = bf16[4,2,2,8,2,4,1024]{6,5,4,3,2,1,0:T(4,128)(2,1)} fusion(bf16[1,2,8,2,2,4,1024]{6,5,3,2,1,4,0:T(4,128)(2,1)S(1)} %get-tuple-element.32, bf16[1,2,8,2,2,4,1024]{6,5,3,2,1,4,0:T(4,128)(2,1)S(1)} %get-tuple-element.33, bf16[1,2,8,2,2,4,1024]{6,5,3,2,1,4,0:T(4,128)(2,1)S(1)} %get-tuple-element.34, ...), kind=kLoop, calls=%fused_computation | loop fusion | flops 3145728 | bytes 4194304 | tf_op jit(solution)/shard_map/transpose | solution.py:187
  31.2 2.5 %reshape.81 = bf16[1024,1024]{1,0:T(8,128)(2,1)S(1)} reshape(bf16[4,2,2,8,2,4,1024]{6,5,4,3,2,1,0:T(4,128)(2,1)} %maximum_bitcast_fusion) | data formatting | bytes 4194304 | tf_op jit(solution)/shard_map/reshape | solution.py:187
  33.7 0.9 reshape.82.taps_ref
  34.7 10.0 %shard_map.59.taps_ref = bf16[16384,512]{1,0:T(8,128)(2,1)} custom-call(f32[128,256]{1,0:T(8,128)S(1)} %reshape.82.taps_ref), custom_call_target="tpu_custom_call" | custom-call | flops 33554432 | bytes 16777216 | tf_op jit(solution)/shard_map/pallas_call | solution.py:59
  44.8 5.8 %copy-done.1 = bf16[16384,512]{1,0:T(8,128)(2,1)S(1)} copy-done((bf16[16384,512]{1,0:T(8,128)(2,1)S(1)}, bf16[16384,512]{1,0:T(8,128)(2,1)}, u32[]{:S(2)}) %copy-start.1) | copy-done | bytes 16777240
  50.6 15.8 %shard_map.60 = bf16[2,2,8,2,4,8,128]{6,5,4,3,2,1,0:T(8,128)(2,1)} custom-call(bf16[136,8,128]{2,1,0:T(8,128)(2,1)S(1)} %concatenate.4.signal_ref, bf16[16384,512]{1,0:T(8,128)(2,1)S(1)} %copy-done.1), custom_call_target="tpu_custom_call" | custom-call | tf_op jit(solution)/shard_map/pallas_call | solution.py:137
  66.4 10.5 %all-to-all-start.1 = ((bf16[64,4,8,128]{3,2,1,0:T(8,128)(2,1)}), bf16[64,4,8,128]{3,2,1,0:T(8,128)(2,1)S(1)}, u32[]{:S(2)}, u32[]{:S(2)}) async-start(bf16[64,4,8,128]{3,2,1,0:T(8,128)(2,1)} %bitcast.9), calls=%async_computation.1 | async-start | bytes 1048576 | tf_op jit(solution)/shard_map/all_to_all | solution.py:191
  76.9 17.3 %all-to-all-done.1 = bf16[64,4,8,128]{3,2,1,0:T(8,128)(2,1)S(1)} async-done(((bf16[64,4,8,128]{3,2,1,0:T(8,128)(2,1)}), bf16[64,4,8,128]{3,2,1,0:T(8,128)(2,1)S(1)}, u32[]{:S(2)}, u32[]{:S(2)}) %all-to-all-start.1) | async-done | bytes 524320 | tf_op jit(solution)/shard_map/all_to_all | solution.py:191
  94.2 0.2 constant_dynamic-slice_fusion.3
  94.5 1.4 %collective-permute-start.3 = (bf16[64,8,128]{2,0,1:T(8,128)(2,1)S(1)}, bf16[64,8,128]{2,0,1:T(8,128)(2,1)S(1)}, u32[]{:S(2)}, u32[]{:S(2)}) collective-permute-start(bf16[64,8,128]{2,0,1:T(8,128)(2,1)S(1)} %bitcast.123), channel_id=1, source_target_pairs={{0,16},{16,32},{32,48},{48,0},{1,17},{17,33},{33,49},{49,1},{2,18}... | collective-permute-start | bytes 393224 | tf_op jit(solution)/shard_map/ppermute | solution.py:155
  95.9 2.7 %collective-permute-start.4 = (bf16[64,8,128]{2,0,1:T(8,128)(2,1)S(1)}, bf16[64,8,128]{2,0,1:T(8,128)(2,1)S(1)}, u32[]{:S(2)}, u32[]{:S(2)}) collective-permute-start(bf16[64,8,128]{2,0,1:T(8,128)(2,1)S(1)} %bitcast.124), channel_id=1, source_target_pairs={{0,32},{16,48},{32,0},{48,16},{1,33},{17,49},{33,1},{49,17},{2,34}... | collective-permute-start | bytes 393224 | tf_op jit(solution)/shard_map/ppermute | solution.py:155
  98.6 1.4 %collective-permute-start.5 = (bf16[64,8,128]{2,0,1:T(8,128)(2,1)S(1)}, bf16[64,8,128]{2,0,1:T(8,128)(2,1)S(1)}, u32[]{:S(2)}, u32[]{:S(2)}) collective-permute-start(bf16[64,8,128]{2,0,1:T(8,128)(2,1)S(1)} %bitcast.125), channel_id=1, source_target_pairs={{0,48},{16,0},{32,16},{48,32},{1,49},{17,1},{33,17},{49,33},{2,50}... | collective-permute-start | bytes 393224 | tf_op jit(solution)/shard_map/ppermute | solution.py:155
  100.0 1.3 %convolution_bitcast_fusion.2 = f32[64,4,1024]{2,0,1:T(8,128)S(1)} fusion(bf16[64,2,4,128]{3,0,2,1:T(8,128)(2,1)S(1)} %bitcast.121, bf16[2,128,1024,1]{2,1,3,0:T(8,128)(2,1)} %bitcast.32), kind=kOutput, calls=%fused_computation.3 | convolution fusion | flops 134217728 | bytes 1703936 | tf_op jit(solution)/shard_map/qpka,pae->qke/dot_general | solution.py:204
  101.4 1.4 %convolution_bitcast_fusion.1 = f32[64,4,1024]{2,0,1:T(8,128)S(1)} fusion(bf16[64,2,4,128]{3,0,2,1:T(8,128)(2,1)S(1)} %bitcast.120, bf16[2,128,1024,1]{2,1,3,0:T(8,128)(2,1)} %bitcast.37), kind=kOutput, calls=%fused_computation.2 | convolution fusion | flops 134217728 | bytes 1703936 | tf_op jit(solution)/shard_map/qpka,pae->qke/dot_general | solution.py:204
  102.8 1.3 %convolution_bitcast_fusion = f32[64,4,1024]{2,0,1:T(8,128)S(1)} fusion(bf16[64,2,4,128]{3,0,2,1:T(8,128)(2,1)S(1)} %bitcast.119, bf16[2,128,1024,1]{2,1,3,0:T(8,128)(2,1)} %bitcast.42), kind=kOutput, calls=%fused_computation.1 | convolution fusion | flops 134217728 | bytes 1703936 | tf_op jit(solution)/shard_map/qpka,pae->qke/dot_general | solution.py:204
  104.1 1.3 %fusion.2 = f32[64,4,1024]{2,0,1:T(8,128)} fusion(f32[64,4,1024]{2,0,1:T(8,128)S(1)} %convolution_bitcast_fusion, f32[64,4,1024]{2,0,1:T(8,128)S(1)} %convolution_bitcast_fusion.1, f32[64,4,1024]{2,0,1:T(8,128)S(1)} %convolution_bitcast_fusion.2, bf16[64,2,4,128]{3,0,2,1:T(8,128)(2,1)S(1)} %bitcast.118, bf16[2,128,1024,1]{2,1,3,0:T(8,128)(2,1)S(1)} %bitcast.117), kind=kOutput, calls=%fused_computation.7 | convolution fusion | flops 135004160 | bytes 4849664 | tf_op jit(solution)/shard_map/qpka,pae->qke/dot_general | solution.py:204
  105.4 2.8 %reshape.94 = f32[2,2,8,2,4,1024]{5,3,2,1,0,4:T(2,128)} reshape(f32[64,4,1024]{2,0,1:T(8,128)} %fusion.2) | data formatting | bytes 2097152 | tf_op jit(solution)/shard_map/reshape | solution.py:210
  108.2 1.6 %copy.55 = f32[2,2,8,2,4,1024]{5,2,1,4,0,3:T(8,128)S(1)} copy(f32[2,2,8,2,4,1024]{5,3,2,1,0,4:T(2,128)} %reshape.94) | data formatting | bytes 2097152 | tf_op jit(solution)/shard_map/reshape | solution.py:210
  109.9 1.2 collective-permute-start.7
  111.2 0.1 pad_maximum_fusion
  111.2 0.4 copy.48
  111.7 1.2 convolution_convert_fusion.3
  112.8 2.4 %collective-permute-start.6 = (bf16[2,128,512]{2,1,0:T(8,128)(2,1)}, bf16[2,128,512]{2,1,0:T(8,128)(2,1)}, u32[]{:S(2)}, u32[]{:S(2)}) collective-permute-start(bf16[2,128,512]{2,1,0:T(8,128)(2,1)} %convolution_convert_fusion.3), channel_id=1, source_target_pairs={{0,128},{128,0},{1,129},{129,1},{2,130},{130,2},{3,131},{131,3},{4... | collective-permute-start | bytes 786440 | tf_op jit(solution)/shard_map/ppermute | solution.py:155
  115.2 0.1 fusion.8
  115.3 0.8 copy.56
  116.2 3.5 %all-to-all-start.2 = ((bf16[16,8,1024]{2,1,0:T(8,128)(2,1)}), bf16[16,8,1024]{2,1,0:T(8,128)(2,1)S(1)}, u32[]{:S(2)}, u32[]{:S(2)}) async-start(bf16[16,8,1024]{2,1,0:T(8,128)(2,1)} %copy.56), calls=%async_computation.2 | async-start | bytes 524288 | tf_op jit(solution)/shard_map/all_to_all | solution.py:215
  119.7 0.5 convolution_convert_fusion.4
  120.2 2.4 %collective-permute-done.6 = bf16[2,128,512]{2,1,0:T(8,128)(2,1)} collective-permute-done((bf16[2,128,512]{2,1,0:T(8,128)(2,1)}, bf16[2,128,512]{2,1,0:T(8,128)(2,1)}, u32[]{:S(2)}, u32[]{:S(2)}) %collective-permute-start.6) | collective-permute-done | bytes 262176 | tf_op jit(solution)/shard_map/ppermute | solution.py:155
  122.6 1.0 convert_reduce_fusion
  123.6 1.0 convolution_convert_fusion.2
  124.6 4.4 %all-to-all-done.2 = bf16[16,8,1024]{2,1,0:T(8,128)(2,1)S(1)} async-done(((bf16[16,8,1024]{2,1,0:T(8,128)(2,1)}), bf16[16,8,1024]{2,1,0:T(8,128)(2,1)S(1)}, u32[]{:S(2)}, u32[]{:S(2)}) %all-to-all-start.2) | async-done | bytes 262176 | tf_op jit(solution)/shard_map/all_to_all | solution.py:215
  129.0 0.6 multiply_bitcast_fusion
  (36 shorter events, 0.4 us)
Async XLA Ops:
  0.6 1.1 copy-start
  0.7 7.1 %copy-start.4 = (pred[256]{0:T(512)(128)(4,1)}, pred[256]{0:T(512)(128)(4,1)S(1)}, u32[]{:S(2)}) copy-start(pred[256]{0:T(512)(128)(4,1)S(1)} %get-tuple-element.26) | copy-start | bytes 772
  0.7 7.1 %copy-start.6 = (pred[256]{0:T(512)(128)(4,1)}, pred[256]{0:T(512)(128)(4,1)S(1)}, u32[]{:S(2)}) copy-start(pred[256]{0:T(512)(128)(4,1)S(1)} %get-tuple-element.27) | copy-start | bytes 772
  2.0 7.7 %copy-start.2 = (bf16[256,1024]{1,0:T(8,128)(2,1)}, bf16[256,1024]{1,0:T(8,128)(2,1)S(1)}, u32[]{:S(2)}) copy-start(bf16[256,1024]{1,0:T(8,128)(2,1)S(1)} %convolution_convert_fusion) | copy-start | bytes 1572868
  2.0 42.7 %collective-permute-start = (bf16[256,1024]{1,0:T(8,128)(2,1)S(1)}, bf16[256,1024]{1,0:T(8,128)(2,1)}, u32[]{:S(2)}, u32[]{:S(2)}) collective-permute-start(bf16[256,1024]{1,0:T(8,128)(2,1)S(1)} %convolution_convert_fusion), channel_id=1, source_target_pairs={{0,16},{16,32},{32,48},{48,0},{1,17},{17,33},{33,49},{49,1},{2,18}... | collective-permute-start | bytes 1572872 | tf_op jit(solution)/shard_map/ppermute | solution.py:155
  4.2 40.6 %collective-permute-start.1 = (bf16[256,1024]{1,0:T(8,128)(2,1)S(1)}, bf16[256,1024]{1,0:T(8,128)(2,1)}, u32[]{:S(2)}, u32[]{:S(2)}) collective-permute-start(bf16[256,1024]{1,0:T(8,128)(2,1)S(1)} %convolution_convert_fusion), channel_id=1, source_target_pairs={{0,32},{16,48},{32,0},{48,16},{1,33},{17,49},{33,1},{49,17},{2,34}... | collective-permute-start | bytes 1572872 | tf_op jit(solution)/shard_map/ppermute | solution.py:155
  6.6 38.1 %collective-permute-start.2 = (bf16[256,1024]{1,0:T(8,128)(2,1)S(1)}, bf16[256,1024]{1,0:T(8,128)(2,1)}, u32[]{:S(2)}, u32[]{:S(2)}) collective-permute-start(bf16[256,1024]{1,0:T(8,128)(2,1)S(1)} %convolution_convert_fusion), channel_id=1, source_target_pairs={{0,48},{16,0},{32,16},{48,32},{1,49},{17,1},{33,17},{49,33},{2,50}... | collective-permute-start | bytes 1572872 | tf_op jit(solution)/shard_map/ppermute | solution.py:155
  10.7 34.1 %all-to-all-start = ((bf16[128,8,128]{2,1,0:T(8,128)(2,1)}), bf16[128,8,128]{2,1,0:T(8,128)(2,1)S(1)}, u32[]{:S(2)}, u32[]{:S(2)}) async-start(bf16[128,8,128]{2,1,0:T(8,128)(2,1)} %bitcast.3), calls=%async_computation | async-start | bytes 524288 | tf_op jit(solution)/shard_map/all_to_all | solution.py:177
  44.8 5.8 %copy-start.1 = (bf16[16384,512]{1,0:T(8,128)(2,1)S(1)}, bf16[16384,512]{1,0:T(8,128)(2,1)}, u32[]{:S(2)}) copy-start(bf16[16384,512]{1,0:T(8,128)(2,1)} %shard_map.59.taps_ref) | copy-start | bytes 50331652
  66.4 27.8 %all-to-all-start.1 = ((bf16[64,4,8,128]{3,2,1,0:T(8,128)(2,1)}), bf16[64,4,8,128]{3,2,1,0:T(8,128)(2,1)S(1)}, u32[]{:S(2)}, u32[]{:S(2)}) async-start(bf16[64,4,8,128]{3,2,1,0:T(8,128)(2,1)} %bitcast.9), calls=%async_computation.1 | async-start | bytes 1048576 | tf_op jit(solution)/shard_map/all_to_all | solution.py:191
  94.5 16.6 %collective-permute-start.3 = (bf16[64,8,128]{2,0,1:T(8,128)(2,1)S(1)}, bf16[64,8,128]{2,0,1:T(8,128)(2,1)S(1)}, u32[]{:S(2)}, u32[]{:S(2)}) collective-permute-start(bf16[64,8,128]{2,0,1:T(8,128)(2,1)S(1)} %bitcast.123), channel_id=1, source_target_pairs={{0,16},{16,32},{32,48},{48,0},{1,17},{17,33},{33,49},{49,1},{2,18}... | collective-permute-start | bytes 393224 | tf_op jit(solution)/shard_map/ppermute | solution.py:155
  95.9 15.2 %collective-permute-start.4 = (bf16[64,8,128]{2,0,1:T(8,128)(2,1)S(1)}, bf16[64,8,128]{2,0,1:T(8,128)(2,1)S(1)}, u32[]{:S(2)}, u32[]{:S(2)}) collective-permute-start(bf16[64,8,128]{2,0,1:T(8,128)(2,1)S(1)} %bitcast.124), channel_id=1, source_target_pairs={{0,32},{16,48},{32,0},{48,16},{1,33},{17,49},{33,1},{49,17},{2,34}... | collective-permute-start | bytes 393224 | tf_op jit(solution)/shard_map/ppermute | solution.py:155
  98.6 12.5 %collective-permute-start.5 = (bf16[64,8,128]{2,0,1:T(8,128)(2,1)S(1)}, bf16[64,8,128]{2,0,1:T(8,128)(2,1)S(1)}, u32[]{:S(2)}, u32[]{:S(2)}) collective-permute-start(bf16[64,8,128]{2,0,1:T(8,128)(2,1)S(1)} %bitcast.125), channel_id=1, source_target_pairs={{0,48},{16,0},{32,16},{48,32},{1,49},{17,1},{33,17},{49,33},{2,50}... | collective-permute-start | bytes 393224 | tf_op jit(solution)/shard_map/ppermute | solution.py:155
  101.4 2.8 %copy-start.3 = (bf16[256,1024]{1,0:T(8,128)(2,1)S(1)}, bf16[256,1024]{1,0:T(8,128)(2,1)}, u32[]{:S(2)}) copy-start(bf16[256,1024]{1,0:T(8,128)(2,1)} %copy-done.2) | copy-start | bytes 1572868
  109.9 5.4 %collective-permute-start.7 = (bf16[16,8,1024]{2,0,1:T(8,128)(2,1)S(1)}, bf16[16,8,1024]{2,0,1:T(8,128)(2,1)S(1)}, u32[]{:S(2)}, u32[]{:S(2)}) collective-permute-start(bf16[16,8,1024]{2,0,1:T(8,128)(2,1)S(1)} %fusion.9), channel_id=1, source_target_pairs={{0,1},{1,0},{2,3},{3,2},{4,5},{5,4},{6,7},{7,6},{8,9},{9,8},{10,11... | collective-permute-start | bytes 786440 | tf_op jit(solution)/shard_map/ppermute | solution.py:155
  112.8 9.7 %collective-permute-start.6 = (bf16[2,128,512]{2,1,0:T(8,128)(2,1)}, bf16[2,128,512]{2,1,0:T(8,128)(2,1)}, u32[]{:S(2)}, u32[]{:S(2)}) collective-permute-start(bf16[2,128,512]{2,1,0:T(8,128)(2,1)} %convolution_convert_fusion.3), channel_id=1, source_target_pairs={{0,128},{128,0},{1,129},{129,1},{2,130},{130,2},{3,131},{131,3},{4... | collective-permute-start | bytes 786440 | tf_op jit(solution)/shard_map/ppermute | solution.py:155
  115.3 8.3 %copy-start.5 = (pred[256]{0:T(512)(128)(4,1)S(1)}, pred[256]{0:T(512)(128)(4,1)}, u32[]{:S(2)}) copy-start(pred[256]{0:T(512)(128)(4,1)} %copy-done.4) | copy-start | bytes 772
  115.3 8.3 %copy-start.7 = (pred[256]{0:T(512)(128)(4,1)S(1)}, pred[256]{0:T(512)(128)(4,1)}, u32[]{:S(2)}) copy-start(pred[256]{0:T(512)(128)(4,1)} %copy-done.6) | copy-start | bytes 772
  116.2 12.7 %all-to-all-start.2 = ((bf16[16,8,1024]{2,1,0:T(8,128)(2,1)}), bf16[16,8,1024]{2,1,0:T(8,128)(2,1)S(1)}, u32[]{:S(2)}, u32[]{:S(2)}) async-start(bf16[16,8,1024]{2,1,0:T(8,128)(2,1)} %copy.56), calls=%async_computation.2 | async-start | bytes 524288 | tf_op jit(solution)/shard_map/all_to_all | solution.py:215

commit v2 on v1

v2 whole, which is shorter than its diff:
```python
import math

import jax
import jax.numpy as jnp
from jax import lax
from jax.experimental import pallas as pl
from jax.experimental.pallas import tpu as pltpu
from jax.sharding import Mesh, PartitionSpec as P

BF16, F32 = jnp.bfloat16, jnp.float32
LANES = 128
AXES = ("s", "yl", "x", "z", "c")
SIZES = (2, 2, 4, 8, 2)
VMEM = pl.BlockSpec(memory_space=pltpu.VMEM)
ANY = pl.BlockSpec(memory_space=pl.ANY)


def toeplitz_kernel(taps_ref, out_ref, rows):
    blocks = out_ref.shape[0] // LANES
    source = lax.broadcasted_iota(jnp.int32, (2 * LANES, 2 * LANES), 0)
    target = lax.broadcasted_iota(jnp.int32, (2 * LANES, 2 * LANES), 1)
    select = source == 2 * (LANES - 1 - target % LANES) + target // LANES

    @pl.when(pl.program_id(0) == 0)
    def _():
        chosen = sum(
            jnp.dot(
                taps_ref[pl.ds(n, taps_ref.shape[0] // 2, stride=2), :],
                select[n * LANES : (n + 1) * LANES].astype(F32),
                precision=lax.Precision.HIGHEST,
                preferred_element_type=F32,
            )
            for n in range(2)
        )
        for parity in range(2):
            rows[parity, 0:8, :] = jnp.zeros((8, LANES), F32)
            rows[parity, 8:, :] = chosen[:, parity * LANES : (parity + 1) * LANES]

    keep = lax.broadcasted_iota(jnp.int32, (LANES, LANES), 1) < LANES - 1 - lax.broadcasted_iota(
        jnp.int32, (LANES, LANES), 0
    )
    first = pl.program_id(0) * blocks

    def body(m, carry):
        row = pl.multiple_of(m * LANES, LANES)
        for parity in range(2):
            before = jnp.broadcast_to(rows[parity, pl.ds(first + m + 7, 1), :], (LANES, LANES))
            here = jnp.broadcast_to(rows[parity, pl.ds(first + m + 8, 1), :], (LANES, LANES))
            tile = pltpu.roll(jnp.where(keep, before, here), 1, 1, stride=1, stride_axis=0)
            high = tile.astype(BF16)
            out_ref[pl.ds(row, LANES), parity * LANES : (parity + 1) * LANES] = high
            out_ref[pl.ds(row, LANES), (2 + parity) * LANES : (3 + parity) * LANES] = (
                tile - high.astype(F32)
            ).astype(BF16)
        return carry

    lax.fori_loop(0, blocks, body, 0, unroll=8)


def toeplitz(filter_taps):
    count = filter_taps.shape[0] // 2
    parts = 4
    return pl.pallas_call(
        toeplitz_kernel,
        grid=(parts,),
        out_shape=jax.ShapeDtypeStruct((count, 4 * LANES), BF16),
        in_specs=[pl.BlockSpec((2 * count // LANES, LANES), lambda i: (0, 0))],
        out_specs=pl.BlockSpec((count // parts, 4 * LANES), lambda i: (i, 0)),
        scratch_shapes=[pltpu.VMEM((2, count // LANES + 8, LANES), F32)],
        compiler_params=pltpu.CompilerParams(vmem_limit_bytes=52 << 20),
        cost_estimate=pl.CostEstimate(
            flops=count * 2048, bytes_accessed=count * 1024, transcendentals=0
        ),
    )(filter_taps.reshape(2 * count // LANES, LANES))


SHIFTS = 16
GROUPS = 8


def filter_kernel(signal_ref, taps_ref, out_ref, held, left, total, table, arrived):
    blocks = signal_ref.shape[0]
    rows = blocks * 8
    steps = blocks // SHIFTS
    per = steps // GROUPS
    depth = SHIFTS * LANES

    def fetch(step):
        part = pl.ds(pl.multiple_of(step * depth, depth), depth)
        return pltpu.make_async_copy(taps_ref.at[part, :], table.at[part, :], arrived.at[step])

    def start(step, carry):
        fetch(step).start()
        return carry

    lax.fori_loop(0, steps, start, 0)

    held[:rows, :] = signal_ref[...].astype(F32).reshape(rows, LANES)
    held[rows:, :] = jnp.zeros((SHIFTS * 8, LANES), F32)

    def fill(i, carry):
        row = pl.multiple_of(i * LANES, LANES)
        for d in range(SHIFTS):
            left[pl.ds(row, LANES), d * LANES : (d + 1) * LANES] = held[
                pl.ds(pl.multiple_of(row + 8 * d, 8), LANES), :
            ].astype(BF16)
        total[pl.ds(row, LANES), :] = jnp.zeros((LANES, 2 * LANES), F32)
        return carry

    lax.fori_loop(0, rows // LANES, fill, 0)
    total[rows:, :] = jnp.zeros((8, 2 * LANES), F32)
    for g in range(GROUPS):
        count = rows - g * per * SHIFTS * 8

        def multiply(j, carry, g=g, count=count):
            step = g * per + j
            fetch(step).wait()
            a = left[pl.ds(pl.multiple_of(step * SHIFTS * 8, SHIFTS * 8), count), :]
            t = table[pl.ds(pl.multiple_of(step * depth, depth), depth), :]
            y = jnp.dot(a, t, preferred_element_type=F32)
            total[0:count, :] += y[:, : 2 * LANES] + y[:, 2 * LANES :]
            return carry

        lax.fori_loop(0, per * (1 + pl.program_id(0)), multiply, 0)

    lane = lax.broadcasted_iota(jnp.int32, (8, LANES), 1)
    sublane = lax.broadcasted_iota(jnp.int32, (8, LANES), 0)
    _, y_count, z_count, c_count, x_count = out_ref.shape[:5]

    def finish(i, carry):
        yx, z = i // z_count, i % z_count
        y, x = yx // x_count, yx % x_count
        for c in range(c_count):
            row = pl.multiple_of((i * c_count + c) * 8, 8)
            same = total[pl.ds(row, 8), :LANES]
            cross = total[pl.ds(row, 8), LANES:]
            after = total[pl.ds(pl.multiple_of(row + 8, 8), 8), LANES:]
            moved = pltpu.roll(jnp.where(lane == 0, after, cross), LANES - 1, 1)
            other = pltpu.roll(jnp.where(sublane < 4, moved, cross), 4, 0)
            out_ref[0, y, z, c, x] = (same + other).astype(BF16)
            out_ref[1, y, z, c, x] = (same - other).astype(BF16)
        return carry

    lax.fori_loop(0, blocks // c_count, finish, 0, unroll=4)


def filtered(signal, taps, sizes):
    s, yl, x, z, c = sizes
    blocks = signal.shape[0]
    depth = SHIFTS * LANES
    return pl.pallas_call(
        filter_kernel,
        grid=(1,),
        out_shape=jax.ShapeDtypeStruct((s, yl, z, c, x, 8, LANES), BF16),
        in_specs=[VMEM, ANY],
        out_specs=VMEM,
        scratch_shapes=[
            pltpu.VMEM(((blocks + SHIFTS) * 8, LANES), F32),
            pltpu.VMEM((blocks * 8, depth), BF16),
            pltpu.VMEM((blocks * 8 + 8, 2 * LANES), F32),
            pltpu.VMEM(taps.shape, BF16),
            pltpu.SemaphoreType.DMA((blocks // SHIFTS,)),
        ],
        compiler_params=pltpu.CompilerParams(vmem_limit_bytes=52 << 20),
        cost_estimate=pl.CostEstimate(
            flops=blocks * 8 * depth * blocks * LANES * 8 // 8,
            bytes_accessed=taps.shape[0] * taps.shape[1] * 2,
            transcendentals=0,
        ),
    )(signal, taps)


def along(array, axis, size, offset):
    return lax.ppermute(array, axis, [(i, (i + offset) % size) for i in range(size)])


TURN_PARTS = 4


def turn_kernel(order_ref, cotangent_ref, out_ref, held, turned, arrived):
    width = held.shape[1]
    part = width // TURN_PARTS
    copies = [
        pltpu.make_async_copy(
            cotangent_ref.at[:, n * part : (n + 1) * part],
            held.at[:, n * part : (n + 1) * part],
            arrived.at[n],
        )
        for n in range(TURN_PARTS)
    ]
    for copy in copies:
        copy.start()
    sign = lax.axis_index("s")
    upper = lax.broadcasted_iota(jnp.int32, (8, LANES), 0) < 4

    def place(i, carry):
        row = pl.multiple_of(i * 8, 8)
        even, odd = turned[pl.ds(row, 8), :LANES], turned[pl.ds(row, 8), LANES:]
        lower_rows = jnp.where(upper, even, pltpu.roll(odd, 4, 0))
        upper_rows = jnp.where(upper, pltpu.roll(even, 4, 0), odd)
        out_ref[i] = jnp.where(sign == 0, lower_rows, upper_rows).astype(BF16)
        return carry

    for n in range(TURN_PARTS):
        copies[n].wait()
        turned[n * part : (n + 1) * part, :] = lax.dot_general(
            held[:, n * part : (n + 1) * part],
            order_ref[...],
            (((0,), (0,)), ((), ())),
            preferred_element_type=F32,
        )
        lax.fori_loop(n * part // 8, (n + 1) * part // 8, place, 0, unroll=8)


def turn(order, cotangent):
    tokens, width = cotangent.shape
    return pl.pallas_call(
        turn_kernel,
        out_shape=jax.ShapeDtypeStruct((width // 8, 8, tokens // 2), BF16),
        in_specs=[VMEM, ANY],
        out_specs=VMEM,
        scratch_shapes=[
            pltpu.VMEM((tokens, width), BF16),
            pltpu.VMEM((width, tokens), F32),
            pltpu.SemaphoreType.DMA((TURN_PARTS,)),
        ],
        compiler_params=pltpu.CompilerParams(vmem_limit_bytes=16 << 20),
    )(order, cotangent)


def pair(first, second, upper):
    first, second = first.astype(F32), second.astype(F32)
    even = jnp.where(upper, first, pltpu.roll(second, 4, 0))
    odd = jnp.where(upper, pltpu.roll(first, 4, 0), second)
    return even.astype(BF16), odd.astype(BF16)


def weight_kernel(spread_ref, *refs):
    *gathered, own_ref, other_ref, left, right, arrived = refs
    x = spread_ref.shape[1]
    half = spread_ref.shape[0] // 2
    tiles = half // 2
    tokens = right.shape[0] // x
    x_here, c_here = lax.axis_index("x"), lax.axis_index("c")
    upper = lax.broadcasted_iota(jnp.int32, (8, LANES), 0) < 4
    copies, row = [], 0
    for n, ref in enumerate(gathered):
        copies.append(
            pltpu.make_async_copy(ref, right.at[row : row + ref.shape[0], :], arrived.at[n])
        )
        row += ref.shape[0]
    for copy in copies:
        copy.start()
    for k in range(x):
        block = lax.rem(x_here - k + x, x)
        for part in range(2):
            core = c_here if part == 0 else 1 - c_here

            def place(i, carry, k=k, block=block, part=part, core=core):
                pairs = [
                    pair(
                        spread_ref[2 * (2 * i + n) + core, block],
                        spread_ref[half + 2 * (2 * i + n) + core, block],
                        upper,
                    )
                    for n in range(2)
                ]
                at = pl.multiple_of(part * tiles * 8 + i * 16, 16)
                for parity in range(2):
                    col = k * tokens + parity * LANES
                    left[pl.ds(at, 16), col : col + LANES] = jnp.concatenate(
                        [pairs[0][parity], pairs[1][parity]], 0
                    )
                return carry

            lax.fori_loop(0, tiles // 2, place, 0, unroll=4)
    for copy in copies:
        copy.wait()
    y = jnp.dot(left[...], right[...], preferred_element_type=F32)
    own_ref[...] = y[: tiles * 8, :]
    other_ref[...] = y[tiles * 8 :, :].astype(BF16)


def weight_part(spread, gathered):
    count, x = spread.shape[:2]
    tokens, width = gathered[0].shape
    rows = count * 4
    return pl.pallas_call(
        weight_kernel,
        out_shape=[
            jax.ShapeDtypeStruct((rows // 2, width), F32),
            jax.ShapeDtypeStruct((rows // 2, width), BF16),
        ],
        in_specs=[VMEM] + [ANY] * len(gathered),
        out_specs=[VMEM, VMEM],
        scratch_shapes=[
            pltpu.VMEM((rows, x * tokens), BF16),
            pltpu.VMEM((x * tokens, width), BF16),
            pltpu.SemaphoreType.DMA((len(gathered),)),
        ],
        compiler_params=pltpu.CompilerParams(vmem_limit_bytes=60 << 20),
        cost_estimate=pl.CostEstimate(
            flops=2 * rows * x * tokens * width,
            bytes_accessed=4 * x * tokens * width,
            transcendentals=0,
        ),
    )(spread, *gathered)


def project_kernel(order_ref, weights_ref, *refs):
    *home, mine_ref, theirs_ref, columns, part, matrix, arrived = refs
    copy = pltpu.make_async_copy(weights_ref, matrix, arrived)
    copy.start()
    x = len(home)
    half = home[0].shape[0] // 2
    width = weights_ref.shape[0]
    yl = width // (LANES * x)
    x_here, sign = lax.axis_index("x"), lax.axis_index("s")
    upper = lax.broadcasted_iota(jnp.int32, (8, LANES), 0) < 4
    per = half // yl
    for k in range(x):
        block = lax.rem(x_here - k + x, x)
        for y in range(yl):

            def place(i, carry, k=k, y=y, block=block):
                q = y * per + 2 * i
                tile_pairs = [
                    pair(home[k][q + n], home[k][half + q + n], upper) for n in range(2)
                ]
                row = pl.multiple_of((y * x + block) * LANES + i * 16, 16)
                for parity in range(2):
                    columns[pl.ds(row, 16), parity * LANES : (parity + 1) * LANES] = (
                        jnp.concatenate([tile_pairs[0][parity], tile_pairs[1][parity]], 0)
                    )
                return carry

            lax.fori_loop(0, per // 2, place, 0, unroll=4)
    copy.wait()
    part[...] = lax.dot_general(
        columns[...], matrix[...], (((0,), (0,)), ((), ())), preferred_element_type=F32
    ).astype(BF16)
    whole = jnp.dot(order_ref[...], part[...], preferred_element_type=F32).astype(BF16)
    side = width // 2

    @pl.when(sign == 0)
    def _():
        mine_ref[...] = whole[:, :side]
        theirs_ref[...] = whole[:, side:]

    @pl.when(sign == 1)
    def _():
        mine_ref[...] = whole[:, side:]
        theirs_ref[...] = whole[:, :side]


def project(order, weights, home):
    tokens, width = order.shape[0], weights.shape[0]
    return pl.pallas_call(
        project_kernel,
        out_shape=[jax.ShapeDtypeStruct((tokens, width // 2), BF16)] * 2,
        in_specs=[VMEM, ANY] + [VMEM] * len(home),
        out_specs=[VMEM, VMEM],
        scratch_shapes=[
            pltpu.VMEM((width, tokens), BF16),
            pltpu.VMEM((tokens, width), BF16),
            pltpu.VMEM((width, width), BF16),
            pltpu.SemaphoreType.DMA,
        ],
        compiler_params=pltpu.CompilerParams(vmem_limit_bytes=24 << 20),
        cost_estimate=pl.CostEstimate(
            flops=2 * tokens * width * width, bytes_accessed=4 * width * width, transcendentals=0
        ),
    )(order, weights, *home)


def body(inputs, cotangent, weights, filter_taps):
    sizes = SIZES
    s, yl, x, z, c = sizes
    tokens, width = inputs.shape
    half = tokens // 2
    groups = yl * x * z * c
    x_here = lax.axis_index("x")
    row = lax.broadcasted_iota(jnp.int32, (tokens, tokens), 0)
    col = lax.broadcasted_iota(jnp.int32, (tokens, tokens), 1)
    order = (row == 2 * (col % half) + col // half).astype(BF16)

    send = turn(order, cotangent)
    signal = lax.all_to_all(send, ("yl", "x", "z", "c"), split_axis=0, concat_axis=0, tiled=True)

    taps = toeplitz(filter_taps)
    taps, inputs = lax.optimization_barrier((taps, inputs))
    sorted_inputs = lax.dot_general(
        order, inputs, (((0,), (0,)), ((), ())), preferred_element_type=F32
    ).astype(BF16)
    before, after = along(sorted_inputs, "x", x, 1), along(sorted_inputs, "x", x, x - 1)

    result = filtered(signal, taps, sizes).reshape(s * yl * z * c, x, 8, half)
    result, before, after = lax.optimization_barrier((result, before, after))
    gathered = [
        sorted_inputs,
        before,
        along(before[:half], "x", x, 1),
        along(after[half:], "x", x, x - 1),
        after,
    ]
    spread = lax.all_to_all(result, ("s", "yl", "z", "c"), split_axis=0, concat_axis=0, tiled=True)
    home = [
        lax.dynamic_index_in_dim(spread, lax.rem(x_here + k, x), 1, keepdims=False)
        for k in range(x)
    ]

    spread, *home = lax.optimization_barrier((spread, *home))
    home = [home[0]] + [along(home[k], "x", x, k) for k in range(1, x)]
    own, other = weight_part(spread, gathered)
    other, *home = lax.optimization_barrier((other, *home))
    other = along(other, "c", c, 1)
    mine, theirs = project(order, weights[0], home)
    reduced = (own + other.astype(F32)).astype(BF16).reshape(yl * z, 8, width)
    theirs, reduced = lax.optimization_barrier((theirs, reduced))
    arrived = along(theirs, "s", s, 1)
    pieces = lax.all_to_all(reduced, ("yl", "z"), split_axis=0, concat_axis=0, tiled=True)
    grad_scale = 1.0 / math.sqrt(tokens * groups)
    weight_grad = jnp.sum(pieces.astype(F32), 0) * grad_scale
    input_grad = (mine.astype(F32) + arrived.astype(F32)).astype(BF16)
    return input_grad, weight_grad[None]


def solution(mesh):
    fine = Mesh(mesh.devices.reshape(SIZES), AXES)
    context = ("yl", "x", "z", "c")
    in_specs = (P(context, None), P(context, None), P("s", None, None), P())
    out_specs = (P(context, "s"), P("s", context, None))
    return jax.shard_map(body, mesh=fine, in_specs=in_specs, out_specs=out_specs, check_vma=False)
```

time: 131 us -> 107 us (0.82)
  local copies, waits for them, and re-layouts: 22.9 us -> 6.93 us
  matrix products: 9.72 us -> 1.18 us
  Pallas kernels: 25.9 us -> 31 us
  waiting for transfers between devices: 24 us -> 20.2 us
  starting transfers between devices: 41.2 us -> 42.8 us
  other arithmetic: 4.76 us -> 3.29 us
    dot_general x8 -> x0, matrix products: 9.37 us -> none  [the longest x4 5.39 us: body(): jnp.einsum('qpka,pae->qke', block.reshape(s * yl * z * c, 2, 4, half), ga...]
    reshape x5 -> x0, local copies, waits for them, and re-layouts: 7.98 us -> none  [the longest x2 4.37 us: body(): partial = partial.reshape(s, yl, z, c, 4, width).transpose(3, 1, 2, 0, 4, 5)]
    all_to_all x1, waiting for transfers between devices: 17.3 us -> 11.3 us  [body(): lax.all_to_all(result, ('s', 'yl', 'z', 'c'), split_axis=0, concat_axis=0...]
    pallas_call x2 -> x5, Pallas kernels: 25.9 us -> 31 us  [the longest x1 14.9 us: filtered(): pl.pallas_call(filter_kernel, grid=(1,), out_shape=jax.ShapeDtypeStruct((...]
    unnamed x20 -> x12, local copies, waits for them, and re-layouts: 6.86 us -> 2.69 us
    another operation x3 -> x0, local copies, waits for them, and re-layouts: 4.01 us -> none  [the longest x1 2.74 us: body(): split = weights[0].reshape(yl, x, z, c, s, 4, width)]
    slice x0 -> x2, local copies, waits for them, and re-layouts: none -> 3.34 us  [the longest x1 1.67 us: body(): before[:half]]
    transpose x1 -> x0, other arithmetic: 2.92 us -> none  [body(): rows = rows.transpose(0, 4, 1, 2, 3, 5, 6).reshape(width, width)]
  transfers between devices with their start and end apart: 11 -> 12, of which waited for: 3 -> 5; matrix products, arithmetic and copies ran while one was open for 23% -> 6% of each run, Pallas kernels for 8% -> 27%
where the time goes in v2:
time: 107 us; the launch traced here: 106 us
  starting transfers between devices  42.8 us (40%)
  Pallas kernels  31 us (29%)
  waiting for transfers between devices  20.2 us (19%)
  local copies, waits for them, and re-layouts  6.93 us (6%)
  other arithmetic  3.29 us (3%)
  matrix products  1.18 us (1%)
    pallas_call x1, Pallas kernels, filtered(): pl.pallas_call(filter_kernel, grid=(1,), out_shape=jax.ShapeDtypeStruct((...  14.9 us
    all_to_all x1, starting transfers between devices, body(): lax.all_to_all(send, ('yl', 'x', 'z', 'c'), split_axis=0, concat_axis=0,...  14.8 us
    ppermute x9, starting transfers between devices, along(): lax.ppermute(array, axis, [(i, (i + offset) % size) for i in range(size)])  13.6 us
    all_to_all x1, waiting for transfers between devices, body(): lax.all_to_all(result, ('s', 'yl', 'z', 'c'), split_axis=0, concat_axis=0...  11.3 us
    all_to_all x1, starting transfers between devices, body(): lax.all_to_all(result, ('s', 'yl', 'z', 'c'), split_axis=0, concat_axis=0...  10.9 us
    pallas_call x1, Pallas kernels, toeplitz(): pl.pallas_call(toeplitz_kernel, grid=(parts,), out_shape=jax.ShapeDtypeSt...  8.55 us
    all_to_all x1, waiting for transfers between devices, body(): lax.all_to_all(reduced, ('yl', 'z'), split_axis=0, concat_axis=0, tiled=T...  5.51 us
    pallas_call x1, Pallas kernels, weight_part(): pl.pallas_call(weight_kernel, out_shape=[jax.ShapeDtypeStruct((rows // 2,...  4.18 us
  transfers between devices with their start and end apart: 12, of which 5 were waited for; matrix products, arithmetic and copies ran while one was open for 6% of the time, Pallas kernels for 27%

profile of v2, /device:TPU:1, one launch (start us, length us, event | category | flops | bytes accessed | tf_op | source)
XLA Modules:
  0.0 106.1 jit_solution(6056545132978829011)
XLA Ops:
  0.6 0.0 copy-start
  0.7 0.0 copy-start.2
  0.7 1.1 %copy-done.2 = bf16[256,1024]{1,0:T(8,128)(2,1)S(1)} copy-done((bf16[256,1024]{1,0:T(8,128)(2,1)S(1)}, bf16[256,1024]{1,0:T(8,128)(2,1)}, u32[]{:S(2)}) %copy-start.2) | copy-done | bytes 524312
  1.8 2.0 %shard_map.59 = bf16[128,8,128]{2,1,0:T(8,128)(2,1)} custom-call(bf16[256,256]{1,0:T(8,128)(2,1)S(1)} %fusion.3.order_ref, bf16[256,1024]{1,0:T(8,128)(2,1)S(1)} %copy-done.2), custom_call_target="tpu_custom_call" | custom-call | tf_op jit(solution)/shard_map/pallas_call | solution.py:217
  3.8 14.8 %all-to-all-start = ((bf16[128,8,128]{2,1,0:T(8,128)(2,1)}), bf16[128,8,128]{2,1,0:T(8,128)(2,1)S(1)}, u32[]{:S(2)}, u32[]{:S(2)}) async-start(bf16[128,8,128]{2,1,0:T(8,128)(2,1)} %shard_map.59), calls=%async_computation | async-start | bytes 524288 | tf_op jit(solution)/shard_map/all_to_all | solution.py:388
  18.6 0.0 copy-start.3
  18.6 0.9 copy-done.3
  19.5 8.5 %shard_map.60.taps_ref = bf16[16384,512]{1,0:T(8,128)(2,1)} custom-call(f32[256,128]{1,0:T(8,128)S(1)} %bitcast.17), custom_call_target="tpu_custom_call" | custom-call | flops 33554432 | bytes 16777216 | tf_op jit(solution)/shard_map/pallas_call | solution.py:63
  28.1 0.0 copy-done
  28.1 1.2 %convolution_convert_fusion.refs_0_ = bf16[256,1024]{1,0:T(8,128)(2,1)} fusion(bf16[256,1024]{1,0:T(8,128)(2,1)S(1)} %copy-done, s32[256]{0:T(256)S(1)} %get-tuple-element.50, s32[256]{0:T(256)S(1)} %get-tuple-element.53, s32[256]{0:T(256)S(1)} %get-tuple-element.51, s32[256]{0:T(256)S(1)} %get-tuple-element.52, pred[256]{0:T(512)(128)(4,1)S(1)} %get-tuple-element.48, ...), kind=kOutput, calls=%fused_computation | convolution fusion | flops 134807552 | bytes 1053184 | tf_op jit(solution)/shard_map/dot_general | solution.py:392
  29.2 0.0 copy-start.1
  29.2 1.4 %collective-permute-start = (bf16[256,1024]{1,0:T(8,128)(2,1)}, bf16[256,1024]{1,0:T(8,128)(2,1)}, u32[]{:S(2)}, u32[]{:S(2)}) collective-permute-start(bf16[256,1024]{1,0:T(8,128)(2,1)} %convolution_convert_fusion.refs_0_), channel_id=1, source_target_pairs={{0,16},{16,32},{32,48},{48,0},{1,17},{17,33},{33,49},{49,1},{2,18}... | collective-permute-start | bytes 1572872 | tf_op jit(solution)/shard_map/ppermute | solution.py:174
  30.6 1.4 %collective-permute-start.1 = (bf16[256,1024]{1,0:T(8,128)(2,1)}, bf16[256,1024]{1,0:T(8,128)(2,1)}, u32[]{:S(2)}, u32[]{:S(2)}) collective-permute-start(bf16[256,1024]{1,0:T(8,128)(2,1)} %convolution_convert_fusion.refs_0_), channel_id=1, source_target_pairs={{0,48},{16,0},{32,16},{48,32},{1,49},{17,1},{33,17},{49,33},{2,50}... | collective-permute-start | bytes 1572872 | tf_op jit(solution)/shard_map/ppermute | solution.py:174
  32.0 0.0 all-to-all-done.signal_ref
  32.1 14.9 %shard_map.61 = bf16[2,2,8,2,4,8,128]{6,5,4,3,2,1,0:T(8,128)(2,1)} custom-call(bf16[128,8,128]{2,1,0:T(8,128)(2,1)S(1)} %all-to-all-done.signal_ref, bf16[16384,512]{1,0:T(8,128)(2,1)} %shard_map.60.taps_ref), custom_call_target="tpu_custom_call" | custom-call | flops 34359738368 | bytes 16777216 | tf_op jit(solution)/shard_map/pallas_call | solution.py:151
  47.0 0.0 collective-permute-done.refs_1_
  47.0 0.0 collective-permute-done.1.refs_4_
  47.0 10.9 %all-to-all-start.1 = ((bf16[64,4,8,128]{3,2,1,0:T(8,128)(2,1)}), bf16[64,4,8,128]{3,2,1,0:T(8,128)(2,1)S(1)}, u32[]{:S(2)}, u32[]{:S(2)}) async-start(bf16[64,4,8,128]{3,2,1,0:T(8,128)(2,1)} %bitcast.2), calls=%async_computation.1 | async-start | bytes 1048576 | tf_op jit(solution)/shard_map/all_to_all | solution.py:406
  57.9 1.7 %slice.6 = bf16[128,1024]{1,0:T(8,128)(2,1)} slice(bf16[256,1024]{1,0:T(8,128)(2,1)} %collective-permute-done.refs_1_), slice={[0:128], [0:1024]} | slice | bytes 524288 | tf_op jit(solution)/shard_map/slice | solution.py:402
  59.5 0.1 collective-permute-start.2
  59.6 1.7 %slice.7 = bf16[128,1024]{1,0:T(8,128)(2,1)} slice(bf16[256,1024]{1,0:T(8,128)(2,1)} %collective-permute-done.1.refs_4_), slice={[128:256], [0:1024]} | slice | bytes 524288 | tf_op jit(solution)/shard_map/slice | solution.py:403
  61.3 2.6 %collective-permute-start.3 = (bf16[128,1024]{1,0:T(8,128)(2,1)}, bf16[128,1024]{1,0:T(8,128)(2,1)}, u32[]{:S(2)}, u32[]{:S(2)}) collective-permute-start(bf16[128,1024]{1,0:T(8,128)(2,1)} %slice.7), channel_id=1, source_target_pairs={{0,48},{16,0},{32,16},{48,32},{1,49},{17,1},{33,17},{49,33},{2,50}... | collective-permute-start | bytes 786440 | tf_op jit(solution)/shard_map/ppermute | solution.py:174
  63.9 11.3 %all-to-all-done.1.spread_ref = bf16[64,4,8,128]{3,2,1,0:T(8,128)(2,1)S(1)} async-done(((bf16[64,4,8,128]{3,2,1,0:T(8,128)(2,1)}), bf16[64,4,8,128]{3,2,1,0:T(8,128)(2,1)S(1)}, u32[]{:S(2)}, u32[]{:S(2)}) %all-to-all-start.1) | async-done | bytes 524320 | tf_op jit(solution)/shard_map/all_to_all | solution.py:406
  75.2 0.0 copy-start.4
  75.2 0.9 dynamic-slice_bitcast_fusion
  76.1 0.1 collective-permute-start.4
  76.2 2.6 %collective-permute-start.5 = (bf16[64,8,128]{2,1,0:T(8,128)(2,1)}, bf16[64,8,128]{2,1,0:T(8,128)(2,1)S(1)}, u32[]{:S(2)}, u32[]{:S(2)}) collective-permute-start(bf16[64,8,128]{2,1,0:T(8,128)(2,1)} %get-tuple-element.32), channel_id=1, source_target_pairs={{0,32},{16,48},{32,0},{48,16},{1,33},{17,49},{33,1},{49,17},{2,34}... | collective-permute-start | bytes 393224 | tf_op jit(solution)/shard_map/ppermute | solution.py:174
  78.8 1.1 %collective-permute-start.6 = (bf16[64,8,128]{2,1,0:T(8,128)(2,1)}, bf16[64,8,128]{2,1,0:T(8,128)(2,1)S(1)}, u32[]{:S(2)}, u32[]{:S(2)}) collective-permute-start(bf16[64,8,128]{2,1,0:T(8,128)(2,1)} %get-tuple-element.33), channel_id=1, source_target_pairs={{0,48},{16,0},{32,16},{48,32},{1,49},{17,1},{33,17},{49,33},{2,50}... | collective-permute-start | bytes 393224 | tf_op jit(solution)/shard_map/ppermute | solution.py:174
  79.9 0.0 collective-permute-done.2.refs_2_
  79.9 0.0 copy-start.5
  79.9 0.0 collective-permute-done.3.refs_3_
  79.9 0.0 copy-done.4
  79.9 0.7 copy-done.5
  80.6 4.2 %shard_map.62 = (f32[128,1024]{1,0:T(8,128)}, bf16[128,1024]{1,0:T(8,128)(2,1)}) custom-call(bf16[64,4,8,128]{3,2,1,0:T(8,128)(2,1)} %copy-done.4, bf16[256,1024]{1,0:T(8,128)(2,1)} %convolution_convert_fusion.refs_0_, bf16[256,1024]{1,0:T(8,128)(2,1)} %collective-permute-done.refs_1_, bf16[128,1024]{1,0:T(8,128)(2,1)} %copy-done.5, ...), custom_call_target="tpu_custom_call" | custom-call | flops 536870912 | bytes 4194304 | tf_op jit(solution)/shard_map/pallas_call | solution.py:288
  84.7 0.0 collective-permute-done.4.refs_1_
  84.8 0.3 collective-permute-done.5.refs_2_
  85.1 0.2 collective-permute-done.6.refs_3_
  85.3 1.5 %collective-permute-start.7 = (bf16[128,1024]{1,0:T(8,128)(2,1)}, bf16[128,1024]{1,0:T(8,128)(2,1)S(1)}, u32[]{:S(2)}, u32[]{:S(2)}) collective-permute-start(bf16[128,1024]{1,0:T(8,128)(2,1)} %get-tuple-element.41), channel_id=1, source_target_pairs={{0,1},{1,0},{2,3},{3,2},{4,5},{5,4},{6,7},{7,6},{8,9},{9,8},{10,11... | collective-permute-start | bytes 786440 | tf_op jit(solution)/shard_map/ppermute | solution.py:174
  86.8 0.0 copy-done.1
  86.8 1.4 %shard_map.63 = (bf16[256,512]{1,0:T(8,128)(2,1)S(1)}, bf16[256,512]{1,0:T(8,128)(2,1)S(1)}) custom-call(bf16[256,256]{1,0:T(8,128)(2,1)S(1)} %fusion.3.order_ref, bf16[1024,1024]{1,0:T(8,128)(2,1)S(1)} %bitcast.16, bf16[64,8,128]{2,1,0:T(8,128)(2,1)S(1)} %get-tuple-element.34.refs_0_, bf16[64,8,128]{2,1,0:T(8,128)(2,1)S(1)} %collective-permute-done.4.refs_1_, ...), custom_call_target="tpu_custom_call" | custom-call | flops 536870912 | bytes 4194304 | tf_op jit(solution)/shard_map/pallas_call | solution.py:358
  88.2 0.0 collective-permute-done.7
  88.2 1.8 %fusion = bf16[16,8,1024]{2,1,0:T(8,128)(2,1)} fusion(f32[128,1024]{1,0:T(8,128)} %get-tuple-element.40, bf16[128,1024]{1,0:T(8,128)(2,1)S(1)} %collective-permute-done.7), kind=kLoop, calls=%fused_computation.4 | loop fusion | flops 393216 | bytes 1048576 | tf_op jit(solution)/shard_map/reshape | solution.py:418
  90.1 2.9 %collective-permute-start.8 = (bf16[256,512]{1,0:T(8,128)(2,1)S(1)}, bf16[256,512]{1,0:T(8,128)(2,1)S(1)}, u32[]{:S(2)}, u32[]{:S(2)}) collective-permute-start(bf16[256,512]{1,0:T(8,128)(2,1)S(1)} %get-tuple-element.42), channel_id=1, source_target_pairs={{0,128},{128,0},{1,129},{129,1},{2,130},{130,2},{3,131},{131,3},{4... | collective-permute-start | bytes 786440 | tf_op jit(solution)/shard_map/ppermute | solution.py:174
  92.9 3.5 %all-to-all-start.2 = ((bf16[16,8,1024]{2,1,0:T(8,128)(2,1)}), bf16[16,8,1024]{2,1,0:T(8,128)(2,1)S(1)}, u32[]{:S(2)}, u32[]{:S(2)}) async-start(bf16[16,8,1024]{2,1,0:T(8,128)(2,1)} %fusion), calls=%async_computation.2 | async-start | bytes 524288 | tf_op jit(solution)/shard_map/all_to_all | solution.py:421
  96.5 2.7 %collective-permute-done.8 = bf16[256,512]{1,0:T(8,128)(2,1)S(1)} collective-permute-done((bf16[256,512]{1,0:T(8,128)(2,1)S(1)}, bf16[256,512]{1,0:T(8,128)(2,1)S(1)}, u32[]{:S(2)}, u32[]{:S(2)}) %collective-permute-start.8) | collective-permute-done | bytes 262176 | tf_op jit(solution)/shard_map/ppermute | solution.py:174
  99.2 0.8 add_convert_fusion
  99.9 5.5 %all-to-all-done.2 = bf16[16,8,1024]{2,1,0:T(8,128)(2,1)S(1)} async-done(((bf16[16,8,1024]{2,1,0:T(8,128)(2,1)}), bf16[16,8,1024]{2,1,0:T(8,128)(2,1)S(1)}, u32[]{:S(2)}, u32[]{:S(2)}) %all-to-all-start.2) | async-done | bytes 262176 | tf_op jit(solution)/shard_map/all_to_all | solution.py:421
  105.5 0.6 multiply_bitcast_fusion
  (5 shorter events, 0.1 us)
Async XLA Ops:
  0.6 27.4 %copy-start = (bf16[256,1024]{1,0:T(8,128)(2,1)S(1)}, bf16[256,1024]{1,0:T(8,128)(2,1)}, u32[]{:S(2)}) copy-start(bf16[256,1024]{1,0:T(8,128)(2,1)} %param.4) | copy-start | bytes 1572868
  0.7 1.1 %copy-start.2 = (bf16[256,1024]{1,0:T(8,128)(2,1)S(1)}, bf16[256,1024]{1,0:T(8,128)(2,1)}, u32[]{:S(2)}) copy-start(bf16[256,1024]{1,0:T(8,128)(2,1)} %cotangent_ref.1) | copy-start | bytes 1572868
  3.8 28.3 %all-to-all-start = ((bf16[128,8,128]{2,1,0:T(8,128)(2,1)}), bf16[128,8,128]{2,1,0:T(8,128)(2,1)S(1)}, u32[]{:S(2)}, u32[]{:S(2)}) async-start(bf16[128,8,128]{2,1,0:T(8,128)(2,1)} %shard_map.59), calls=%async_computation | async-start | bytes 524288 | tf_op jit(solution)/shard_map/all_to_all | solution.py:388
  18.6 0.9 copy-start.3
  29.2 57.6 %copy-start.1 = (bf16[1,1024,1024]{2,1,0:T(8,128)(2,1)S(1)}, bf16[1,1024,1024]{2,1,0:T(8,128)(2,1)}, u32[]{:S(2)}) copy-start(bf16[1,1024,1024]{2,1,0:T(8,128)(2,1)} %param.6) | copy-start | bytes 6291460
  29.2 17.7 %collective-permute-start = (bf16[256,1024]{1,0:T(8,128)(2,1)}, bf16[256,1024]{1,0:T(8,128)(2,1)}, u32[]{:S(2)}, u32[]{:S(2)}) collective-permute-start(bf16[256,1024]{1,0:T(8,128)(2,1)} %convolution_convert_fusion.refs_0_), channel_id=1, source_target_pairs={{0,16},{16,32},{32,48},{48,0},{1,17},{17,33},{33,49},{49,1},{2,18}... | collective-permute-start | bytes 1572872 | tf_op jit(solution)/shard_map/ppermute | solution.py:174
  30.6 16.3 %collective-permute-start.1 = (bf16[256,1024]{1,0:T(8,128)(2,1)}, bf16[256,1024]{1,0:T(8,128)(2,1)}, u32[]{:S(2)}, u32[]{:S(2)}) collective-permute-start(bf16[256,1024]{1,0:T(8,128)(2,1)} %convolution_convert_fusion.refs_0_), channel_id=1, source_target_pairs={{0,48},{16,0},{32,16},{48,32},{1,49},{17,1},{33,17},{49,33},{2,50}... | collective-permute-start | bytes 1572872 | tf_op jit(solution)/shard_map/ppermute | solution.py:174
  47.0 28.2 %all-to-all-start.1 = ((bf16[64,4,8,128]{3,2,1,0:T(8,128)(2,1)}), bf16[64,4,8,128]{3,2,1,0:T(8,128)(2,1)S(1)}, u32[]{:S(2)}, u32[]{:S(2)}) async-start(bf16[64,4,8,128]{3,2,1,0:T(8,128)(2,1)} %bitcast.2), calls=%async_computation.1 | async-start | bytes 1048576 | tf_op jit(solution)/shard_map/all_to_all | solution.py:406
  59.5 20.3 %collective-permute-start.2 = (bf16[128,1024]{1,0:T(8,128)(2,1)}, bf16[128,1024]{1,0:T(8,128)(2,1)S(1)}, u32[]{:S(2)}, u32[]{:S(2)}) collective-permute-start(bf16[128,1024]{1,0:T(8,128)(2,1)} %slice.6), channel_id=1, source_target_pairs={{0,16},{16,32},{32,48},{48,0},{1,17},{17,33},{33,49},{49,1},{2,18}... | collective-permute-start | bytes 786440 | tf_op jit(solution)/shard_map/ppermute | solution.py:174
  61.3 18.6 %collective-permute-start.3 = (bf16[128,1024]{1,0:T(8,128)(2,1)}, bf16[128,1024]{1,0:T(8,128)(2,1)}, u32[]{:S(2)}, u32[]{:S(2)}) collective-permute-start(bf16[128,1024]{1,0:T(8,128)(2,1)} %slice.7), channel_id=1, source_target_pairs={{0,48},{16,0},{32,16},{48,32},{1,49},{17,1},{33,17},{49,33},{2,50}... | collective-permute-start | bytes 786440 | tf_op jit(solution)/shard_map/ppermute | solution.py:174
  75.2 4.7 %copy-start.4 = (bf16[64,4,8,128]{3,2,1,0:T(8,128)(2,1)}, bf16[64,4,8,128]{3,2,1,0:T(8,128)(2,1)S(1)}, u32[]{:S(2)}) copy-start(bf16[64,4,8,128]{3,2,1,0:T(8,128)(2,1)S(1)} %all-to-all-done.1.spread_ref) | copy-start | bytes 1572868
  76.1 8.7 %collective-permute-start.4 = (bf16[64,8,128]{2,1,0:T(8,128)(2,1)}, bf16[64,8,128]{2,1,0:T(8,128)(2,1)S(1)}, u32[]{:S(2)}, u32[]{:S(2)}) collective-permute-start(bf16[64,8,128]{2,1,0:T(8,128)(2,1)} %get-tuple-element.31), channel_id=1, source_target_pairs={{0,16},{16,32},{32,48},{48,0},{1,17},{17,33},{33,49},{49,1},{2,18}... | collective-permute-start | bytes 393224 | tf_op jit(solution)/shard_map/ppermute | solution.py:174
  76.2 8.9 %collective-permute-start.5 = (bf16[64,8,128]{2,1,0:T(8,128)(2,1)}, bf16[64,8,128]{2,1,0:T(8,128)(2,1)S(1)}, u32[]{:S(2)}, u32[]{:S(2)}) collective-permute-start(bf16[64,8,128]{2,1,0:T(8,128)(2,1)} %get-tuple-element.32), channel_id=1, source_target_pairs={{0,32},{16,48},{32,0},{48,16},{1,33},{17,49},{33,1},{49,17},{2,34}... | collective-permute-start | bytes 393224 | tf_op jit(solution)/shard_map/ppermute | solution.py:174
  78.8 6.6 %collective-permute-start.6 = (bf16[64,8,128]{2,1,0:T(8,128)(2,1)}, bf16[64,8,128]{2,1,0:T(8,128)(2,1)S(1)}, u32[]{:S(2)}, u32[]{:S(2)}) collective-permute-start(bf16[64,8,128]{2,1,0:T(8,128)(2,1)} %get-tuple-element.33), channel_id=1, source_target_pairs={{0,48},{16,0},{32,16},{48,32},{1,49},{17,1},{33,17},{49,33},{2,50}... | collective-permute-start | bytes 393224 | tf_op jit(solution)/shard_map/ppermute | solution.py:174
  79.9 0.7 copy-start.5
  85.3 2.9 %collective-permute-start.7 = (bf16[128,1024]{1,0:T(8,128)(2,1)}, bf16[128,1024]{1,0:T(8,128)(2,1)S(1)}, u32[]{:S(2)}, u32[]{:S(2)}) collective-permute-start(bf16[128,1024]{1,0:T(8,128)(2,1)} %get-tuple-element.41), channel_id=1, source_target_pairs={{0,1},{1,0},{2,3},{3,2},{4,5},{5,4},{6,7},{7,6},{8,9},{9,8},{10,11... | collective-permute-start | bytes 786440 | tf_op jit(solution)/shard_map/ppermute | solution.py:174
  90.1 9.1 %collective-permute-start.8 = (bf16[256,512]{1,0:T(8,128)(2,1)S(1)}, bf16[256,512]{1,0:T(8,128)(2,1)S(1)}, u32[]{:S(2)}, u32[]{:S(2)}) collective-permute-start(bf16[256,512]{1,0:T(8,128)(2,1)S(1)} %get-tuple-element.42), channel_id=1, source_target_pairs={{0,128},{128,0},{1,129},{129,1},{2,130},{130,2},{3,131},{131,3},{4... | collective-permute-start | bytes 786440 | tf_op jit(solution)/shard_map/ppermute | solution.py:174
  92.9 12.5 %all-to-all-start.2 = ((bf16[16,8,1024]{2,1,0:T(8,128)(2,1)}), bf16[16,8,1024]{2,1,0:T(8,128)(2,1)S(1)}, u32[]{:S(2)}, u32[]{:S(2)}) async-start(bf16[16,8,1024]{2,1,0:T(8,128)(2,1)} %fusion), calls=%async_computation.2 | async-start | bytes 524288 | tf_op jit(solution)/shard_map/all_to_all | solution.py:421

commit v3 on v2

--- a/solution.py
+++ b/solution.py
@@ -174,22 +174,10 @@
     return lax.ppermute(array, axis, [(i, (i + offset) % size) for i in range(size)])
 
 
-TURN_PARTS = 4
-
-
-def turn_kernel(order_ref, cotangent_ref, out_ref, held, turned, arrived):
-    width = held.shape[1]
-    part = width // TURN_PARTS
-    copies = [
-        pltpu.make_async_copy(
-            cotangent_ref.at[:, n * part : (n + 1) * part],
-            held.at[:, n * part : (n + 1) * part],
-            arrived.at[n],
-        )
-        for n in range(TURN_PARTS)
-    ]
-    for copy in copies:
-        copy.start()
+def turn_kernel(order_ref, cotangent_ref, out_ref, turned):
+    turned[...] = lax.dot_general(
+        cotangent_ref[...], order_ref[...], (((0,), (0,)), ((), ())), preferred_element_type=F32
+    )
     sign = lax.axis_index("s")
     upper = lax.broadcasted_iota(jnp.int32, (8, LANES), 0) < 4
 
@@ -201,15 +189,7 @@
         out_ref[i] = jnp.where(sign == 0, lower_rows, upper_rows).astype(BF16)
         return carry
 
-    for n in range(TURN_PARTS):
-        copies[n].wait()
-        turned[n * part : (n + 1) * part, :] = lax.dot_general(
-            held[:, n * part : (n + 1) * part],
-            order_ref[...],
-            (((0,), (0,)), ((), ())),
-            preferred_element_type=F32,
-        )
-        lax.fori_loop(n * part // 8, (n + 1) * part // 8, place, 0, unroll=8)
+    lax.fori_loop(0, out_ref.shape[0], place, 0, unroll=8)
 
 
 def turn(order, cotangent):
@@ -217,13 +197,9 @@
     return pl.pallas_call(
         turn_kernel,
         out_shape=jax.ShapeDtypeStruct((width // 8, 8, tokens // 2), BF16),
-        in_specs=[VMEM, ANY],
+        in_specs=[VMEM, VMEM],
         out_specs=VMEM,
-        scratch_shapes=[
-            pltpu.VMEM((tokens, width), BF16),
-            pltpu.VMEM((width, tokens), F32),
-            pltpu.SemaphoreType.DMA((TURN_PARTS,)),
-        ],
+        scratch_shapes=[pltpu.VMEM((width, tokens), F32)],
         compiler_params=pltpu.CompilerParams(vmem_limit_bytes=16 << 20),
     )(order, cotangent)
 
@@ -235,76 +211,81 @@
     return even.astype(BF16), odd.astype(BF16)
 
 
-def weight_kernel(spread_ref, *refs):
-    *gathered, own_ref, other_ref, left, right, arrived = refs
-    x = spread_ref.shape[1]
-    half = spread_ref.shape[0] // 2
+def weight_kernel(order_ref, spread_ref, *refs):
+    *gathered, own_ref, other_ref, blocks, left, turned, right, sent, arrived = refs
+    x = blocks.shape[0]
+    half = blocks.shape[1] // 2
     tiles = half // 2
     tokens = right.shape[0] // x
     x_here, c_here = lax.axis_index("x"), lax.axis_index("c")
     upper = lax.broadcasted_iota(jnp.int32, (8, LANES), 0) < 4
-    copies, row = [], 0
+    fetches, copies, row = [], [], 0
+    for k in range(x):
+        block = lax.rem(x_here - k + x, x)
+        fetches.append(pltpu.make_async_copy(spread_ref.at[:, block], blocks.at[k], sent.at[k]))
+        fetches[k].start()
     for n, ref in enumerate(gathered):
         copies.append(
             pltpu.make_async_copy(ref, right.at[row : row + ref.shape[0], :], arrived.at[n])
         )
         row += ref.shape[0]
-    for copy in copies:
-        copy.start()
+        copies[n].start()
     for k in range(x):
-        block = lax.rem(x_here - k + x, x)
+        fetches[k].wait()
         for part in range(2):
             core = c_here if part == 0 else 1 - c_here
 
-            def place(i, carry, k=k, block=block, part=part, core=core):
+            def place(i, carry, k=k, part=part, core=core):
                 pairs = [
                     pair(
-                        spread_ref[2 * (2 * i + n) + core, block],
-                        spread_ref[half + 2 * (2 * i + n) + core, block],
+                        blocks[k, 2 * (2 * i + n) + core],
+                        blocks[k, half + 2 * (2 * i + n) + core],
                         upper,
                     )
                     for n in range(2)
                 ]
                 at = pl.multiple_of(part * tiles * 8 + i * 16, 16)
                 for parity in range(2):
-                    col = k * tokens + parity * LANES
-                    left[pl.ds(at, 16), col : col + LANES] = jnp.concatenate(
-                        [pairs[0][parity], pairs[1][parity]], 0
+                    left[pl.ds(at, 16), parity * LANES : (parity + 1) * LANES] = (
+                        jnp.concatenate([pairs[0][parity], pairs[1][parity]], 0)
                     )
                 return carry
 
             lax.fori_loop(0, tiles // 2, place, 0, unroll=4)
+        turned[:, k * tokens : (k + 1) * tokens] = lax.dot_general(
+            left[...], order_ref[...], (((1,), (1,)), ((), ())), preferred_element_type=F32
+        ).astype(BF16)
     for copy in copies:
         copy.wait()
-    y = jnp.dot(left[...], right[...], preferred_element_type=F32)
+    y = jnp.dot(turned[...], right[...], preferred_element_type=F32).astype(BF16)
     own_ref[...] = y[: tiles * 8, :]
-    other_ref[...] = y[tiles * 8 :, :].astype(BF16)
-
-
-def weight_part(spread, gathered):
+    other_ref[...] = y[tiles * 8 :, :]
+
+
+def weight_part(order, spread, gathered):
     count, x = spread.shape[:2]
     tokens, width = gathered[0].shape
     rows = count * 4
     return pl.pallas_call(
         weight_kernel,
-        out_shape=[
-            jax.ShapeDtypeStruct((rows // 2, width), F32),
-            jax.ShapeDtypeStruct((rows // 2, width), BF16),
-        ],
-        in_specs=[VMEM] + [ANY] * len(gathered),
+        out_shape=[jax.ShapeDtypeStruct((rows // 2, width), BF16)] * 2,
+        in_specs=[VMEM] + [ANY] * (1 + len(gathered)),
         out_specs=[VMEM, VMEM],
         scratch_shapes=[
+            pltpu.VMEM((x, count, 8, LANES), BF16),
+            pltpu.VMEM((rows, tokens), BF16),
             pltpu.VMEM((rows, x * tokens), BF16),
             pltpu.VMEM((x * tokens, width), BF16),
+            pltpu.SemaphoreType.DMA((x,)),
             pltpu.SemaphoreType.DMA((len(gathered),)),
         ],
-        compiler_params=pltpu.CompilerParams(vmem_limit_bytes=60 << 20),
+        compiler_params=pltpu.CompilerParams(vmem_limit_bytes=24 << 20),
         cost_estimate=pl.CostEstimate(
             flops=2 * rows * x * tokens * width,
             bytes_accessed=4 * x * tokens * width,
             transcendentals=0,
         ),
-    )(spread, *gathered)
+    )(order, spread, *gathered)
 
 
 def project_kernel(order_ref, weights_ref, *refs):
@@ -389,15 +370,12 @@
 
     taps = toeplitz(filter_taps)
     taps, inputs = lax.optimization_barrier((taps, inputs))
-    sorted_inputs = lax.dot_general(
-        order, inputs, (((0,), (0,)), ((), ())), preferred_element_type=F32
-    ).astype(BF16)
-    before, after = along(sorted_inputs, "x", x, 1), along(sorted_inputs, "x", x, x - 1)
+    before, after = along(inputs, "x", x, 1), along(inputs, "x", x, x - 1)
 
     result = filtered(signal, taps, sizes).reshape(s * yl * z * c, x, 8, half)
     result, before, after = lax.optimization_barrier((result, before, after))
     gathered = [
-        sorted_inputs,
+        inputs,
         before,
         along(before[:half], "x", x, 1),
         along(after[half:], "x", x, x - 1),
@@ -409,15 +387,14 @@
         for k in range(x)
     ]
 
-    spread, *home = lax.optimization_barrier((spread, *home))
+    own, other = weight_part(order, spread, gathered)
+    other, *home = lax.optimization_barrier((other, *home))
     home = [home[0]] + [along(home[k], "x", x, k) for k in range(1, x)]
-    own, other = weight_part(spread, gathered)
-    other, *home = lax.optimization_barrier((other, *home))
     other = along(other, "c", c, 1)
+    reduced = (own.astype(F32) + other.astype(F32)).astype(BF16).reshape(yl * z, 8, width)
+    _, *home = lax.optimization_barrier((reduced, *home))
     mine, theirs = project(order, weights[0], home)
-    reduced = (own + other.astype(F32)).astype(BF16).reshape(yl * z, 8, width)
-    theirs, reduced = lax.optimization_barrier((theirs, reduced))
-    arrived = along(theirs, "s", s, 1)
+    arrived = jnp.concatenate([along(theirs[:half], "s", s, 1), along(theirs[half:], "s", s, 1)])
     pieces = lax.all_to_all(reduced, ("yl", "z"), split_axis=0, concat_axis=0, tiled=True)
     grad_scale = 1.0 / math.sqrt(tokens * groups)
     weight_grad = jnp.sum(pieces.astype(F32), 0) * grad_scale

time: 107 us -> 102 us (0.953)
  Pallas kernels: 31 us -> 27.6 us
  starting transfers between devices: 42.8 us -> 41.3 us
  waiting for transfers between devices: 20.2 us -> 21.5 us
  matrix products: 1.18 us -> 0 us
    ppermute x9 -> x10, waiting for transfers between devices: 3.31 us -> 13.3 us  [along(): lax.ppermute(array, axis, [(i, (i + offset) % size) for i in range(size)])]
    all_to_all x1, waiting for transfers between devices: 5.51 us -> 0.01 us  [body(): lax.all_to_all(reduced, ('yl', 'z'), split_axis=0, concat_axis=0, tiled=T...]
    all_to_all x1, waiting for transfers between devices: 11.3 us -> 7.03 us  [body(): lax.all_to_all(result, ('s', 'yl', 'z', 'c'), split_axis=0, concat_axis=0...]
    pallas_call x1, Pallas kernels: 4.18 us -> 2.24 us  [weight_part(): pl.pallas_call(weight_kernel, out_shape=[jax.ShapeDtypeStruct((rows // 2,...]
    unnamed x12, local copies, waits for them, and re-layouts: 2.69 us -> 4.58 us
    dot_general x1 -> x0, matrix products: 1.18 us -> none  [body(): lax.dot_general(order, inputs, (((0,), (0,)), ((), ())), preferred_elemen...]
    all_to_all x1, starting transfers between devices: 10.9 us -> 9.7 us  [body(): lax.all_to_all(result, ('s', 'yl', 'z', 'c'), split_axis=0, concat_axis=0...]
    all_to_all x1, waiting for transfers between devices: 0.04 us -> 1.21 us  [body(): lax.all_to_all(send, ('yl', 'x', 'z', 'c'), split_axis=0, concat_axis=0,...]
  transfers between devices with their start and end apart: 12 -> 13, of which waited for: 5 -> 7; matrix products, arithmetic and copies ran while one was open for 6% -> 4% of each run, Pallas kernels for 27% -> 24%
where the time goes in v3:
time: 102 us; the launch traced here: 101 us
  starting transfers between devices  41.3 us (40%)
  Pallas kernels  27.6 us (27%)
  waiting for transfers between devices  21.5 us (21%)
  local copies, waits for them, and re-layouts  7.75 us (8%)
  other arithmetic  2.25 us (2%)
    all_to_all x1, starting transfers between devices, body(): lax.all_to_all(send, ('yl', 'x', 'z', 'c'), split_axis=0, concat_axis=0,...  14.8 us
    pallas_call x1, Pallas kernels, filtered(): pl.pallas_call(filter_kernel, grid=(1,), out_shape=jax.ShapeDtypeStruct((...  14.1 us
    ppermute x10, waiting for transfers between devices, along(): lax.ppermute(array, axis, [(i, (i + offset) % size) for i in range(size)])  13.3 us
    ppermute x10, starting transfers between devices, along(): lax.ppermute(array, axis, [(i, (i + offset) % size) for i in range(size)])  12.6 us
    all_to_all x1, starting transfers between devices, body(): lax.all_to_all(result, ('s', 'yl', 'z', 'c'), split_axis=0, concat_axis=0...  9.7 us
    pallas_call x1, Pallas kernels, toeplitz(): pl.pallas_call(toeplitz_kernel, grid=(parts,), out_shape=jax.ShapeDtypeSt...  8.56 us
    all_to_all x1, waiting for transfers between devices, body(): lax.all_to_all(result, ('s', 'yl', 'z', 'c'), split_axis=0, concat_axis=0...  7.03 us
    unnamed x12, local copies, waits for them, and re-layouts  4.58 us
  transfers between devices with their start and end apart: 13, of which 7 were waited for; matrix products, arithmetic and copies ran while one was open for 4% of the time, Pallas kernels for 24%

profile of v3, /device:TPU:1, one launch (start us, length us, event | category | flops | bytes accessed | tf_op | source)
XLA Modules:
  0.0 101.2 jit_solution(12730885959541155750)
XLA Ops:
  0.7 0.0 copy-start.3
  0.7 1.0 %copy-done.3 = bf16[256,1024]{1,0:T(8,128)(2,1)S(1)} copy-done((bf16[256,1024]{1,0:T(8,128)(2,1)S(1)}, bf16[256,1024]{1,0:T(8,128)(2,1)}, u32[]{:S(2)}) %copy-start.3) | copy-done | bytes 524312
  1.8 1.3 %shard_map.59 = bf16[128,8,128]{2,1,0:T(8,128)(2,1)} custom-call(bf16[256,256]{1,0:T(8,128)(2,1)S(1)} %fusion.1.order_ref, bf16[256,1024]{1,0:T(8,128)(2,1)S(1)} %copy-done.3), custom_call_target="tpu_custom_call" | custom-call | tf_op jit(solution)/shard_map/pallas_call | solution.py:197
  3.1 14.8 %all-to-all-start = ((bf16[128,8,128]{2,1,0:T(8,128)(2,1)}), bf16[128,8,128]{2,1,0:T(8,128)(2,1)S(1)}, u32[]{:S(2)}, u32[]{:S(2)}) async-start(bf16[128,8,128]{2,1,0:T(8,128)(2,1)} %shard_map.59), calls=%async_computation | async-start | bytes 524288 | tf_op jit(solution)/shard_map/all_to_all | solution.py:369
  17.8 0.0 copy-start.5
  17.9 0.9 copy-done.5
  18.8 8.6 %shard_map.60.taps_ref = bf16[16384,512]{1,0:T(8,128)(2,1)} custom-call(f32[256,128]{1,0:T(8,128)S(1)} %bitcast.17), custom_call_target="tpu_custom_call" | custom-call | flops 33554432 | bytes 16777216 | tf_op jit(solution)/shard_map/pallas_call | solution.py:63
  27.3 0.0 copy-start
  27.3 1.4 %collective-permute-start = (bf16[256,1024]{1,0:T(8,128)(2,1)}, bf16[256,1024]{1,0:T(8,128)(2,1)S(1)}, u32[]{:S(2)}, u32[]{:S(2)}) collective-permute-start(bf16[256,1024]{1,0:T(8,128)(2,1)} %refs_0_), channel_id=1, source_target_pairs={{0,16},{16,32},{32,48},{48,0},{1,17},{17,33},{33,49},{49,1},{2,18}... | collective-permute-start | bytes 1572872 | tf_op jit(solution)/shard_map/ppermute | solution.py:174
  28.7 1.4 %collective-permute-start.1 = (bf16[256,1024]{1,0:T(8,128)(2,1)}, bf16[256,1024]{1,0:T(8,128)(2,1)S(1)}, u32[]{:S(2)}, u32[]{:S(2)}) collective-permute-start(bf16[256,1024]{1,0:T(8,128)(2,1)} %refs_0_), channel_id=1, source_target_pairs={{0,48},{16,0},{32,16},{48,32},{1,49},{17,1},{33,17},{49,33},{2,50}... | collective-permute-start | bytes 1572872 | tf_op jit(solution)/shard_map/ppermute | solution.py:174
  30.1 1.2 %all-to-all-done.signal_ref = bf16[128,8,128]{2,1,0:T(8,128)(2,1)S(1)} async-done(((bf16[128,8,128]{2,1,0:T(8,128)(2,1)}), bf16[128,8,128]{2,1,0:T(8,128)(2,1)S(1)}, u32[]{:S(2)}, u32[]{:S(2)}) %all-to-all-start) | async-done | bytes 262176 | tf_op jit(solution)/shard_map/all_to_all | solution.py:369
  31.3 14.1 %shard_map.61 = bf16[2,2,8,2,4,8,128]{6,5,4,3,2,1,0:T(8,128)(2,1)S(1)} custom-call(bf16[128,8,128]{2,1,0:T(8,128)(2,1)S(1)} %all-to-all-done.signal_ref, bf16[16384,512]{1,0:T(8,128)(2,1)} %shard_map.60.taps_ref), custom_call_target="tpu_custom_call" | custom-call | flops 34359738368 | bytes 16777216 | tf_op jit(solution)/shard_map/pallas_call | solution.py:151
  45.4 0.0 copy-start.4
  45.4 0.8 copy-done.4
  46.2 0.0 collective-permute-done.refs_1_
  46.2 0.0 collective-permute-done.1.refs_4_
  46.2 0.0 copy-start.1
  46.2 0.8 copy-done.1
  47.0 9.7 %all-to-all-start.1 = ((bf16[64,4,8,128]{3,2,1,0:T(8,128)(2,1)}), bf16[64,4,8,128]{3,2,1,0:T(8,128)(2,1)S(1)}, u32[]{:S(2)}, u32[]{:S(2)}) async-start(bf16[64,4,8,128]{3,2,1,0:T(8,128)(2,1)} %bitcast.16), calls=%async_computation.1 | async-start | bytes 1048576 | tf_op jit(solution)/shard_map/all_to_all | solution.py:384
  56.7 0.7 slice.12
  57.5 0.1 collective-permute-start.2
  57.5 1.7 %slice.13 = bf16[128,1024]{1,0:T(8,128)(2,1)} slice(bf16[256,1024]{1,0:T(8,128)(2,1)} %copy-done.1), slice={[128:256], [0:1024]} | slice | bytes 524288 | tf_op jit(solution)/shard_map/slice | solution.py:381
  59.2 2.6 %collective-permute-start.3 = (bf16[128,1024]{1,0:T(8,128)(2,1)}, bf16[128,1024]{1,0:T(8,128)(2,1)}, u32[]{:S(2)}, u32[]{:S(2)}) collective-permute-start(bf16[128,1024]{1,0:T(8,128)(2,1)} %slice.13), channel_id=1, source_target_pairs={{0,48},{16,0},{32,16},{48,32},{1,49},{17,1},{33,17},{49,33},{2,50}... | collective-permute-start | bytes 786440 | tf_op jit(solution)/shard_map/ppermute | solution.py:174
  61.8 4.5 %collective-permute-done.2.refs_2_ = bf16[128,1024]{1,0:T(8,128)(2,1)S(1)} collective-permute-done((bf16[128,1024]{1,0:T(8,128)(2,1)}, bf16[128,1024]{1,0:T(8,128)(2,1)S(1)}, u32[]{:S(2)}, u32[]{:S(2)}) %collective-permute-start.2) | collective-permute-done | bytes 262176 | tf_op jit(solution)/shard_map/ppermute | solution.py:174
  66.3 0.7 collective-permute-done.3.refs_3_
  67.0 7.0 %all-to-all-done.1.spread_ref = bf16[64,4,8,128]{3,2,1,0:T(8,128)(2,1)S(1)} async-done(((bf16[64,4,8,128]{3,2,1,0:T(8,128)(2,1)}), bf16[64,4,8,128]{3,2,1,0:T(8,128)(2,1)S(1)}, u32[]{:S(2)}, u32[]{:S(2)}) %all-to-all-start.1) | async-done | bytes 524320 | tf_op jit(solution)/shard_map/all_to_all | solution.py:384
  74.1 1.0 %copy-done.2 = bf16[256,1024]{1,0:T(8,128)(2,1)S(1)} copy-done((bf16[256,1024]{1,0:T(8,128)(2,1)S(1)}, bf16[256,1024]{1,0:T(8,128)(2,1)}, u32[]{:S(2)}) %copy-start.2) | copy-done | bytes 524312
  75.1 2.2 %shard_map.62 = (bf16[128,1024]{1,0:T(8,128)(2,1)S(1)}, bf16[128,1024]{1,0:T(8,128)(2,1)S(1)}) custom-call(bf16[256,256]{1,0:T(8,128)(2,1)S(1)} %fusion.1.order_ref, bf16[64,4,8,128]{3,2,1,0:T(8,128)(2,1)S(1)} %all-to-all-done.1.spread_ref, bf16[256,1024]{1,0:T(8,128)(2,1)} %refs_0_, bf16[256,1024]{1,0:T(8,128)(2,1)S(1)} %collective-permute-done.refs_1_, ...), custom_call_target="tpu_custom_call" | custom-call | flops 536870912 | bytes 4194304 | tf_op jit(solution)/shard_map/pallas_call | solution.py:269
  77.3 0.8 dynamic-slice_bitcast_fusion
  78.1 0.3 collective-permute-start.4
  78.4 0.1 collective-permute-start.5
  78.5 2.6 %collective-permute-start.6 = (bf16[64,8,128]{2,1,0:T(8,128)(2,1)S(1)}, bf16[64,8,128]{2,1,0:T(8,128)(2,1)S(1)}, u32[]{:S(2)}, u32[]{:S(2)}) collective-permute-start(bf16[64,8,128]{2,1,0:T(8,128)(2,1)S(1)} %get-tuple-element.30), channel_id=1, source_target_pairs={{0,32},{16,48},{32,0},{48,16},{1,33},{17,49},{33,1},{49,17},{2,34}... | collective-permute-start | bytes 393224 | tf_op jit(solution)/shard_map/ppermute | solution.py:174
  81.1 1.1 %collective-permute-start.7 = (bf16[64,8,128]{2,1,0:T(8,128)(2,1)S(1)}, bf16[64,8,128]{2,1,0:T(8,128)(2,1)S(1)}, u32[]{:S(2)}, u32[]{:S(2)}) collective-permute-start(bf16[64,8,128]{2,1,0:T(8,128)(2,1)S(1)} %get-tuple-element.31), channel_id=1, source_target_pairs={{0,48},{16,0},{32,16},{48,32},{1,49},{17,1},{33,17},{49,33},{2,50}... | collective-permute-start | bytes 393224 | tf_op jit(solution)/shard_map/ppermute | solution.py:174
  82.2 0.0 collective-permute-done.4
  82.2 0.8 fusion
  83.0 4.2 %all-to-all-start.2 = ((bf16[16,8,1024]{2,1,0:T(8,128)(2,1)}), bf16[16,8,1024]{2,1,0:T(8,128)(2,1)S(1)}, u32[]{:S(2)}, u32[]{:S(2)}) async-start(bf16[16,8,1024]{2,1,0:T(8,128)(2,1)} %fusion), calls=%async_computation.2 | async-start | bytes 524288 | tf_op jit(solution)/shard_map/all_to_all | solution.py:398
  87.1 0.0 collective-permute-done.5.refs_1_
  87.2 0.4 collective-permute-done.6.refs_2_
  87.6 0.0 collective-permute-done.7.refs_3_
  87.6 0.0 copy-done
  87.6 1.4 %shard_map.63 = (bf16[256,512]{1,0:T(8,128)(2,1)S(1)}, bf16[256,512]{1,0:T(8,128)(2,1)S(1)}) custom-call(bf16[256,256]{1,0:T(8,128)(2,1)S(1)} %fusion.1.order_ref, bf16[1024,1024]{1,0:T(8,128)(2,1)S(1)} %bitcast.15, bf16[64,8,128]{2,1,0:T(8,128)(2,1)S(1)} %get-tuple-element.32.refs_0_, bf16[64,8,128]{2,1,0:T(8,128)(2,1)S(1)} %collective-permute-done.5.refs_1_, ...), custom_call_target="tpu_custom_call" | custom-call | flops 536870912 | bytes 4194304 | tf_op jit(solution)/shard_map/pallas_call | solution.py:339
  89.1 2.2 %collective-permute-start.9 = (bf16[128,512]{1,0:T(8,128)(2,1)S(1)}, bf16[128,512]{1,0:T(8,128)(2,1)S(1)}, u32[]{:S(2)}, u32[]{:S(2)}) collective-permute-start(bf16[128,512]{1,0:T(8,128)(2,1)S(1)} %get-tuple-element.43), channel_id=1, source_target_pairs={{0,128},{128,0},{1,129},{129,1},{2,130},{130,2},{3,131},{131,3},{4... | collective-permute-start | bytes 393224 | tf_op jit(solution)/shard_map/ppermute | solution.py:174
  91.3 0.8 collective-permute-start.8
  92.1 3.9 %collective-permute-done.9 = bf16[128,512]{1,0:T(8,128)(2,1)S(1)} collective-permute-done((bf16[128,512]{1,0:T(8,128)(2,1)S(1)}, bf16[128,512]{1,0:T(8,128)(2,1)S(1)}, u32[]{:S(2)}, u32[]{:S(2)}) %collective-permute-start.9) | collective-permute-done | bytes 131104 | tf_op jit(solution)/shard_map/ppermute | solution.py:174
  96.1 3.7 %collective-permute-done.8 = bf16[128,512]{1,0:T(8,128)(2,1)S(1)} collective-permute-done((bf16[128,512]{1,0:T(8,128)(2,1)S(1)}, bf16[128,512]{1,0:T(8,128)(2,1)S(1)}, u32[]{:S(2)}, u32[]{:S(2)}) %collective-permute-start.8) | collective-permute-done | bytes 131104 | tf_op jit(solution)/shard_map/ppermute | solution.py:174
  99.8 0.8 add_convert_fusion
  100.5 0.0 all-to-all-done.2
  100.6 0.6 multiply_bitcast_fusion
  (7 shorter events, 0.1 us)
Async XLA Ops:
  0.7 1.0 %copy-start.3 = (bf16[256,1024]{1,0:T(8,128)(2,1)S(1)}, bf16[256,1024]{1,0:T(8,128)(2,1)}, u32[]{:S(2)}) copy-start(bf16[256,1024]{1,0:T(8,128)(2,1)} %cotangent_ref.1) | copy-start | bytes 1572868
  3.1 28.3 %all-to-all-start = ((bf16[128,8,128]{2,1,0:T(8,128)(2,1)}), bf16[128,8,128]{2,1,0:T(8,128)(2,1)S(1)}, u32[]{:S(2)}, u32[]{:S(2)}) async-start(bf16[128,8,128]{2,1,0:T(8,128)(2,1)} %shard_map.59), calls=%async_computation | async-start | bytes 524288 | tf_op jit(solution)/shard_map/all_to_all | solution.py:369
  17.8 0.9 copy-start.5
  27.3 60.3 %copy-start = (bf16[1,1024,1024]{2,1,0:T(8,128)(2,1)S(1)}, bf16[1,1024,1024]{2,1,0:T(8,128)(2,1)}, u32[]{:S(2)}) copy-start(bf16[1,1024,1024]{2,1,0:T(8,128)(2,1)} %param.6) | copy-start | bytes 6291460
  27.3 18.9 %collective-permute-start = (bf16[256,1024]{1,0:T(8,128)(2,1)}, bf16[256,1024]{1,0:T(8,128)(2,1)S(1)}, u32[]{:S(2)}, u32[]{:S(2)}) collective-permute-start(bf16[256,1024]{1,0:T(8,128)(2,1)} %refs_0_), channel_id=1, source_target_pairs={{0,16},{16,32},{32,48},{48,0},{1,17},{17,33},{33,49},{49,1},{2,18}... | collective-permute-start | bytes 1572872 | tf_op jit(solution)/shard_map/ppermute | solution.py:174
  28.7 17.5 %collective-permute-start.1 = (bf16[256,1024]{1,0:T(8,128)(2,1)}, bf16[256,1024]{1,0:T(8,128)(2,1)S(1)}, u32[]{:S(2)}, u32[]{:S(2)}) collective-permute-start(bf16[256,1024]{1,0:T(8,128)(2,1)} %refs_0_), channel_id=1, source_target_pairs={{0,48},{16,0},{32,16},{48,32},{1,49},{17,1},{33,17},{49,33},{2,50}... | collective-permute-start | bytes 1572872 | tf_op jit(solution)/shard_map/ppermute | solution.py:174
  45.4 0.8 copy-start.4
  46.2 0.8 copy-start.1
  47.0 27.0 %all-to-all-start.1 = ((bf16[64,4,8,128]{3,2,1,0:T(8,128)(2,1)}), bf16[64,4,8,128]{3,2,1,0:T(8,128)(2,1)S(1)}, u32[]{:S(2)}, u32[]{:S(2)}) async-start(bf16[64,4,8,128]{3,2,1,0:T(8,128)(2,1)} %bitcast.16), calls=%async_computation.1 | async-start | bytes 1048576 | tf_op jit(solution)/shard_map/all_to_all | solution.py:384
  57.5 8.8 %collective-permute-start.2 = (bf16[128,1024]{1,0:T(8,128)(2,1)}, bf16[128,1024]{1,0:T(8,128)(2,1)S(1)}, u32[]{:S(2)}, u32[]{:S(2)}) collective-permute-start(bf16[128,1024]{1,0:T(8,128)(2,1)} %slice.12), channel_id=1, source_target_pairs={{0,16},{16,32},{32,48},{48,0},{1,17},{17,33},{33,49},{49,1},{2,18}... | collective-permute-start | bytes 786440 | tf_op jit(solution)/shard_map/ppermute | solution.py:174
  59.2 7.8 %collective-permute-start.3 = (bf16[128,1024]{1,0:T(8,128)(2,1)}, bf16[128,1024]{1,0:T(8,128)(2,1)}, u32[]{:S(2)}, u32[]{:S(2)}) collective-permute-start(bf16[128,1024]{1,0:T(8,128)(2,1)} %slice.13), channel_id=1, source_target_pairs={{0,48},{16,0},{32,16},{48,32},{1,49},{17,1},{33,17},{49,33},{2,50}... | collective-permute-start | bytes 786440 | tf_op jit(solution)/shard_map/ppermute | solution.py:174
  74.1 1.0 %copy-start.2 = (bf16[256,1024]{1,0:T(8,128)(2,1)S(1)}, bf16[256,1024]{1,0:T(8,128)(2,1)}, u32[]{:S(2)}) copy-start(bf16[256,1024]{1,0:T(8,128)(2,1)} %copy-done.1) | copy-start | bytes 1572868
  78.1 4.1 %collective-permute-start.4 = (bf16[128,1024]{1,0:T(8,128)(2,1)S(1)}, bf16[128,1024]{1,0:T(8,128)(2,1)S(1)}, u32[]{:S(2)}, u32[]{:S(2)}) collective-permute-start(bf16[128,1024]{1,0:T(8,128)(2,1)S(1)} %get-tuple-element.27), channel_id=1, source_target_pairs={{0,1},{1,0},{2,3},{3,2},{4,5},{5,4},{6,7},{7,6},{8,9},{9,8},{10,11... | collective-permute-start | bytes 786440 | tf_op jit(solution)/shard_map/ppermute | solution.py:174
  78.4 8.7 %collective-permute-start.5 = (bf16[64,8,128]{2,1,0:T(8,128)(2,1)}, bf16[64,8,128]{2,1,0:T(8,128)(2,1)S(1)}, u32[]{:S(2)}, u32[]{:S(2)}) collective-permute-start(bf16[64,8,128]{2,1,0:T(8,128)(2,1)} %get-tuple-element.29), channel_id=1, source_target_pairs={{0,16},{16,32},{32,48},{48,0},{1,17},{17,33},{33,49},{49,1},{2,18}... | collective-permute-start | bytes 393224 | tf_op jit(solution)/shard_map/ppermute | solution.py:174
  78.5 9.1 %collective-permute-start.6 = (bf16[64,8,128]{2,1,0:T(8,128)(2,1)S(1)}, bf16[64,8,128]{2,1,0:T(8,128)(2,1)S(1)}, u32[]{:S(2)}, u32[]{:S(2)}) collective-permute-start(bf16[64,8,128]{2,1,0:T(8,128)(2,1)S(1)} %get-tuple-element.30), channel_id=1, source_target_pairs={{0,32},{16,48},{32,0},{48,16},{1,33},{17,49},{33,1},{49,17},{2,34}... | collective-permute-start | bytes 393224 | tf_op jit(solution)/shard_map/ppermute | solution.py:174
  81.1 6.5 %collective-permute-start.7 = (bf16[64,8,128]{2,1,0:T(8,128)(2,1)S(1)}, bf16[64,8,128]{2,1,0:T(8,128)(2,1)S(1)}, u32[]{:S(2)}, u32[]{:S(2)}) collective-permute-start(bf16[64,8,128]{2,1,0:T(8,128)(2,1)S(1)} %get-tuple-element.31), channel_id=1, source_target_pairs={{0,48},{16,0},{32,16},{48,32},{1,49},{17,1},{33,17},{49,33},{2,50}... | collective-permute-start | bytes 393224 | tf_op jit(solution)/shard_map/ppermute | solution.py:174
  83.0 17.6 %all-to-all-start.2 = ((bf16[16,8,1024]{2,1,0:T(8,128)(2,1)}), bf16[16,8,1024]{2,1,0:T(8,128)(2,1)S(1)}, u32[]{:S(2)}, u32[]{:S(2)}) async-start(bf16[16,8,1024]{2,1,0:T(8,128)(2,1)} %fusion), calls=%async_computation.2 | async-start | bytes 524288 | tf_op jit(solution)/shard_map/all_to_all | solution.py:398
  89.1 7.0 %collective-permute-start.9 = (bf16[128,512]{1,0:T(8,128)(2,1)S(1)}, bf16[128,512]{1,0:T(8,128)(2,1)S(1)}, u32[]{:S(2)}, u32[]{:S(2)}) collective-permute-start(bf16[128,512]{1,0:T(8,128)(2,1)S(1)} %get-tuple-element.43), channel_id=1, source_target_pairs={{0,128},{128,0},{1,129},{129,1},{2,130},{130,2},{3,131},{131,3},{4... | collective-permute-start | bytes 393224 | tf_op jit(solution)/shard_map/ppermute | solution.py:174
  91.3 8.4 %collective-permute-start.8 = (bf16[128,512]{1,0:T(8,128)(2,1)S(1)}, bf16[128,512]{1,0:T(8,128)(2,1)S(1)}, u32[]{:S(2)}, u32[]{:S(2)}) collective-permute-start(bf16[128,512]{1,0:T(8,128)(2,1)S(1)} %get-tuple-element.42), channel_id=1, source_target_pairs={{0,128},{128,0},{1,129},{129,1},{2,130},{130,2},{3,131},{131,3},{4... | collective-permute-start | bytes 393224 | tf_op jit(solution)/shard_map/ppermute | solution.py:174

commit v4 on v3

--- a/solution.py
+++ b/solution.py
@@ -211,81 +211,96 @@
     return even.astype(BF16), odd.astype(BF16)
 
 
-def weight_kernel(order_ref, spread_ref, *refs):
-    *gathered, own_ref, other_ref, blocks, left, turned, right, sent, arrived = refs
-    x = blocks.shape[0]
-    half = blocks.shape[1] // 2
-    tiles = half // 2
-    tokens = right.shape[0] // x
-    x_here, c_here = lax.axis_index("x"), lax.axis_index("c")
-    upper = lax.broadcasted_iota(jnp.int32, (8, LANES), 0) < 4
-    fetches, copies, row = [], [], 0
-    for k in range(x):
-        block = lax.rem(x_here - k + x, x)
-        fetches.append(pltpu.make_async_copy(spread_ref.at[:, block], blocks.at[k], sent.at[k]))
-        fetches[k].start()
+def arrange_kernel(order_ref, *refs):
+    *gathered, out_ref, held, arrived = refs
+    tokens = order_ref.shape[0]
+    copies, row = [], 0
     for n, ref in enumerate(gathered):
         copies.append(
-            pltpu.make_async_copy(ref, right.at[row : row + ref.shape[0], :], arrived.at[n])
+            pltpu.make_async_copy(ref, held.at[row : row + ref.shape[0], :], arrived.at[n])
         )
         row += ref.shape[0]
         copies[n].start()
+    for copy in copies:
+        copy.wait()
+    for k in range(row // tokens):
+        part = slice(k * tokens, (k + 1) * tokens)
+        out_ref[part, :] = lax.dot_general(
+            order_ref[...], held[part, :], (((0,), (0,)), ((), ())), preferred_element_type=F32
+        ).astype(BF16)
+
+
+def arrange(order, gathered):
+    rows, width = sum(part.shape[0] for part in gathered), gathered[0].shape[1]
+    return pl.pallas_call(
+        arrange_kernel,
+        out_shape=jax.ShapeDtypeStruct((rows, width), BF16),
+        in_specs=[VMEM] + [ANY] * len(gathered),
+        out_specs=VMEM,
+        scratch_shapes=[
+            pltpu.VMEM((rows, width), BF16),
+            pltpu.SemaphoreType.DMA((len(gathered),)),
+        ],
+        compiler_params=pltpu.CompilerParams(vmem_limit_bytes=24 << 20),
+        cost_estimate=pl.CostEstimate(
+            flops=2 * rows * order.shape[0] * width,
+            bytes_accessed=4 * rows * width,
+            transcendentals=0,
+        ),
+    )(order, *gathered)
+
+
+def weight_kernel(spread_ref, inputs_ref, own_ref, other_ref, left):
+    x = spread_ref.shape[1]
+    half = spread_ref.shape[0] // 2
+    tiles = half // 2
+    x_here, c_here = lax.axis_index("x"), lax.axis_index("c")
+    upper = lax.broadcasted_iota(jnp.int32, (8, LANES), 0) < 4
     for k in range(x):
-        fetches[k].wait()
+        block = lax.rem(x_here - k + x, x)
         for part in range(2):
             core = c_here if part == 0 else 1 - c_here
 
-            def place(i, carry, k=k, part=part, core=core):
+            def place(i, carry, k=k, block=block, part=part, core=core):
                 pairs = [
                     pair(
-                        blocks[k, 2 * (2 * i + n) + core],
-                        blocks[k, half + 2 * (2 * i + n) + core],
+                        spread_ref[2 * (2 * i + n) + core, block],
+                        spread_ref[half + 2 * (2 * i + n) + core, block],
                         upper,
                     )
                     for n in range(2)
                 ]
                 at = pl.multiple_of(part * tiles * 8 + i * 16, 16)
                 for parity in range(2):
-                    left[pl.ds(at, 16), parity * LANES : (parity + 1) * LANES] = (
-                        jnp.concatenate([pairs[0][parity], pairs[1][parity]], 0)
+                    col = (2 * k + parity) * LANES
+                    left[pl.ds(at, 16), col : col + LANES] = jnp.concatenate(
+                        [pairs[0][parity], pairs[1][parity]], 0
                     )
                 return carry
 
             lax.fori_loop(0, tiles // 2, place, 0, unroll=4)
-        turned[:, k * tokens : (k + 1) * tokens] = lax.dot_general(
-            left[...], order_ref[...], (((1,), (1,)), ((), ())), preferred_element_type=F32
-        ).astype(BF16)
-    for copy in copies:
-        copy.wait()
-    y = jnp.dot(turned[...], right[...], preferred_element_type=F32).astype(BF16)
+    y = jnp.dot(left[...], inputs_ref[...], preferred_element_type=F32).astype(BF16)
     own_ref[...] = y[: tiles * 8, :]
     other_ref[...] = y[tiles * 8 :, :]
 
 
-def weight_part(order, spread, gathered):
-    count, x = spread.shape[:2]
-    tokens, width = gathered[0].shape
+def weight_part(spread, arranged):
+    count = spread.shape[0]
+    depth, width = arranged.shape
     rows = count * 4
     return pl.pallas_call(
         weight_kernel,
         out_shape=[jax.ShapeDtypeStruct((rows // 2, width), BF16)] * 2,
-        in_specs=[VMEM] + [ANY] * (1 + len(gathered)),
+        in_specs=[VMEM, VMEM],
         out_specs=[VMEM, VMEM],
-        scratch_shapes=[
-            pltpu.VMEM((x, count, 8, LANES), BF16),
-            pltpu.VMEM((rows, tokens), BF16),
-            pltpu.VMEM((rows, x * tokens), BF16),
-            pltpu.VMEM((x * tokens, width), BF16),
-            pltpu.SemaphoreType.DMA((x,)),
-            pltpu.SemaphoreType.DMA((len(gathered),)),
-        ],
+        scratch_shapes=[pltpu.VMEM((rows, depth), BF16)],
         compiler_params=pltpu.CompilerParams(vmem_limit_bytes=24 << 20),
         cost_estimate=pl.CostEstimate(
-            flops=2 * rows * x * tokens * width,
-            bytes_accessed=4 * x * tokens * width,
+            flops=2 * rows * depth * width,
+            bytes_accessed=4 * depth * width,
             transcendentals=0,
         ),
-    )(order, spread, *gathered)
+    )(spread, arranged)
 
 
 def project_kernel(order_ref, weights_ref, *refs):
@@ -387,7 +402,7 @@
         for k in range(x)
     ]
 
-    own, other = weight_part(order, spread, gathered)
+    own, other = weight_part(spread, arrange(order, gathered))
     other, *home = lax.optimization_barrier((other, *home))
     home = [home[0]] + [along(home[k], "x", x, k) for k in range(1, x)]
     other = along(other, "c", c, 1)

time: 102 us -> 100 us (0.980)
  waiting for transfers between devices: 21.5 us -> 19.3 us
  starting transfers between devices: 41.3 us -> 42.6 us
  local copies, waits for them, and re-layouts: 7.75 us -> 6.5 us
    all_to_all x1, waiting for transfers between devices: 7.03 us -> 3.72 us  [body(): lax.all_to_all(result, ('s', 'yl', 'z', 'c'), split_axis=0, concat_axis=0...]
    slice x1, local copies, waits for them, and re-layouts: 1.67 us -> 0.02 us  [body(): after[half:]]
    pallas_call x1, Pallas kernels: 2.24 us -> 1.04 us  [weight_part(): pl.pallas_call(weight_kernel, out_shape=[jax.ShapeDtypeStruct((rows // 2,...]
    unnamed x12 -> x18, local copies, waits for them, and re-layouts: 4.58 us -> 5.68 us
    ppermute x10, waiting for transfers between devices: 13.3 us -> 14.4 us  [along(): lax.ppermute(array, axis, [(i, (i + offset) % size) for i in range(size)])]
  transfers between devices with their start and end apart: 13 -> 13, of which waited for: 7 -> 5; matrix products, arithmetic and copies ran while one was open for 4% -> 2% of each run, Pallas kernels for 24% -> 26%
where the time goes in v4:
time: 100 us; the launch traced here: 99.6 us
  starting transfers between devices  42.6 us (43%)
  Pallas kernels  28.2 us (28%)
  waiting for transfers between devices  19.3 us (19%)
  local copies, waits for them, and re-layouts  6.5 us (6%)
  other arithmetic  2.25 us (2%)
    pallas_call x1, Pallas kernels, filtered(): pl.pallas_call(filter_kernel, grid=(1,), out_shape=jax.ShapeDtypeStruct((...  14.9 us
    all_to_all x1, starting transfers between devices, body(): lax.all_to_all(send, ('yl', 'x', 'z', 'c'), split_axis=0, concat_axis=0,...  14.8 us
    ppermute x10, waiting for transfers between devices, along(): lax.ppermute(array, axis, [(i, (i + offset) % size) for i in range(size)])  14.4 us
    ppermute x10, starting transfers between devices, along(): lax.ppermute(array, axis, [(i, (i + offset) % size) for i in range(size)])  13 us
    all_to_all x1, starting transfers between devices, body(): lax.all_to_all(result, ('s', 'yl', 'z', 'c'), split_axis=0, concat_axis=0...  9.72 us
    pallas_call x1, Pallas kernels, toeplitz(): pl.pallas_call(toeplitz_kernel, grid=(parts,), out_shape=jax.ShapeDtypeSt...  8.57 us
    unnamed x18, local copies, waits for them, and re-layouts  5.68 us
    all_to_all x1, starting transfers between devices, body(): lax.all_to_all(reduced, ('yl', 'z'), split_axis=0, concat_axis=0, tiled=T...  5.09 us
  transfers between devices with their start and end apart: 13, of which 5 were waited for; matrix products, arithmetic and copies ran while one was open for 2% of the time, Pallas kernels for 26%

profile of v4, /device:TPU:1, one launch (start us, length us, event | category | flops | bytes accessed | tf_op | source)
XLA Modules:
  0.0 99.6 jit_solution(7183810688765910213)
XLA Ops:
  0.7 0.0 copy-start.5
  0.7 1.0 %copy-done.5 = bf16[256,1024]{1,0:T(8,128)(2,1)S(1)} copy-done((bf16[256,1024]{1,0:T(8,128)(2,1)S(1)}, bf16[256,1024]{1,0:T(8,128)(2,1)}, u32[]{:S(2)}) %copy-start.5) | copy-done | bytes 524312
  1.8 1.3 %shard_map.59 = bf16[128,8,128]{2,1,0:T(8,128)(2,1)} custom-call(bf16[256,256]{1,0:T(8,128)(2,1)S(1)} %fusion.1.order_ref, bf16[256,1024]{1,0:T(8,128)(2,1)S(1)} %copy-done.5), custom_call_target="tpu_custom_call" | custom-call | tf_op jit(solution)/shard_map/pallas_call | solution.py:197
  3.1 14.8 %all-to-all-start = ((bf16[128,8,128]{2,1,0:T(8,128)(2,1)}), bf16[128,8,128]{2,1,0:T(8,128)(2,1)S(1)}, u32[]{:S(2)}, u32[]{:S(2)}) async-start(bf16[128,8,128]{2,1,0:T(8,128)(2,1)} %shard_map.59), calls=%async_computation | async-start | bytes 524288 | tf_op jit(solution)/shard_map/all_to_all | solution.py:384
  17.8 0.0 copy-start.8
  17.9 0.9 copy-done.8
  18.8 8.6 %shard_map.60.taps_ref = bf16[16384,512]{1,0:T(8,128)(2,1)} custom-call(f32[256,128]{1,0:T(8,128)S(1)} %bitcast.16), custom_call_target="tpu_custom_call" | custom-call | flops 33554432 | bytes 16777216 | tf_op jit(solution)/shard_map/pallas_call | solution.py:63
  27.3 0.0 copy-done.3
  27.3 1.4 %collective-permute-start = (bf16[256,1024]{1,0:T(8,128)(2,1)S(1)}, bf16[256,1024]{1,0:T(8,128)(2,1)S(1)}, u32[]{:S(2)}, u32[]{:S(2)}) collective-permute-start(bf16[256,1024]{1,0:T(8,128)(2,1)S(1)} %copy-done.3), channel_id=1, source_target_pairs={{0,16},{16,32},{32,48},{48,0},{1,17},{17,33},{33,49},{49,1},{2,18}... | collective-permute-start | bytes 1572872 | tf_op jit(solution)/shard_map/ppermute | solution.py:174
  28.7 1.4 %collective-permute-start.1 = (bf16[256,1024]{1,0:T(8,128)(2,1)S(1)}, bf16[256,1024]{1,0:T(8,128)(2,1)S(1)}, u32[]{:S(2)}, u32[]{:S(2)}) collective-permute-start(bf16[256,1024]{1,0:T(8,128)(2,1)S(1)} %copy-done.3), channel_id=1, source_target_pairs={{0,48},{16,0},{32,16},{48,32},{1,49},{17,1},{33,17},{49,33},{2,50}... | collective-permute-start | bytes 1572872 | tf_op jit(solution)/shard_map/ppermute | solution.py:174
  30.1 1.2 %all-to-all-done.signal_ref = bf16[128,8,128]{2,1,0:T(8,128)(2,1)S(1)} async-done(((bf16[128,8,128]{2,1,0:T(8,128)(2,1)}), bf16[128,8,128]{2,1,0:T(8,128)(2,1)S(1)}, u32[]{:S(2)}, u32[]{:S(2)}) %all-to-all-start) | async-done | bytes 262176 | tf_op jit(solution)/shard_map/all_to_all | solution.py:384
  31.3 14.9 %shard_map.61 = bf16[2,2,8,2,4,8,128]{6,5,4,3,2,1,0:T(8,128)(2,1)} custom-call(bf16[128,8,128]{2,1,0:T(8,128)(2,1)S(1)} %all-to-all-done.signal_ref, bf16[16384,512]{1,0:T(8,128)(2,1)} %shard_map.60.taps_ref), custom_call_target="tpu_custom_call" | custom-call | flops 34359738368 | bytes 16777216 | tf_op jit(solution)/shard_map/pallas_call | solution.py:151
  46.2 0.0 collective-permute-done.refs_1_
  46.2 0.0 collective-permute-done.1.refs_4_
  46.2 0.0 copy-start.1
  46.2 9.7 %all-to-all-start.1 = ((bf16[64,4,8,128]{3,2,1,0:T(8,128)(2,1)}), bf16[64,4,8,128]{3,2,1,0:T(8,128)(2,1)S(1)}, u32[]{:S(2)}, u32[]{:S(2)}) async-start(bf16[64,4,8,128]{3,2,1,0:T(8,128)(2,1)} %bitcast.2), calls=%async_computation.1 | async-start | bytes 1048576 | tf_op jit(solution)/shard_map/all_to_all | solution.py:399
  56.0 0.3 collective-permute-start.2
  56.4 2.7 %collective-permute-start.3 = (bf16[128,1024]{1,0:T(8,128)(2,1)S(1)}, bf16[128,1024]{1,0:T(8,128)(2,1)S(1)}, u32[]{:S(2)}, u32[]{:S(2)}) collective-permute-start(bf16[128,1024]{1,0:T(8,128)(2,1)S(1)} %slice.13), channel_id=1, source_target_pairs={{0,48},{16,0},{32,16},{48,32},{1,49},{17,1},{33,17},{49,33},{2,50}... | collective-permute-start | bytes 786440 | tf_op jit(solution)/shard_map/ppermute | solution.py:174
  59.0 5.9 %collective-permute-done.2.refs_2_ = bf16[128,1024]{1,0:T(8,128)(2,1)S(1)} collective-permute-done((bf16[128,1024]{1,0:T(8,128)(2,1)S(1)}, bf16[128,1024]{1,0:T(8,128)(2,1)S(1)}, u32[]{:S(2)}, u32[]{:S(2)}) %collective-permute-start.2) | collective-permute-done | bytes 262176 | tf_op jit(solution)/shard_map/ppermute | solution.py:174
  64.9 0.0 copy-done.1
  64.9 0.0 collective-permute-done.3.refs_3_
  64.9 0.7 copy-done.6
  65.6 1.0 %copy-done.2 = bf16[256,1024]{1,0:T(8,128)(2,1)S(1)} copy-done((bf16[256,1024]{1,0:T(8,128)(2,1)S(1)}, bf16[256,1024]{1,0:T(8,128)(2,1)}, u32[]{:S(2)}) %copy-start.2) | copy-done | bytes 524312
  66.7 1.0 %copy-done.4 = bf16[256,1024]{1,0:T(8,128)(2,1)S(1)} copy-done((bf16[256,1024]{1,0:T(8,128)(2,1)S(1)}, bf16[256,1024]{1,0:T(8,128)(2,1)}, u32[]{:S(2)}) %copy-start.4) | copy-done | bytes 524312
  67.7 0.9 copy-done.7
  68.6 0.9 shard_map.62.inputs_ref
  69.6 3.7 %all-to-all-done.1.spread_ref = bf16[64,4,8,128]{3,2,1,0:T(8,128)(2,1)S(1)} async-done(((bf16[64,4,8,128]{3,2,1,0:T(8,128)(2,1)}), bf16[64,4,8,128]{3,2,1,0:T(8,128)(2,1)S(1)}, u32[]{:S(2)}, u32[]{:S(2)}) %all-to-all-start.1) | async-done | bytes 524320 | tf_op jit(solution)/shard_map/all_to_all | solution.py:399
  73.3 1.0 %shard_map.63 = (bf16[128,1024]{1,0:T(8,128)(2,1)S(1)}, bf16[128,1024]{1,0:T(8,128)(2,1)S(1)}) custom-call(bf16[64,4,8,128]{3,2,1,0:T(8,128)(2,1)S(1)} %all-to-all-done.1.spread_ref, bf16[1024,1024]{1,0:T(8,128)(2,1)S(1)} %shard_map.62.inputs_ref), custom_call_target="tpu_custom_call" | custom-call | flops 536870912 | bytes 4194304 | tf_op jit(solution)/shard_map/pallas_call | solution.py:291
  74.4 0.0 copy-start
  74.4 0.8 dynamic-slice_bitcast_fusion
  75.1 0.3 collective-permute-start.4
  75.4 0.1 collective-permute-start.5
  75.5 2.6 %collective-permute-start.6 = (bf16[64,8,128]{2,1,0:T(8,128)(2,1)S(1)}, bf16[64,8,128]{2,1,0:T(8,128)(2,1)S(1)}, u32[]{:S(2)}, u32[]{:S(2)}) collective-permute-start(bf16[64,8,128]{2,1,0:T(8,128)(2,1)S(1)} %get-tuple-element.30), channel_id=1, source_target_pairs={{0,32},{16,48},{32,0},{48,16},{1,33},{17,49},{33,1},{49,17},{2,34}... | collective-permute-start | bytes 393224 | tf_op jit(solution)/shard_map/ppermute | solution.py:174
  78.1 1.1 %collective-permute-start.7 = (bf16[64,8,128]{2,1,0:T(8,128)(2,1)S(1)}, bf16[64,8,128]{2,1,0:T(8,128)(2,1)S(1)}, u32[]{:S(2)}, u32[]{:S(2)}) collective-permute-start(bf16[64,8,128]{2,1,0:T(8,128)(2,1)S(1)} %get-tuple-element.31), channel_id=1, source_target_pairs={{0,48},{16,0},{32,16},{48,32},{1,49},{17,1},{33,17},{49,33},{2,50}... | collective-permute-start | bytes 393224 | tf_op jit(solution)/shard_map/ppermute | solution.py:174
  79.2 0.0 collective-permute-done.4
  79.2 0.8 fusion
  80.0 5.1 %all-to-all-start.2 = ((bf16[16,8,1024]{2,1,0:T(8,128)(2,1)}), bf16[16,8,1024]{2,1,0:T(8,128)(2,1)S(1)}, u32[]{:S(2)}, u32[]{:S(2)}) async-start(bf16[16,8,1024]{2,1,0:T(8,128)(2,1)} %fusion), calls=%async_computation.2 | async-start | bytes 524288 | tf_op jit(solution)/shard_map/all_to_all | solution.py:413
  85.1 0.0 collective-permute-done.5.refs_1_
  85.1 0.0 collective-permute-done.6.refs_2_
  85.1 0.0 collective-permute-done.7.refs_3_
  85.1 1.4 %shard_map.64 = (bf16[256,512]{1,0:T(8,128)(2,1)S(1)}, bf16[256,512]{1,0:T(8,128)(2,1)S(1)}) custom-call(bf16[256,256]{1,0:T(8,128)(2,1)S(1)} %fusion.1.order_ref, bf16[1024,1024]{1,0:T(8,128)(2,1)S(1)} %bitcast.15, bf16[64,8,128]{2,1,0:T(8,128)(2,1)S(1)} %get-tuple-element.32.refs_0_, bf16[64,8,128]{2,1,0:T(8,128)(2,1)S(1)} %collective-permute-done.5.refs_1_, ...), custom_call_target="tpu_custom_call" | custom-call | flops 536870912 | bytes 4194304 | tf_op jit(solution)/shard_map/pallas_call | solution.py:354
  86.6 2.7 %collective-permute-start.9 = (bf16[128,512]{1,0:T(8,128)(2,1)S(1)}, bf16[128,512]{1,0:T(8,128)(2,1)S(1)}, u32[]{:S(2)}, u32[]{:S(2)}) collective-permute-start(bf16[128,512]{1,0:T(8,128)(2,1)S(1)} %get-tuple-element.43), channel_id=1, source_target_pairs={{0,128},{128,0},{1,129},{129,1},{2,130},{130,2},{3,131},{131,3},{4... | collective-permute-start | bytes 393224 | tf_op jit(solution)/shard_map/ppermute | solution.py:174
  89.3 0.4 collective-permute-start.8
  89.7 4.5 %collective-permute-done.9 = bf16[128,512]{1,0:T(8,128)(2,1)S(1)} collective-permute-done((bf16[128,512]{1,0:T(8,128)(2,1)S(1)}, bf16[128,512]{1,0:T(8,128)(2,1)S(1)}, u32[]{:S(2)}, u32[]{:S(2)}) %collective-permute-start.9) | collective-permute-done | bytes 131104 | tf_op jit(solution)/shard_map/ppermute | solution.py:174
  94.1 4.0 %collective-permute-done.8 = bf16[128,512]{1,0:T(8,128)(2,1)S(1)} collective-permute-done((bf16[128,512]{1,0:T(8,128)(2,1)S(1)}, bf16[128,512]{1,0:T(8,128)(2,1)S(1)}, u32[]{:S(2)}, u32[]{:S(2)}) %collective-permute-start.8) | collective-permute-done | bytes 131104 | tf_op jit(solution)/shard_map/ppermute | solution.py:174
  98.2 0.8 add_convert_fusion
  98.9 0.0 all-to-all-done.2
  99.0 0.6 multiply_bitcast_fusion
  (14 shorter events, 0.2 us)
Async XLA Ops:
  0.7 1.0 %copy-start.5 = (bf16[256,1024]{1,0:T(8,128)(2,1)S(1)}, bf16[256,1024]{1,0:T(8,128)(2,1)}, u32[]{:S(2)}) copy-start(bf16[256,1024]{1,0:T(8,128)(2,1)} %cotangent_ref.1) | copy-start | bytes 1572868
  3.1 28.3 %all-to-all-start = ((bf16[128,8,128]{2,1,0:T(8,128)(2,1)}), bf16[128,8,128]{2,1,0:T(8,128)(2,1)S(1)}, u32[]{:S(2)}, u32[]{:S(2)}) async-start(bf16[128,8,128]{2,1,0:T(8,128)(2,1)} %shard_map.59), calls=%async_computation | async-start | bytes 524288 | tf_op jit(solution)/shard_map/all_to_all | solution.py:384
  17.8 0.9 copy-start.8
  18.8 8.6 %copy-start.3 = (bf16[256,1024]{1,0:T(8,128)(2,1)S(1)}, bf16[256,1024]{1,0:T(8,128)(2,1)}, u32[]{:S(2)}) copy-start(bf16[256,1024]{1,0:T(8,128)(2,1)} %refs_0_) | copy-start | bytes 1572868
  27.3 18.9 %collective-permute-start = (bf16[256,1024]{1,0:T(8,128)(2,1)S(1)}, bf16[256,1024]{1,0:T(8,128)(2,1)S(1)}, u32[]{:S(2)}, u32[]{:S(2)}) collective-permute-start(bf16[256,1024]{1,0:T(8,128)(2,1)S(1)} %copy-done.3), channel_id=1, source_target_pairs={{0,16},{16,32},{32,48},{48,0},{1,17},{17,33},{33,49},{49,1},{2,18}... | collective-permute-start | bytes 1572872 | tf_op jit(solution)/shard_map/ppermute | solution.py:174
  28.7 17.5 %collective-permute-start.1 = (bf16[256,1024]{1,0:T(8,128)(2,1)S(1)}, bf16[256,1024]{1,0:T(8,128)(2,1)S(1)}, u32[]{:S(2)}, u32[]{:S(2)}) collective-permute-start(bf16[256,1024]{1,0:T(8,128)(2,1)S(1)} %copy-done.3), channel_id=1, source_target_pairs={{0,48},{16,0},{32,16},{48,32},{1,49},{17,1},{33,17},{49,33},{2,50}... | collective-permute-start | bytes 1572872 | tf_op jit(solution)/shard_map/ppermute | solution.py:174
  46.2 18.7 %copy-start.1 = (bf16[256,1024]{1,0:T(8,128)(2,1)}, bf16[256,1024]{1,0:T(8,128)(2,1)S(1)}, u32[]{:S(2)}) copy-start(bf16[256,1024]{1,0:T(8,128)(2,1)S(1)} %collective-permute-done.1.refs_4_) | copy-start | bytes 1572868
  46.2 27.1 %all-to-all-start.1 = ((bf16[64,4,8,128]{3,2,1,0:T(8,128)(2,1)}), bf16[64,4,8,128]{3,2,1,0:T(8,128)(2,1)S(1)}, u32[]{:S(2)}, u32[]{:S(2)}) async-start(bf16[64,4,8,128]{3,2,1,0:T(8,128)(2,1)} %bitcast.2), calls=%async_computation.1 | async-start | bytes 1048576 | tf_op jit(solution)/shard_map/all_to_all | solution.py:399
  56.0 8.9 %collective-permute-start.2 = (bf16[128,1024]{1,0:T(8,128)(2,1)S(1)}, bf16[128,1024]{1,0:T(8,128)(2,1)S(1)}, u32[]{:S(2)}, u32[]{:S(2)}) collective-permute-start(bf16[128,1024]{1,0:T(8,128)(2,1)S(1)} %slice.12), channel_id=1, source_target_pairs={{0,16},{16,32},{32,48},{48,0},{1,17},{17,33},{33,49},{49,1},{2,18}... | collective-permute-start | bytes 786440 | tf_op jit(solution)/shard_map/ppermute | solution.py:174
  56.4 8.5 %collective-permute-start.3 = (bf16[128,1024]{1,0:T(8,128)(2,1)S(1)}, bf16[128,1024]{1,0:T(8,128)(2,1)S(1)}, u32[]{:S(2)}, u32[]{:S(2)}) collective-permute-start(bf16[128,1024]{1,0:T(8,128)(2,1)S(1)} %slice.13), channel_id=1, source_target_pairs={{0,48},{16,0},{32,16},{48,32},{1,49},{17,1},{33,17},{49,33},{2,50}... | collective-permute-start | bytes 786440 | tf_op jit(solution)/shard_map/ppermute | solution.py:174
  64.9 0.7 copy-start.6
  65.6 1.0 %copy-start.2 = (bf16[256,1024]{1,0:T(8,128)(2,1)S(1)}, bf16[256,1024]{1,0:T(8,128)(2,1)}, u32[]{:S(2)}) copy-start(bf16[256,1024]{1,0:T(8,128)(2,1)} %copy-done.1) | copy-start | bytes 1572868
  66.7 1.0 %copy-start.4 = (bf16[256,1024]{1,0:T(8,128)(2,1)S(1)}, bf16[256,1024]{1,0:T(8,128)(2,1)}, u32[]{:S(2)}) copy-start(bf16[256,1024]{1,0:T(8,128)(2,1)} %refs_0_) | copy-start | bytes 1572868
  67.7 0.9 copy-start.7
  74.4 10.8 %copy-start = (bf16[1,1024,1024]{2,1,0:T(8,128)(2,1)S(1)}, bf16[1,1024,1024]{2,1,0:T(8,128)(2,1)}, u32[]{:S(2)}) copy-start(bf16[1,1024,1024]{2,1,0:T(8,128)(2,1)} %param.6) | copy-start | bytes 6291460
  75.1 4.1 %collective-permute-start.4 = (bf16[128,1024]{1,0:T(8,128)(2,1)S(1)}, bf16[128,1024]{1,0:T(8,128)(2,1)S(1)}, u32[]{:S(2)}, u32[]{:S(2)}) collective-permute-start(bf16[128,1024]{1,0:T(8,128)(2,1)S(1)} %get-tuple-element.27), channel_id=1, source_target_pairs={{0,1},{1,0},{2,3},{3,2},{4,5},{5,4},{6,7},{7,6},{8,9},{9,8},{10,11... | collective-permute-start | bytes 786440 | tf_op jit(solution)/shard_map/ppermute | solution.py:174
  75.4 9.6 %collective-permute-start.5 = (bf16[64,8,128]{2,1,0:T(8,128)(2,1)}, bf16[64,8,128]{2,1,0:T(8,128)(2,1)S(1)}, u32[]{:S(2)}, u32[]{:S(2)}) collective-permute-start(bf16[64,8,128]{2,1,0:T(8,128)(2,1)} %get-tuple-element.29), channel_id=1, source_target_pairs={{0,16},{16,32},{32,48},{48,0},{1,17},{17,33},{33,49},{49,1},{2,18}... | collective-permute-start | bytes 393224 | tf_op jit(solution)/shard_map/ppermute | solution.py:174
  75.5 9.6 %collective-permute-start.6 = (bf16[64,8,128]{2,1,0:T(8,128)(2,1)S(1)}, bf16[64,8,128]{2,1,0:T(8,128)(2,1)S(1)}, u32[]{:S(2)}, u32[]{:S(2)}) collective-permute-start(bf16[64,8,128]{2,1,0:T(8,128)(2,1)S(1)} %get-tuple-element.30), channel_id=1, source_target_pairs={{0,32},{16,48},{32,0},{48,16},{1,33},{17,49},{33,1},{49,17},{2,34}... | collective-permute-start | bytes 393224 | tf_op jit(solution)/shard_map/ppermute | solution.py:174
  78.1 7.0 %collective-permute-start.7 = (bf16[64,8,128]{2,1,0:T(8,128)(2,1)S(1)}, bf16[64,8,128]{2,1,0:T(8,128)(2,1)S(1)}, u32[]{:S(2)}, u32[]{:S(2)}) collective-permute-start(bf16[64,8,128]{2,1,0:T(8,128)(2,1)S(1)} %get-tuple-element.31), channel_id=1, source_target_pairs={{0,48},{16,0},{32,16},{48,32},{1,49},{17,1},{33,17},{49,33},{2,50}... | collective-permute-start | bytes 393224 | tf_op jit(solution)/shard_map/ppermute | solution.py:174
  80.0 19.0 %all-to-all-start.2 = ((bf16[16,8,1024]{2,1,0:T(8,128)(2,1)}), bf16[16,8,1024]{2,1,0:T(8,128)(2,1)S(1)}, u32[]{:S(2)}, u32[]{:S(2)}) async-start(bf16[16,8,1024]{2,1,0:T(8,128)(2,1)} %fusion), calls=%async_computation.2 | async-start | bytes 524288 | tf_op jit(solution)/shard_map/all_to_all | solution.py:413
  86.6 7.5 %collective-permute-start.9 = (bf16[128,512]{1,0:T(8,128)(2,1)S(1)}, bf16[128,512]{1,0:T(8,128)(2,1)S(1)}, u32[]{:S(2)}, u32[]{:S(2)}) collective-permute-start(bf16[128,512]{1,0:T(8,128)(2,1)S(1)} %get-tuple-element.43), channel_id=1, source_target_pairs={{0,128},{128,0},{1,129},{129,1},{2,130},{130,2},{3,131},{131,3},{4... | collective-permute-start | bytes 393224 | tf_op jit(solution)/shard_map/ppermute | solution.py:174
  89.3 8.9 %collective-permute-start.8 = (bf16[128,512]{1,0:T(8,128)(2,1)S(1)}, bf16[128,512]{1,0:T(8,128)(2,1)S(1)}, u32[]{:S(2)}, u32[]{:S(2)}) collective-permute-start(bf16[128,512]{1,0:T(8,128)(2,1)S(1)} %get-tuple-element.42), channel_id=1, source_target_pairs={{0,128},{128,0},{1,129},{129,1},{2,130},{130,2},{3,131},{131,3},{4... | collective-permute-start | bytes 393224 | tf_op jit(solution)/shard_map/ppermute | solution.py:174

commit v5 on v4

--- a/solution.py
+++ b/solution.py
@@ -1,3 +1,4 @@
+import functools
 import math
 
 import jax
@@ -141,7 +142,7 @@
             out_ref[1, y, z, c, x] = (same - other).astype(BF16)
         return carry
 
-    lax.fori_loop(0, blocks // c_count, finish, 0, unroll=4)
+    lax.fori_loop(0, blocks // c_count, finish, 0, unroll=8)
 
 
 def filtered(signal, taps, sizes):
@@ -250,7 +251,7 @@
     )(order, *gathered)
 
 
-def weight_kernel(spread_ref, inputs_ref, own_ref, other_ref, left):
+def weight_kernel(scale, spread_ref, inputs_ref, own_ref, other_ref, left):
     x = spread_ref.shape[1]
     half = spread_ref.shape[0] // 2
     tiles = half // 2
@@ -279,17 +280,17 @@
                 return carry
 
             lax.fori_loop(0, tiles // 2, place, 0, unroll=4)
-    y = jnp.dot(left[...], inputs_ref[...], preferred_element_type=F32).astype(BF16)
+    y = (jnp.dot(left[...], inputs_ref[...], preferred_element_type=F32) * scale).astype(BF16)
     own_ref[...] = y[: tiles * 8, :]
     other_ref[...] = y[tiles * 8 :, :]
 
 
-def weight_part(spread, arranged):
+def weight_part(spread, arranged, scale):
     count = spread.shape[0]
     depth, width = arranged.shape
     rows = count * 4
     return pl.pallas_call(
-        weight_kernel,
+        functools.partial(weight_kernel, scale),
         out_shape=[jax.ShapeDtypeStruct((rows // 2, width), BF16)] * 2,
         in_specs=[VMEM, VMEM],
         out_specs=[VMEM, VMEM],
@@ -402,7 +403,8 @@
         for k in range(x)
     ]
 
-    own, other = weight_part(spread, arrange(order, gathered))
+    grad_scale = 1.0 / math.sqrt(tokens * groups)
+    own, other = weight_part(spread, arrange(order, gathered), grad_scale)
     other, *home = lax.optimization_barrier((other, *home))
     home = [home[0]] + [along(home[k], "x", x, k) for k in range(1, x)]
     other = along(other, "c", c, 1)
@@ -411,8 +413,7 @@
     mine, theirs = project(order, weights[0], home)
     arrived = jnp.concatenate([along(theirs[:half], "s", s, 1), along(theirs[half:], "s", s, 1)])
     pieces = lax.all_to_all(reduced, ("yl", "z"), split_axis=0, concat_axis=0, tiled=True)
-    grad_scale = 1.0 / math.sqrt(tokens * groups)
-    weight_grad = jnp.sum(pieces.astype(F32), 0) * grad_scale
+    weight_grad = jnp.sum(pieces.astype(F32), 0)
     input_grad = (mine.astype(F32) + arrived.astype(F32)).astype(BF16)
     return input_grad, weight_grad[None]
 

time: 100 us -> 99.9 us (level)
  no operation moved by 1% of the time
where the time goes in v5:
time: 99.9 us; the launch traced here: 99.4 us
  starting transfers between devices  42.6 us (43%)
  Pallas kernels  27.9 us (28%)
  waiting for transfers between devices  19.3 us (19%)
  local copies, waits for them, and re-layouts  6.5 us (7%)
  other arithmetic  2.24 us (2%)
    all_to_all x1, starting transfers between devices, body(): lax.all_to_all(send, ('yl', 'x', 'z', 'c'), split_axis=0, concat_axis=0,...  14.8 us
    pallas_call x1, Pallas kernels, filtered(): pl.pallas_call(filter_kernel, grid=(1,), out_shape=jax.ShapeDtypeStruct((...  14.7 us
    ppermute x10, waiting for transfers between devices, along(): lax.ppermute(array, axis, [(i, (i + offset) % size) for i in range(size)])  14.4 us
    ppermute x10, starting transfers between devices, along(): lax.ppermute(array, axis, [(i, (i + offset) % size) for i in range(size)])  13 us
    all_to_all x1, starting transfers between devices, body(): lax.all_to_all(result, ('s', 'yl', 'z', 'c'), split_axis=0, concat_axis=0...  9.72 us
    pallas_call x1, Pallas kernels, toeplitz(): pl.pallas_call(toeplitz_kernel, grid=(parts,), out_shape=jax.ShapeDtypeSt...  8.57 us
    unnamed x18, local copies, waits for them, and re-layouts  5.68 us
    all_to_all x1, starting transfers between devices, body(): lax.all_to_all(reduced, ('yl', 'z'), split_axis=0, concat_axis=0, tiled=T...  5.09 us
  transfers between devices with their start and end apart: 13, of which 5 were waited for; matrix products, arithmetic and copies ran while one was open for 2% of the time, Pallas kernels for 26%

profile of v5, /device:TPU:1, one launch (start us, length us, event | category | flops | bytes accessed | tf_op | source)
XLA Modules:
  0.0 99.4 jit_solution(12606189513388034434)
XLA Ops:
  0.7 0.0 copy-start.5
  0.7 1.0 %copy-done.5 = bf16[256,1024]{1,0:T(8,128)(2,1)S(1)} copy-done((bf16[256,1024]{1,0:T(8,128)(2,1)S(1)}, bf16[256,1024]{1,0:T(8,128)(2,1)}, u32[]{:S(2)}) %copy-start.5) | copy-done | bytes 524312
  1.8 1.3 %shard_map.59 = bf16[128,8,128]{2,1,0:T(8,128)(2,1)} custom-call(bf16[256,256]{1,0:T(8,128)(2,1)S(1)} %fusion.1.order_ref, bf16[256,1024]{1,0:T(8,128)(2,1)S(1)} %copy-done.5), custom_call_target="tpu_custom_call" | custom-call | tf_op jit(solution)/shard_map/pallas_call | solution.py:198
  3.1 14.8 %all-to-all-start = ((bf16[128,8,128]{2,1,0:T(8,128)(2,1)}), bf16[128,8,128]{2,1,0:T(8,128)(2,1)S(1)}, u32[]{:S(2)}, u32[]{:S(2)}) async-start(bf16[128,8,128]{2,1,0:T(8,128)(2,1)} %shard_map.59), calls=%async_computation | async-start | bytes 524288 | tf_op jit(solution)/shard_map/all_to_all | solution.py:385
  17.8 0.0 copy-start.8
  17.9 0.9 copy-done.8
  18.8 8.6 %shard_map.60.taps_ref = bf16[16384,512]{1,0:T(8,128)(2,1)} custom-call(f32[256,128]{1,0:T(8,128)S(1)} %bitcast.15), custom_call_target="tpu_custom_call" | custom-call | flops 33554432 | bytes 16777216 | tf_op jit(solution)/shard_map/pallas_call | solution.py:64
  27.3 0.0 copy-done.3
  27.3 1.4 %collective-permute-start = (bf16[256,1024]{1,0:T(8,128)(2,1)S(1)}, bf16[256,1024]{1,0:T(8,128)(2,1)S(1)}, u32[]{:S(2)}, u32[]{:S(2)}) collective-permute-start(bf16[256,1024]{1,0:T(8,128)(2,1)S(1)} %copy-done.3), channel_id=1, source_target_pairs={{0,16},{16,32},{32,48},{48,0},{1,17},{17,33},{33,49},{49,1},{2,18}... | collective-permute-start | bytes 1572872 | tf_op jit(solution)/shard_map/ppermute | solution.py:175
  28.7 1.4 %collective-permute-start.1 = (bf16[256,1024]{1,0:T(8,128)(2,1)S(1)}, bf16[256,1024]{1,0:T(8,128)(2,1)S(1)}, u32[]{:S(2)}, u32[]{:S(2)}) collective-permute-start(bf16[256,1024]{1,0:T(8,128)(2,1)S(1)} %copy-done.3), channel_id=1, source_target_pairs={{0,48},{16,0},{32,16},{48,32},{1,49},{17,1},{33,17},{49,33},{2,50}... | collective-permute-start | bytes 1572872 | tf_op jit(solution)/shard_map/ppermute | solution.py:175
  30.1 1.2 %all-to-all-done.signal_ref = bf16[128,8,128]{2,1,0:T(8,128)(2,1)S(1)} async-done(((bf16[128,8,128]{2,1,0:T(8,128)(2,1)}), bf16[128,8,128]{2,1,0:T(8,128)(2,1)S(1)}, u32[]{:S(2)}, u32[]{:S(2)}) %all-to-all-start) | async-done | bytes 262176 | tf_op jit(solution)/shard_map/all_to_all | solution.py:385
  31.3 14.7 %shard_map.61 = bf16[2,2,8,2,4,8,128]{6,5,4,3,2,1,0:T(8,128)(2,1)} custom-call(bf16[128,8,128]{2,1,0:T(8,128)(2,1)S(1)} %all-to-all-done.signal_ref, bf16[16384,512]{1,0:T(8,128)(2,1)} %shard_map.60.taps_ref), custom_call_target="tpu_custom_call" | custom-call | flops 34359738368 | bytes 16777216 | tf_op jit(solution)/shard_map/pallas_call | solution.py:152
  46.0 0.0 collective-permute-done.refs_1_
  46.0 0.0 collective-permute-done.1.refs_4_
  46.0 0.0 copy-start.1
  46.0 9.7 %all-to-all-start.1 = ((bf16[64,4,8,128]{3,2,1,0:T(8,128)(2,1)}), bf16[64,4,8,128]{3,2,1,0:T(8,128)(2,1)S(1)}, u32[]{:S(2)}, u32[]{:S(2)}) async-start(bf16[64,4,8,128]{3,2,1,0:T(8,128)(2,1)} %bitcast.2), calls=%async_computation.1 | async-start | bytes 1048576 | tf_op jit(solution)/shard_map/all_to_all | solution.py:400
  55.8 0.3 collective-permute-start.2
  56.2 2.7 %collective-permute-start.3 = (bf16[128,1024]{1,0:T(8,128)(2,1)S(1)}, bf16[128,1024]{1,0:T(8,128)(2,1)S(1)}, u32[]{:S(2)}, u32[]{:S(2)}) collective-permute-start(bf16[128,1024]{1,0:T(8,128)(2,1)S(1)} %slice.13), channel_id=1, source_target_pairs={{0,48},{16,0},{32,16},{48,32},{1,49},{17,1},{33,17},{49,33},{2,50}... | collective-permute-start | bytes 786440 | tf_op jit(solution)/shard_map/ppermute | solution.py:175
  58.8 5.9 %collective-permute-done.2.refs_2_ = bf16[128,1024]{1,0:T(8,128)(2,1)S(1)} collective-permute-done((bf16[128,1024]{1,0:T(8,128)(2,1)S(1)}, bf16[128,1024]{1,0:T(8,128)(2,1)S(1)}, u32[]{:S(2)}, u32[]{:S(2)}) %collective-permute-start.2) | collective-permute-done | bytes 262176 | tf_op jit(solution)/shard_map/ppermute | solution.py:175
  64.7 0.0 copy-done.1
  64.7 0.0 collective-permute-done.3.refs_3_
  64.7 0.7 copy-done.6
  65.4 1.0 %copy-done.2 = bf16[256,1024]{1,0:T(8,128)(2,1)S(1)} copy-done((bf16[256,1024]{1,0:T(8,128)(2,1)S(1)}, bf16[256,1024]{1,0:T(8,128)(2,1)}, u32[]{:S(2)}) %copy-start.2) | copy-done | bytes 524312
  66.4 1.0 %copy-done.4 = bf16[256,1024]{1,0:T(8,128)(2,1)S(1)} copy-done((bf16[256,1024]{1,0:T(8,128)(2,1)S(1)}, bf16[256,1024]{1,0:T(8,128)(2,1)}, u32[]{:S(2)}) %copy-start.4) | copy-done | bytes 524312
  67.5 0.9 copy-done.7
  68.4 0.9 shard_map.62.inputs_ref
  69.4 3.7 %all-to-all-done.1.spread_ref = bf16[64,4,8,128]{3,2,1,0:T(8,128)(2,1)S(1)} async-done(((bf16[64,4,8,128]{3,2,1,0:T(8,128)(2,1)}), bf16[64,4,8,128]{3,2,1,0:T(8,128)(2,1)S(1)}, u32[]{:S(2)}, u32[]{:S(2)}) %all-to-all-start.1) | async-done | bytes 524320 | tf_op jit(solution)/shard_map/all_to_all | solution.py:400
  73.1 1.0 %shard_map.63 = (bf16[128,1024]{1,0:T(8,128)(2,1)S(1)}, bf16[128,1024]{1,0:T(8,128)(2,1)S(1)}) custom-call(bf16[64,4,8,128]{3,2,1,0:T(8,128)(2,1)S(1)} %all-to-all-done.1.spread_ref, bf16[1024,1024]{1,0:T(8,128)(2,1)S(1)} %shard_map.62.inputs_ref), custom_call_target="tpu_custom_call" | custom-call | flops 536870912 | bytes 4194304 | tf_op jit(solution)/shard_map/pallas_call | solution.py:292
  74.1 0.0 copy-start
  74.2 0.8 dynamic-slice_bitcast_fusion
  74.9 0.3 collective-permute-start.4
  75.2 0.1 collective-permute-start.5
  75.3 2.6 %collective-permute-start.6 = (bf16[64,8,128]{2,1,0:T(8,128)(2,1)S(1)}, bf16[64,8,128]{2,1,0:T(8,128)(2,1)S(1)}, u32[]{:S(2)}, u32[]{:S(2)}) collective-permute-start(bf16[64,8,128]{2,1,0:T(8,128)(2,1)S(1)} %get-tuple-element.30), channel_id=1, source_target_pairs={{0,32},{16,48},{32,0},{48,16},{1,33},{17,49},{33,1},{49,17},{2,34}... | collective-permute-start | bytes 393224 | tf_op jit(solution)/shard_map/ppermute | solution.py:175
  77.9 1.1 %collective-permute-start.7 = (bf16[64,8,128]{2,1,0:T(8,128)(2,1)S(1)}, bf16[64,8,128]{2,1,0:T(8,128)(2,1)S(1)}, u32[]{:S(2)}, u32[]{:S(2)}) collective-permute-start(bf16[64,8,128]{2,1,0:T(8,128)(2,1)S(1)} %get-tuple-element.31), channel_id=1, source_target_pairs={{0,48},{16,0},{32,16},{48,32},{1,49},{17,1},{33,17},{49,33},{2,50}... | collective-permute-start | bytes 393224 | tf_op jit(solution)/shard_map/ppermute | solution.py:175
  79.0 0.0 collective-permute-done.4
  79.0 0.8 fusion
  79.8 5.1 %all-to-all-start.2 = ((bf16[16,8,1024]{2,1,0:T(8,128)(2,1)}), bf16[16,8,1024]{2,1,0:T(8,128)(2,1)S(1)}, u32[]{:S(2)}, u32[]{:S(2)}) async-start(bf16[16,8,1024]{2,1,0:T(8,128)(2,1)} %fusion), calls=%async_computation.2 | async-start | bytes 524288 | tf_op jit(solution)/shard_map/all_to_all | solution.py:415
  84.9 0.0 collective-permute-done.5.refs_1_
  84.9 0.0 collective-permute-done.6.refs_2_
  84.9 0.0 collective-permute-done.7.refs_3_
  84.9 1.4 %shard_map.64 = (bf16[256,512]{1,0:T(8,128)(2,1)S(1)}, bf16[256,512]{1,0:T(8,128)(2,1)S(1)}) custom-call(bf16[256,256]{1,0:T(8,128)(2,1)S(1)} %fusion.1.order_ref, bf16[1024,1024]{1,0:T(8,128)(2,1)S(1)} %bitcast.14, bf16[64,8,128]{2,1,0:T(8,128)(2,1)S(1)} %get-tuple-element.32.refs_0_, bf16[64,8,128]{2,1,0:T(8,128)(2,1)S(1)} %collective-permute-done.5.refs_1_, ...), custom_call_target="tpu_custom_call" | custom-call | flops 536870912 | bytes 4194304 | tf_op jit(solution)/shard_map/pallas_call | solution.py:355
  86.4 2.7 %collective-permute-start.9 = (bf16[128,512]{1,0:T(8,128)(2,1)S(1)}, bf16[128,512]{1,0:T(8,128)(2,1)S(1)}, u32[]{:S(2)}, u32[]{:S(2)}) collective-permute-start(bf16[128,512]{1,0:T(8,128)(2,1)S(1)} %get-tuple-element.43), channel_id=1, source_target_pairs={{0,128},{128,0},{1,129},{129,1},{2,130},{130,2},{3,131},{131,3},{4... | collective-permute-start | bytes 393224 | tf_op jit(solution)/shard_map/ppermute | solution.py:175
  89.1 0.4 collective-permute-start.8
  89.4 4.5 %collective-permute-done.9 = bf16[128,512]{1,0:T(8,128)(2,1)S(1)} collective-permute-done((bf16[128,512]{1,0:T(8,128)(2,1)S(1)}, bf16[128,512]{1,0:T(8,128)(2,1)S(1)}, u32[]{:S(2)}, u32[]{:S(2)}) %collective-permute-start.9) | collective-permute-done | bytes 131104 | tf_op jit(solution)/shard_map/ppermute | solution.py:175
  93.9 4.0 %collective-permute-done.8 = bf16[128,512]{1,0:T(8,128)(2,1)S(1)} collective-permute-done((bf16[128,512]{1,0:T(8,128)(2,1)S(1)}, bf16[128,512]{1,0:T(8,128)(2,1)S(1)}, u32[]{:S(2)}, u32[]{:S(2)}) %collective-permute-start.8) | collective-permute-done | bytes 131104 | tf_op jit(solution)/shard_map/ppermute | solution.py:175
  97.9 0.8 add_convert_fusion
  98.7 0.0 all-to-all-done.2
  98.7 0.7 convert_reduce_fusion
  (13 shorter events, 0.1 us)
Async XLA Ops:
  0.7 1.0 %copy-start.5 = (bf16[256,1024]{1,0:T(8,128)(2,1)S(1)}, bf16[256,1024]{1,0:T(8,128)(2,1)}, u32[]{:S(2)}) copy-start(bf16[256,1024]{1,0:T(8,128)(2,1)} %cotangent_ref.1) | copy-start | bytes 1572868
  3.1 28.3 %all-to-all-start = ((bf16[128,8,128]{2,1,0:T(8,128)(2,1)}), bf16[128,8,128]{2,1,0:T(8,128)(2,1)S(1)}, u32[]{:S(2)}, u32[]{:S(2)}) async-start(bf16[128,8,128]{2,1,0:T(8,128)(2,1)} %shard_map.59), calls=%async_computation | async-start | bytes 524288 | tf_op jit(solution)/shard_map/all_to_all | solution.py:385
  17.8 0.9 copy-start.8
  18.8 8.6 %copy-start.3 = (bf16[256,1024]{1,0:T(8,128)(2,1)S(1)}, bf16[256,1024]{1,0:T(8,128)(2,1)}, u32[]{:S(2)}) copy-start(bf16[256,1024]{1,0:T(8,128)(2,1)} %refs_0_) | copy-start | bytes 1572868
  27.3 18.7 %collective-permute-start = (bf16[256,1024]{1,0:T(8,128)(2,1)S(1)}, bf16[256,1024]{1,0:T(8,128)(2,1)S(1)}, u32[]{:S(2)}, u32[]{:S(2)}) collective-permute-start(bf16[256,1024]{1,0:T(8,128)(2,1)S(1)} %copy-done.3), channel_id=1, source_target_pairs={{0,16},{16,32},{32,48},{48,0},{1,17},{17,33},{33,49},{49,1},{2,18}... | collective-permute-start | bytes 1572872 | tf_op jit(solution)/shard_map/ppermute | solution.py:175
  28.7 17.3 %collective-permute-start.1 = (bf16[256,1024]{1,0:T(8,128)(2,1)S(1)}, bf16[256,1024]{1,0:T(8,128)(2,1)S(1)}, u32[]{:S(2)}, u32[]{:S(2)}) collective-permute-start(bf16[256,1024]{1,0:T(8,128)(2,1)S(1)} %copy-done.3), channel_id=1, source_target_pairs={{0,48},{16,0},{32,16},{48,32},{1,49},{17,1},{33,17},{49,33},{2,50}... | collective-permute-start | bytes 1572872 | tf_op jit(solution)/shard_map/ppermute | solution.py:175
  46.0 18.7 %copy-start.1 = (bf16[256,1024]{1,0:T(8,128)(2,1)}, bf16[256,1024]{1,0:T(8,128)(2,1)S(1)}, u32[]{:S(2)}) copy-start(bf16[256,1024]{1,0:T(8,128)(2,1)S(1)} %collective-permute-done.1.refs_4_) | copy-start | bytes 1572868
  46.0 27.1 %all-to-all-start.1 = ((bf16[64,4,8,128]{3,2,1,0:T(8,128)(2,1)}), bf16[64,4,8,128]{3,2,1,0:T(8,128)(2,1)S(1)}, u32[]{:S(2)}, u32[]{:S(2)}) async-start(bf16[64,4,8,128]{3,2,1,0:T(8,128)(2,1)} %bitcast.2), calls=%async_computation.1 | async-start | bytes 1048576 | tf_op jit(solution)/shard_map/all_to_all | solution.py:400
  55.8 8.9 %collective-permute-start.2 = (bf16[128,1024]{1,0:T(8,128)(2,1)S(1)}, bf16[128,1024]{1,0:T(8,128)(2,1)S(1)}, u32[]{:S(2)}, u32[]{:S(2)}) collective-permute-start(bf16[128,1024]{1,0:T(8,128)(2,1)S(1)} %slice.12), channel_id=1, source_target_pairs={{0,16},{16,32},{32,48},{48,0},{1,17},{17,33},{33,49},{49,1},{2,18}... | collective-permute-start | bytes 786440 | tf_op jit(solution)/shard_map/ppermute | solution.py:175
  56.2 8.5 %collective-permute-start.3 = (bf16[128,1024]{1,0:T(8,128)(2,1)S(1)}, bf16[128,1024]{1,0:T(8,128)(2,1)S(1)}, u32[]{:S(2)}, u32[]{:S(2)}) collective-permute-start(bf16[128,1024]{1,0:T(8,128)(2,1)S(1)} %slice.13), channel_id=1, source_target_pairs={{0,48},{16,0},{32,16},{48,32},{1,49},{17,1},{33,17},{49,33},{2,50}... | collective-permute-start | bytes 786440 | tf_op jit(solution)/shard_map/ppermute | solution.py:175
  64.7 0.7 copy-start.6
  65.4 1.0 %copy-start.2 = (bf16[256,1024]{1,0:T(8,128)(2,1)S(1)}, bf16[256,1024]{1,0:T(8,128)(2,1)}, u32[]{:S(2)}) copy-start(bf16[256,1024]{1,0:T(8,128)(2,1)} %copy-done.1) | copy-start | bytes 1572868
  66.4 1.0 %copy-start.4 = (bf16[256,1024]{1,0:T(8,128)(2,1)S(1)}, bf16[256,1024]{1,0:T(8,128)(2,1)}, u32[]{:S(2)}) copy-start(bf16[256,1024]{1,0:T(8,128)(2,1)} %refs_0_) | copy-start | bytes 1572868
  67.5 0.9 copy-start.7
  74.1 10.8 %copy-start = (bf16[1,1024,1024]{2,1,0:T(8,128)(2,1)S(1)}, bf16[1,1024,1024]{2,1,0:T(8,128)(2,1)}, u32[]{:S(2)}) copy-start(bf16[1,1024,1024]{2,1,0:T(8,128)(2,1)} %param.6) | copy-start | bytes 6291460
  74.9 4.1 %collective-permute-start.4 = (bf16[128,1024]{1,0:T(8,128)(2,1)S(1)}, bf16[128,1024]{1,0:T(8,128)(2,1)S(1)}, u32[]{:S(2)}, u32[]{:S(2)}) collective-permute-start(bf16[128,1024]{1,0:T(8,128)(2,1)S(1)} %get-tuple-element.27), channel_id=1, source_target_pairs={{0,1},{1,0},{2,3},{3,2},{4,5},{5,4},{6,7},{7,6},{8,9},{9,8},{10,11... | collective-permute-start | bytes 786440 | tf_op jit(solution)/shard_map/ppermute | solution.py:175
  75.2 9.6 %collective-permute-start.5 = (bf16[64,8,128]{2,1,0:T(8,128)(2,1)}, bf16[64,8,128]{2,1,0:T(8,128)(2,1)S(1)}, u32[]{:S(2)}, u32[]{:S(2)}) collective-permute-start(bf16[64,8,128]{2,1,0:T(8,128)(2,1)} %get-tuple-element.29), channel_id=1, source_target_pairs={{0,16},{16,32},{32,48},{48,0},{1,17},{17,33},{33,49},{49,1},{2,18}... | collective-permute-start | bytes 393224 | tf_op jit(solution)/shard_map/ppermute | solution.py:175
  75.3 9.6 %collective-permute-start.6 = (bf16[64,8,128]{2,1,0:T(8,128)(2,1)S(1)}, bf16[64,8,128]{2,1,0:T(8,128)(2,1)S(1)}, u32[]{:S(2)}, u32[]{:S(2)}) collective-permute-start(bf16[64,8,128]{2,1,0:T(8,128)(2,1)S(1)} %get-tuple-element.30), channel_id=1, source_target_pairs={{0,32},{16,48},{32,0},{48,16},{1,33},{17,49},{33,1},{49,17},{2,34}... | collective-permute-start | bytes 393224 | tf_op jit(solution)/shard_map/ppermute | solution.py:175
  77.9 7.0 %collective-permute-start.7 = (bf16[64,8,128]{2,1,0:T(8,128)(2,1)S(1)}, bf16[64,8,128]{2,1,0:T(8,128)(2,1)S(1)}, u32[]{:S(2)}, u32[]{:S(2)}) collective-permute-start(bf16[64,8,128]{2,1,0:T(8,128)(2,1)S(1)} %get-tuple-element.31), channel_id=1, source_target_pairs={{0,48},{16,0},{32,16},{48,32},{1,49},{17,1},{33,17},{49,33},{2,50}... | collective-permute-start | bytes 393224 | tf_op jit(solution)/shard_map/ppermute | solution.py:175
  79.8 18.9 %all-to-all-start.2 = ((bf16[16,8,1024]{2,1,0:T(8,128)(2,1)}), bf16[16,8,1024]{2,1,0:T(8,128)(2,1)S(1)}, u32[]{:S(2)}, u32[]{:S(2)}) async-start(bf16[16,8,1024]{2,1,0:T(8,128)(2,1)} %fusion), calls=%async_computation.2 | async-start | bytes 524288 | tf_op jit(solution)/shard_map/all_to_all | solution.py:415
  86.4 7.5 %collective-permute-start.9 = (bf16[128,512]{1,0:T(8,128)(2,1)S(1)}, bf16[128,512]{1,0:T(8,128)(2,1)S(1)}, u32[]{:S(2)}, u32[]{:S(2)}) collective-permute-start(bf16[128,512]{1,0:T(8,128)(2,1)S(1)} %get-tuple-element.43), channel_id=1, source_target_pairs={{0,128},{128,0},{1,129},{129,1},{2,130},{130,2},{3,131},{131,3},{4... | collective-permute-start | bytes 393224 | tf_op jit(solution)/shard_map/ppermute | solution.py:175
  89.1 8.9 %collective-permute-start.8 = (bf16[128,512]{1,0:T(8,128)(2,1)S(1)}, bf16[128,512]{1,0:T(8,128)(2,1)S(1)}, u32[]{:S(2)}, u32[]{:S(2)}) collective-permute-start(bf16[128,512]{1,0:T(8,128)(2,1)S(1)} %get-tuple-element.42), channel_id=1, source_target_pairs={{0,128},{128,0},{1,129},{129,1},{2,130},{130,2},{3,131},{131,3},{4... | collective-permute-start | bytes 393224 | tf_op jit(solution)/shard_map/ppermute | solution.py:175

commit v6 on v5

--- a/solution.py
+++ b/solution.py
@@ -213,22 +213,23 @@
 
 
 def arrange_kernel(order_ref, *refs):
-    *gathered, out_ref, held, arrived = refs
+    *gathered, out_ref = refs
     tokens = order_ref.shape[0]
-    copies, row = [], 0
-    for n, ref in enumerate(gathered):
-        copies.append(
-            pltpu.make_async_copy(ref, held.at[row : row + ref.shape[0], :], arrived.at[n])
-        )
-        row += ref.shape[0]
-        copies[n].start()
-    for copy in copies:
-        copy.wait()
-    for k in range(row // tokens):
-        part = slice(k * tokens, (k + 1) * tokens)
-        out_ref[part, :] = lax.dot_general(
-            order_ref[...], held[part, :], (((0,), (0,)), ((), ())), preferred_element_type=F32
-        ).astype(BF16)
+    row = 0
+    while gathered:
+        total, taken = 0, 0
+        while taken < tokens:
+            piece = gathered.pop(0)
+            count = piece.shape[0]
+            total = total + lax.dot_general(
+                order_ref[taken : taken + count, :],
+                piece[...],
+                (((0,), (0,)), ((), ())),
+                preferred_element_type=F32,
+            )
+            taken += count
+        out_ref[row : row + tokens, :] = total.astype(BF16)
+        row += tokens
 
 
 def arrange(order, gathered):
@@ -236,12 +237,8 @@
     return pl.pallas_call(
         arrange_kernel,
         out_shape=jax.ShapeDtypeStruct((rows, width), BF16),
-        in_specs=[VMEM] + [ANY] * len(gathered),
+        in_specs=[VMEM] * (1 + len(gathered)),
         out_specs=VMEM,
-        scratch_shapes=[
-            pltpu.VMEM((rows, width), BF16),
-            pltpu.SemaphoreType.DMA((len(gathered),)),
-        ],
         compiler_params=pltpu.CompilerParams(vmem_limit_bytes=24 << 20),
         cost_estimate=pl.CostEstimate(
             flops=2 * rows * order.shape[0] * width,

time: 99.9 us -> 99.8 us (level)
  no operation moved by 1% of the time
where the time goes in v6:
time: 99.8 us; the launch traced here: 99.2 us
  starting transfers between devices  42.5 us (43%)
  Pallas kernels  27.9 us (28%)
  waiting for transfers between devices  19.3 us (19%)
  local copies, waits for them, and re-layouts  6.5 us (7%)
  other arithmetic  2.24 us (2%)
    all_to_all x1, starting transfers between devices, body(): lax.all_to_all(send, ('yl', 'x', 'z', 'c'), split_axis=0, concat_axis=0,...  14.8 us
    pallas_call x1, Pallas kernels, filtered(): pl.pallas_call(filter_kernel, grid=(1,), out_shape=jax.ShapeDtypeStruct((...  14.7 us
    ppermute x10, waiting for transfers between devices, along(): lax.ppermute(array, axis, [(i, (i + offset) % size) for i in range(size)])  14.3 us
    ppermute x10, starting transfers between devices, along(): lax.ppermute(array, axis, [(i, (i + offset) % size) for i in range(size)])  13 us
    all_to_all x1, starting transfers between devices, body(): lax.all_to_all(result, ('s', 'yl', 'z', 'c'), split_axis=0, concat_axis=0...  9.72 us
    pallas_call x1, Pallas kernels, toeplitz(): pl.pallas_call(toeplitz_kernel, grid=(parts,), out_shape=jax.ShapeDtypeSt...  8.57 us
    unnamed x18, local copies, waits for them, and re-layouts  5.68 us
    all_to_all x1, starting transfers between devices, body(): lax.all_to_all(reduced, ('yl', 'z'), split_axis=0, concat_axis=0, tiled=T...  5.02 us
  transfers between devices with their start and end apart: 13, of which 5 were waited for; matrix products, arithmetic and copies ran while one was open for 2% of the time, Pallas kernels for 26%

profile of v6, /device:TPU:1, one launch (start us, length us, event | category | flops | bytes accessed | tf_op | source)
XLA Modules:
  0.0 99.2 jit_solution(11875315569346722724)
XLA Ops:
  0.7 0.0 copy-start.5
  0.7 1.0 %copy-done.5 = bf16[256,1024]{1,0:T(8,128)(2,1)S(1)} copy-done((bf16[256,1024]{1,0:T(8,128)(2,1)S(1)}, bf16[256,1024]{1,0:T(8,128)(2,1)}, u32[]{:S(2)}) %copy-start.5) | copy-done | bytes 524312
  1.8 1.3 %shard_map.59 = bf16[128,8,128]{2,1,0:T(8,128)(2,1)} custom-call(bf16[256,256]{1,0:T(8,128)(2,1)S(1)} %fusion.1.order_ref, bf16[256,1024]{1,0:T(8,128)(2,1)S(1)} %copy-done.5), custom_call_target="tpu_custom_call" | custom-call | tf_op jit(solution)/shard_map/pallas_call | solution.py:198
  3.1 14.8 %all-to-all-start = ((bf16[128,8,128]{2,1,0:T(8,128)(2,1)}), bf16[128,8,128]{2,1,0:T(8,128)(2,1)S(1)}, u32[]{:S(2)}, u32[]{:S(2)}) async-start(bf16[128,8,128]{2,1,0:T(8,128)(2,1)} %shard_map.59), calls=%async_computation | async-start | bytes 524288 | tf_op jit(solution)/shard_map/all_to_all | solution.py:382
  17.8 0.0 copy-start.8
  17.9 0.9 copy-done.8
  18.8 8.6 %shard_map.60.taps_ref = bf16[16384,512]{1,0:T(8,128)(2,1)} custom-call(f32[256,128]{1,0:T(8,128)S(1)} %bitcast.15), custom_call_target="tpu_custom_call" | custom-call | flops 33554432 | bytes 16777216 | tf_op jit(solution)/shard_map/pallas_call | solution.py:64
  27.3 0.0 copy-done.3
  27.3 1.4 %collective-permute-start = (bf16[256,1024]{1,0:T(8,128)(2,1)S(1)}, bf16[256,1024]{1,0:T(8,128)(2,1)S(1)}, u32[]{:S(2)}, u32[]{:S(2)}) collective-permute-start(bf16[256,1024]{1,0:T(8,128)(2,1)S(1)} %copy-done.3), channel_id=1, source_target_pairs={{0,16},{16,32},{32,48},{48,0},{1,17},{17,33},{33,49},{49,1},{2,18}... | collective-permute-start | bytes 1572872 | tf_op jit(solution)/shard_map/ppermute | solution.py:175
  28.7 1.4 %collective-permute-start.1 = (bf16[256,1024]{1,0:T(8,128)(2,1)S(1)}, bf16[256,1024]{1,0:T(8,128)(2,1)S(1)}, u32[]{:S(2)}, u32[]{:S(2)}) collective-permute-start(bf16[256,1024]{1,0:T(8,128)(2,1)S(1)} %copy-done.3), channel_id=1, source_target_pairs={{0,48},{16,0},{32,16},{48,32},{1,49},{17,1},{33,17},{49,33},{2,50}... | collective-permute-start | bytes 1572872 | tf_op jit(solution)/shard_map/ppermute | solution.py:175
  30.1 1.2 %all-to-all-done.signal_ref = bf16[128,8,128]{2,1,0:T(8,128)(2,1)S(1)} async-done(((bf16[128,8,128]{2,1,0:T(8,128)(2,1)}), bf16[128,8,128]{2,1,0:T(8,128)(2,1)S(1)}, u32[]{:S(2)}, u32[]{:S(2)}) %all-to-all-start) | async-done | bytes 262176 | tf_op jit(solution)/shard_map/all_to_all | solution.py:382
  31.3 14.7 %shard_map.61 = bf16[2,2,8,2,4,8,128]{6,5,4,3,2,1,0:T(8,128)(2,1)} custom-call(bf16[128,8,128]{2,1,0:T(8,128)(2,1)S(1)} %all-to-all-done.signal_ref, bf16[16384,512]{1,0:T(8,128)(2,1)} %shard_map.60.taps_ref), custom_call_target="tpu_custom_call" | custom-call | flops 34359738368 | bytes 16777216 | tf_op jit(solution)/shard_map/pallas_call | solution.py:152
  46.0 0.0 collective-permute-done.refs_1_
  46.0 0.0 collective-permute-done.1.refs_4_
  46.0 0.0 copy-start.1
  46.0 9.7 %all-to-all-start.1 = ((bf16[64,4,8,128]{3,2,1,0:T(8,128)(2,1)}), bf16[64,4,8,128]{3,2,1,0:T(8,128)(2,1)S(1)}, u32[]{:S(2)}, u32[]{:S(2)}) async-start(bf16[64,4,8,128]{3,2,1,0:T(8,128)(2,1)} %bitcast.2), calls=%async_computation.1 | async-start | bytes 1048576 | tf_op jit(solution)/shard_map/all_to_all | solution.py:397
  55.8 0.3 collective-permute-start.2
  56.2 2.7 %collective-permute-start.3 = (bf16[128,1024]{1,0:T(8,128)(2,1)S(1)}, bf16[128,1024]{1,0:T(8,128)(2,1)S(1)}, u32[]{:S(2)}, u32[]{:S(2)}) collective-permute-start(bf16[128,1024]{1,0:T(8,128)(2,1)S(1)} %slice.13), channel_id=1, source_target_pairs={{0,48},{16,0},{32,16},{48,32},{1,49},{17,1},{33,17},{49,33},{2,50}... | collective-permute-start | bytes 786440 | tf_op jit(solution)/shard_map/ppermute | solution.py:175
  58.8 5.9 %collective-permute-done.2.refs_2_ = bf16[128,1024]{1,0:T(8,128)(2,1)S(1)} collective-permute-done((bf16[128,1024]{1,0:T(8,128)(2,1)S(1)}, bf16[128,1024]{1,0:T(8,128)(2,1)S(1)}, u32[]{:S(2)}, u32[]{:S(2)}) %collective-permute-start.2) | collective-permute-done | bytes 262176 | tf_op jit(solution)/shard_map/ppermute | solution.py:175
  64.7 0.0 collective-permute-done.3.refs_3_
  64.7 0.7 copy-done.6
  65.4 1.0 %copy-done.2 = bf16[256,1024]{1,0:T(8,128)(2,1)S(1)} copy-done((bf16[256,1024]{1,0:T(8,128)(2,1)S(1)}, bf16[256,1024]{1,0:T(8,128)(2,1)}, u32[]{:S(2)}) %copy-start.2) | copy-done | bytes 524312
  66.4 1.0 %copy-done.4 = bf16[256,1024]{1,0:T(8,128)(2,1)S(1)} copy-done((bf16[256,1024]{1,0:T(8,128)(2,1)S(1)}, bf16[256,1024]{1,0:T(8,128)(2,1)}, u32[]{:S(2)}) %copy-start.4) | copy-done | bytes 524312
  67.5 0.9 copy-done.7
  68.4 0.9 shard_map.62.inputs_ref
  69.3 3.8 %all-to-all-done.1.spread_ref = bf16[64,4,8,128]{3,2,1,0:T(8,128)(2,1)S(1)} async-done(((bf16[64,4,8,128]{3,2,1,0:T(8,128)(2,1)}), bf16[64,4,8,128]{3,2,1,0:T(8,128)(2,1)S(1)}, u32[]{:S(2)}, u32[]{:S(2)}) %all-to-all-start.1) | async-done | bytes 524320 | tf_op jit(solution)/shard_map/all_to_all | solution.py:397
  73.1 1.0 %shard_map.63 = (bf16[128,1024]{1,0:T(8,128)(2,1)S(1)}, bf16[128,1024]{1,0:T(8,128)(2,1)S(1)}) custom-call(bf16[64,4,8,128]{3,2,1,0:T(8,128)(2,1)S(1)} %all-to-all-done.1.spread_ref, bf16[1024,1024]{1,0:T(8,128)(2,1)S(1)} %shard_map.62.inputs_ref), custom_call_target="tpu_custom_call" | custom-call | flops 536870912 | bytes 4194304 | tf_op jit(solution)/shard_map/pallas_call | solution.py:289
  74.1 0.0 copy-start
  74.2 0.8 dynamic-slice_bitcast_fusion
  74.9 0.3 collective-permute-start.4
  75.2 0.1 collective-permute-start.5
  75.3 2.6 %collective-permute-start.6 = (bf16[64,8,128]{2,1,0:T(8,128)(2,1)S(1)}, bf16[64,8,128]{2,1,0:T(8,128)(2,1)S(1)}, u32[]{:S(2)}, u32[]{:S(2)}) collective-permute-start(bf16[64,8,128]{2,1,0:T(8,128)(2,1)S(1)} %get-tuple-element.30), channel_id=1, source_target_pairs={{0,32},{16,48},{32,0},{48,16},{1,33},{17,49},{33,1},{49,17},{2,34}... | collective-permute-start | bytes 393224 | tf_op jit(solution)/shard_map/ppermute | solution.py:175
  77.9 1.1 %collective-permute-start.7 = (bf16[64,8,128]{2,1,0:T(8,128)(2,1)S(1)}, bf16[64,8,128]{2,1,0:T(8,128)(2,1)S(1)}, u32[]{:S(2)}, u32[]{:S(2)}) collective-permute-start(bf16[64,8,128]{2,1,0:T(8,128)(2,1)S(1)} %get-tuple-element.31), channel_id=1, source_target_pairs={{0,48},{16,0},{32,16},{48,32},{1,49},{17,1},{33,17},{49,33},{2,50}... | collective-permute-start | bytes 393224 | tf_op jit(solution)/shard_map/ppermute | solution.py:175
  79.0 0.0 collective-permute-done.4
  79.0 0.8 fusion
  79.8 5.0 %all-to-all-start.2 = ((bf16[16,8,1024]{2,1,0:T(8,128)(2,1)}), bf16[16,8,1024]{2,1,0:T(8,128)(2,1)S(1)}, u32[]{:S(2)}, u32[]{:S(2)}) async-start(bf16[16,8,1024]{2,1,0:T(8,128)(2,1)} %fusion), calls=%async_computation.2 | async-start | bytes 524288 | tf_op jit(solution)/shard_map/all_to_all | solution.py:412
  84.8 0.0 collective-permute-done.5.refs_1_
  84.8 0.0 collective-permute-done.6.refs_2_
  84.8 0.0 collective-permute-done.7.refs_3_
  84.8 0.0 copy-done
  84.8 1.4 %shard_map.64 = (bf16[256,512]{1,0:T(8,128)(2,1)S(1)}, bf16[256,512]{1,0:T(8,128)(2,1)S(1)}) custom-call(bf16[256,256]{1,0:T(8,128)(2,1)S(1)} %fusion.1.order_ref, bf16[1024,1024]{1,0:T(8,128)(2,1)S(1)} %bitcast.14, bf16[64,8,128]{2,1,0:T(8,128)(2,1)S(1)} %get-tuple-element.32.refs_0_, bf16[64,8,128]{2,1,0:T(8,128)(2,1)S(1)} %collective-permute-done.5.refs_1_, ...), custom_call_target="tpu_custom_call" | custom-call | flops 536870912 | bytes 4194304 | tf_op jit(solution)/shard_map/pallas_call | solution.py:352
  86.3 2.7 %collective-permute-start.9 = (bf16[128,512]{1,0:T(8,128)(2,1)S(1)}, bf16[128,512]{1,0:T(8,128)(2,1)S(1)}, u32[]{:S(2)}, u32[]{:S(2)}) collective-permute-start(bf16[128,512]{1,0:T(8,128)(2,1)S(1)} %get-tuple-element.43), channel_id=1, source_target_pairs={{0,128},{128,0},{1,129},{129,1},{2,130},{130,2},{3,131},{131,3},{4... | collective-permute-start | bytes 393224 | tf_op jit(solution)/shard_map/ppermute | solution.py:175
  89.0 0.4 collective-permute-start.8
  89.4 4.4 %collective-permute-done.9 = bf16[128,512]{1,0:T(8,128)(2,1)S(1)} collective-permute-done((bf16[128,512]{1,0:T(8,128)(2,1)S(1)}, bf16[128,512]{1,0:T(8,128)(2,1)S(1)}, u32[]{:S(2)}, u32[]{:S(2)}) %collective-permute-start.9) | collective-permute-done | bytes 131104 | tf_op jit(solution)/shard_map/ppermute | solution.py:175
  93.8 4.0 %collective-permute-done.8 = bf16[128,512]{1,0:T(8,128)(2,1)S(1)} collective-permute-done((bf16[128,512]{1,0:T(8,128)(2,1)S(1)}, bf16[128,512]{1,0:T(8,128)(2,1)S(1)}, u32[]{:S(2)}, u32[]{:S(2)}) %collective-permute-start.8) | collective-permute-done | bytes 131104 | tf_op jit(solution)/shard_map/ppermute | solution.py:175
  97.8 0.8 add_convert_fusion
  98.6 0.0 all-to-all-done.2
  98.6 0.7 convert_reduce_fusion
  (13 shorter events, 0.1 us)
Async XLA Ops:
  0.7 1.0 %copy-start.5 = (bf16[256,1024]{1,0:T(8,128)(2,1)S(1)}, bf16[256,1024]{1,0:T(8,128)(2,1)}, u32[]{:S(2)}) copy-start(bf16[256,1024]{1,0:T(8,128)(2,1)} %cotangent_ref.1) | copy-start | bytes 1572868
  3.1 28.3 %all-to-all-start = ((bf16[128,8,128]{2,1,0:T(8,128)(2,1)}), bf16[128,8,128]{2,1,0:T(8,128)(2,1)S(1)}, u32[]{:S(2)}, u32[]{:S(2)}) async-start(bf16[128,8,128]{2,1,0:T(8,128)(2,1)} %shard_map.59), calls=%async_computation | async-start | bytes 524288 | tf_op jit(solution)/shard_map/all_to_all | solution.py:382
  17.8 0.9 copy-start.8
  18.8 8.6 %copy-start.3 = (bf16[256,1024]{1,0:T(8,128)(2,1)S(1)}, bf16[256,1024]{1,0:T(8,128)(2,1)}, u32[]{:S(2)}) copy-start(bf16[256,1024]{1,0:T(8,128)(2,1)} %refs_0_) | copy-start | bytes 1572868
  27.3 18.7 %collective-permute-start = (bf16[256,1024]{1,0:T(8,128)(2,1)S(1)}, bf16[256,1024]{1,0:T(8,128)(2,1)S(1)}, u32[]{:S(2)}, u32[]{:S(2)}) collective-permute-start(bf16[256,1024]{1,0:T(8,128)(2,1)S(1)} %copy-done.3), channel_id=1, source_target_pairs={{0,16},{16,32},{32,48},{48,0},{1,17},{17,33},{33,49},{49,1},{2,18}... | collective-permute-start | bytes 1572872 | tf_op jit(solution)/shard_map/ppermute | solution.py:175
  28.7 17.3 %collective-permute-start.1 = (bf16[256,1024]{1,0:T(8,128)(2,1)S(1)}, bf16[256,1024]{1,0:T(8,128)(2,1)S(1)}, u32[]{:S(2)}, u32[]{:S(2)}) collective-permute-start(bf16[256,1024]{1,0:T(8,128)(2,1)S(1)} %copy-done.3), channel_id=1, source_target_pairs={{0,48},{16,0},{32,16},{48,32},{1,49},{17,1},{33,17},{49,33},{2,50}... | collective-permute-start | bytes 1572872 | tf_op jit(solution)/shard_map/ppermute | solution.py:175
  46.0 18.7 %copy-start.1 = (bf16[256,1024]{1,0:T(8,128)(2,1)}, bf16[256,1024]{1,0:T(8,128)(2,1)S(1)}, u32[]{:S(2)}) copy-start(bf16[256,1024]{1,0:T(8,128)(2,1)S(1)} %collective-permute-done.1.refs_4_) | copy-start | bytes 1572868
  46.0 27.1 %all-to-all-start.1 = ((bf16[64,4,8,128]{3,2,1,0:T(8,128)(2,1)}), bf16[64,4,8,128]{3,2,1,0:T(8,128)(2,1)S(1)}, u32[]{:S(2)}, u32[]{:S(2)}) async-start(bf16[64,4,8,128]{3,2,1,0:T(8,128)(2,1)} %bitcast.2), calls=%async_computation.1 | async-start | bytes 1048576 | tf_op jit(solution)/shard_map/all_to_all | solution.py:397
  55.8 8.9 %collective-permute-start.2 = (bf16[128,1024]{1,0:T(8,128)(2,1)S(1)}, bf16[128,1024]{1,0:T(8,128)(2,1)S(1)}, u32[]{:S(2)}, u32[]{:S(2)}) collective-permute-start(bf16[128,1024]{1,0:T(8,128)(2,1)S(1)} %slice.12), channel_id=1, source_target_pairs={{0,16},{16,32},{32,48},{48,0},{1,17},{17,33},{33,49},{49,1},{2,18}... | collective-permute-start | bytes 786440 | tf_op jit(solution)/shard_map/ppermute | solution.py:175
  56.2 8.5 %collective-permute-start.3 = (bf16[128,1024]{1,0:T(8,128)(2,1)S(1)}, bf16[128,1024]{1,0:T(8,128)(2,1)S(1)}, u32[]{:S(2)}, u32[]{:S(2)}) collective-permute-start(bf16[128,1024]{1,0:T(8,128)(2,1)S(1)} %slice.13), channel_id=1, source_target_pairs={{0,48},{16,0},{32,16},{48,32},{1,49},{17,1},{33,17},{49,33},{2,50}... | collective-permute-start | bytes 786440 | tf_op jit(solution)/shard_map/ppermute | solution.py:175
  64.7 0.7 copy-start.6
  65.4 1.0 %copy-start.2 = (bf16[256,1024]{1,0:T(8,128)(2,1)S(1)}, bf16[256,1024]{1,0:T(8,128)(2,1)}, u32[]{:S(2)}) copy-start(bf16[256,1024]{1,0:T(8,128)(2,1)} %copy-done.1) | copy-start | bytes 1572868
  66.4 1.0 %copy-start.4 = (bf16[256,1024]{1,0:T(8,128)(2,1)S(1)}, bf16[256,1024]{1,0:T(8,128)(2,1)}, u32[]{:S(2)}) copy-start(bf16[256,1024]{1,0:T(8,128)(2,1)} %refs_0_) | copy-start | bytes 1572868
  67.5 0.9 copy-start.7
  74.1 10.7 %copy-start = (bf16[1,1024,1024]{2,1,0:T(8,128)(2,1)S(1)}, bf16[1,1024,1024]{2,1,0:T(8,128)(2,1)}, u32[]{:S(2)}) copy-start(bf16[1,1024,1024]{2,1,0:T(8,128)(2,1)} %param.6) | copy-start | bytes 6291460
  74.9 4.1 %collective-permute-start.4 = (bf16[128,1024]{1,0:T(8,128)(2,1)S(1)}, bf16[128,1024]{1,0:T(8,128)(2,1)S(1)}, u32[]{:S(2)}, u32[]{:S(2)}) collective-permute-start(bf16[128,1024]{1,0:T(8,128)(2,1)S(1)} %get-tuple-element.27), channel_id=1, source_target_pairs={{0,1},{1,0},{2,3},{3,2},{4,5},{5,4},{6,7},{7,6},{8,9},{9,8},{10,11... | collective-permute-start | bytes 786440 | tf_op jit(solution)/shard_map/ppermute | solution.py:175
  75.2 9.6 %collective-permute-start.5 = (bf16[64,8,128]{2,1,0:T(8,128)(2,1)}, bf16[64,8,128]{2,1,0:T(8,128)(2,1)S(1)}, u32[]{:S(2)}, u32[]{:S(2)}) collective-permute-start(bf16[64,8,128]{2,1,0:T(8,128)(2,1)} %get-tuple-element.29), channel_id=1, source_target_pairs={{0,16},{16,32},{32,48},{48,0},{1,17},{17,33},{33,49},{49,1},{2,18}... | collective-permute-start | bytes 393224 | tf_op jit(solution)/shard_map/ppermute | solution.py:175
  75.3 9.5 %collective-permute-start.6 = (bf16[64,8,128]{2,1,0:T(8,128)(2,1)S(1)}, bf16[64,8,128]{2,1,0:T(8,128)(2,1)S(1)}, u32[]{:S(2)}, u32[]{:S(2)}) collective-permute-start(bf16[64,8,128]{2,1,0:T(8,128)(2,1)S(1)} %get-tuple-element.30), channel_id=1, source_target_pairs={{0,32},{16,48},{32,0},{48,16},{1,33},{17,49},{33,1},{49,17},{2,34}... | collective-permute-start | bytes 393224 | tf_op jit(solution)/shard_map/ppermute | solution.py:175
  77.9 6.9 %collective-permute-start.7 = (bf16[64,8,128]{2,1,0:T(8,128)(2,1)S(1)}, bf16[64,8,128]{2,1,0:T(8,128)(2,1)S(1)}, u32[]{:S(2)}, u32[]{:S(2)}) collective-permute-start(bf16[64,8,128]{2,1,0:T(8,128)(2,1)S(1)} %get-tuple-element.31), channel_id=1, source_target_pairs={{0,48},{16,0},{32,16},{48,32},{1,49},{17,1},{33,17},{49,33},{2,50}... | collective-permute-start | bytes 393224 | tf_op jit(solution)/shard_map/ppermute | solution.py:175
  79.8 18.8 %all-to-all-start.2 = ((bf16[16,8,1024]{2,1,0:T(8,128)(2,1)}), bf16[16,8,1024]{2,1,0:T(8,128)(2,1)S(1)}, u32[]{:S(2)}, u32[]{:S(2)}) async-start(bf16[16,8,1024]{2,1,0:T(8,128)(2,1)} %fusion), calls=%async_computation.2 | async-start | bytes 524288 | tf_op jit(solution)/shard_map/all_to_all | solution.py:412
  86.3 7.4 %collective-permute-start.9 = (bf16[128,512]{1,0:T(8,128)(2,1)S(1)}, bf16[128,512]{1,0:T(8,128)(2,1)S(1)}, u32[]{:S(2)}, u32[]{:S(2)}) collective-permute-start(bf16[128,512]{1,0:T(8,128)(2,1)S(1)} %get-tuple-element.43), channel_id=1, source_target_pairs={{0,128},{128,0},{1,129},{129,1},{2,130},{130,2},{3,131},{131,3},{4... | collective-permute-start | bytes 393224 | tf_op jit(solution)/shard_map/ppermute | solution.py:175
  89.0 8.8 %collective-permute-start.8 = (bf16[128,512]{1,0:T(8,128)(2,1)S(1)}, bf16[128,512]{1,0:T(8,128)(2,1)S(1)}, u32[]{:S(2)}, u32[]{:S(2)}) collective-permute-start(bf16[128,512]{1,0:T(8,128)(2,1)S(1)} %get-tuple-element.42), channel_id=1, source_target_pairs={{0,128},{128,0},{1,129},{129,1},{2,130},{130,2},{3,131},{131,3},{4... | collective-permute-start | bytes 393224 | tf_op jit(solution)/shard_map/ppermute | solution.py:175
